TPU v7x, 32 devices: a whole 2x2x4 slice. The times are simulated.
32 devices in a mesh: ctx: 8 (over z, x), head: 4 (over y, core).
Axes of the slice: x: 2, y: 2, z: 4, core: 2. Of those that a mesh axis runs over, the one named last changes fastest.
Arguments:
- queries: bfloat16 [2048, 2048], P('ctx', 'head'), may hold values from -32 to 32
- key_heads: bfloat16 [2048, 2048], P('ctx', 'head'), may hold values from -32 to 32
- value_heads: bfloat16 [2048, 2048], P('ctx', 'head'), may hold values from -6 to 6
- out_weight: bfloat16 [4096, 2048], P('ctx', 'head'), may hold values from -0.5 to 0.5
- block_lists: int32 [16, 3], replicated, may hold values from 0 to 15, as said below
- out_grad: bfloat16 [2048, 4096], P('ctx', 'head'), may hold values from -6 to 6
Outputs:
- attended: bfloat16 [2048, 4096], P('ctx', 'head')
- query_grad: bfloat16 [2048, 2048], P('ctx', 'head')
- key_grad: bfloat16 [2048, 2048], P('ctx', 'head')
- value_grad: bfloat16 [2048, 2048], P('ctx', 'head')
- weight_grad: float32 [4096, 2048], P('ctx', 'head')
Inputs may be any that keep to these rules, and one draw needn't show every extreme that they name: `block_lists`: every entry of row b lies within 4 blocks of b, and the first entry of each row lies exactly 4 blocks away from b.
All inputs are finite; a program needn't handle non-finite values.
Results may differ from a plain program's by a relative error of at most 0.028.
Values may be sent and summed in bfloat16 or wider, within the bound.
No kernel may reach another device: no remote copies, remote signals or barrier semaphores. Data moves between devices by JAX's collectives and lax.ppermute only.
A program may use at most 128 MiB of HBM per device.

v0:
```python
import functools

import jax
import jax.numpy as jnp
from jax import lax
from jax.experimental import pallas as pl
from jax.experimental.pallas import tpu as pltpu
from jax.sharding import PartitionSpec as P

HD = 128
BLK = 128
REACH = 4

CHEAP = pl.CostEstimate(flops=1, bytes_accessed=1, transcendentals=0)

NT = (((1,), (1,)), ((), ()))
TN = (((0,), (0,)), ((), ()))
NN = (((1,), (0,)), ((), ()))


def mm(a, b, dims):
    return lax.dot_general(a, b, dims, preferred_element_type=jnp.float32)


def shifted(x, by):
    peers = lax.axis_size("ctx")
    return lax.ppermute(x, "ctx", [(i, i + by) for i in range(peers) if 0 <= i + by < peers])


def tree_strides(peers):
    strides = []
    stride = 1
    while stride < peers:
        strides.append(stride)
        stride *= 2
    return strides


def from_first(x):
    peers = lax.axis_size("ctx")
    me = lax.axis_index("ctx")
    for stride in reversed(tree_strides(peers)):
        pairs = [(i, i + stride) for i in range(0, peers, 2 * stride) if i + stride < peers]
        got = lax.ppermute(x, "ctx", pairs)
        x = jnp.where(me % (2 * stride) == stride, got, x)
    return x


def to_first(x):
    peers = lax.axis_size("ctx")
    for stride in tree_strides(peers):
        pairs = [(i + stride, i) for i in range(0, peers, 2 * stride) if i + stride < peers]
        x = x + lax.ppermute(x.astype(jnp.bfloat16), "ctx", pairs).astype(x.dtype)
    return x


def turned(x, by, length):
    return lax.ppermute(x, "ctx", [(2 * z + n, 2 * ((z + by) % length) + n) for z in range(length) for n in range(2)])


def swapped(piece, places):
    return lax.ppermute(piece, "ctx", [(2 * z + n, 2 * z + 1 - n) for z in places for n in range(2)])


def tied(x, *others):
    return lax.optimization_barrier((x,) + others)[0]


def start_weights(pieces, held_ref, sems):
    place = lax.div(lax.axis_index("ctx"), 2)
    own, beside, middle, outer, far, farthest = pieces
    low = place < 2
    inner = (place == 1) | (place == 2)

    def send(piece, slot):
        pltpu.make_async_copy(piece, held_ref.at[slot], sems.at[slot]).start()

    send(own, place)
    send(beside, place + 1 - 2 * lax.rem(place, 2))

    @pl.when(inner)
    def _():
        send(middle, 3 - place)
        send(far, jnp.where(low, 3, 0))

    @pl.when(jnp.logical_not(inner))
    def _():
        send(outer, jnp.where(low, 2, 1))
        send(farthest, 3 - place)


def weight_at(held_ref, sems, b):
    pltpu.make_async_copy(held_ref.at[b], held_ref.at[b], sems.at[b]).wait()
    return held_ref[b]


def grads_kernel(length, rows_hbm_ref, *rest):
    pieces = rest[:6]
    grad_ref, other_ref, rows_ref, held_ref, sems, row_sem = rest[6:]
    tokens = grad_ref.shape[0]
    width = rows_ref.shape[1] // length
    rows = pltpu.make_async_copy(rows_hbm_ref, rows_ref, row_sem)
    rows.start()
    start_weights(pieces, held_ref, sems)
    rows.wait()
    total = None
    for b in range(length):
        part = mm(rows_ref[:, b * width : (b + 1) * width], weight_at(held_ref, sems, b), NN)
        total = part if total is None else total + part
    grad_ref[...] = total[:tokens]
    other_ref[...] = total[tokens:].astype(jnp.bfloat16)


def outs_kernel(length, mixed_ref, other_ref, *rest):
    pieces = rest[:6]
    out_ref, held_ref, sems = rest[6:]
    tokens = mixed_ref.shape[0]
    width = out_ref.shape[1] // length
    start_weights(pieces, held_ref, sems)
    for b in range(length):
        weight = weight_at(held_ref, sems, b)
        columns = slice(b * width, (b + 1) * width)
        out_ref[:tokens, columns] = mm(mixed_ref[...], weight, NT).astype(jnp.bfloat16)
        out_ref[tokens:, columns] = mm(other_ref[...], weight, NT).astype(jnp.bfloat16)


def weight_kernel(length, rows_hbm_ref, mixed_ref, other_ref, own_ref, *rest):
    sends = rest[: length - 1]
    rows_ref, both_ref, row_sem = rest[length - 1 :]
    width = own_ref.shape[0]
    tokens = mixed_ref.shape[0]
    place = lax.div(lax.axis_index("ctx"), 2)
    rows = pltpu.make_async_copy(rows_hbm_ref, rows_ref, row_sem)
    rows.start()
    both_ref[:tokens, :] = mixed_ref[...]
    both_ref[tokens:, :] = other_ref[...]
    rows.wait()
    for n, out_ref in enumerate((own_ref,) + sends):
        column = pl.multiple_of(lax.rem(place + n, length) * width, 128)
        out_ref[...] = mm(rows_ref[:, pl.ds(column, width)], both_ref[...], TN).astype(out_ref.dtype)


def finish_kernel(scale, run_ref, own_ref, a_ref, b_ref, c_ref, first_ref, key_ref, value_ref):
    there = jnp.where((run_ref[0] == 0) & (pl.program_id(0) == 0), 1.0, 0.0).astype(jnp.float32)
    for n, out_ref in enumerate((key_ref, value_ref)):
        total = own_ref[n] + a_ref[n].astype(jnp.float32) + b_ref[n].astype(jnp.float32) + c_ref[n].astype(jnp.float32)
        total = total + there * first_ref[n]
        out_ref[...] = (total * (scale if n == 0 else 1.0)).astype(jnp.bfloat16)


def runs_away(offset, run):
    side = lax.rem(run, 2)
    if offset == "pair":
        return 1 - 2 * side
    if offset == "across":
        return 2 * side - 1
    return offset


def block_bias(lists_ref, run, per_dev, total_blocks, offset, i, j):
    row = run * per_dev + i
    key = (run + runs_away(offset, run)) * per_dev + j
    hit = (key - row <= 1) & (row - key <= 1)
    for n in range(lists_ref.shape[1]):
        hit = hit | (lists_ref[row, n] == key)
    hit = hit & (key >= 1) & (key < total_blocks)
    return jnp.where(hit, 0.0, -jnp.inf).astype(jnp.float32)


def fwd_kernel(offsets, per_dev, scale, run_ref, lists_ref, q_ref, k_ref, v_ref, *rest):
    bands = rest[: len(offsets)]
    first_ref, mixed_ref, lse_ref, s_ref = rest[len(offsets) :]
    total_blocks = lists_ref.shape[0]
    run = run_ref[0]
    q = q_ref[...]
    tokens = q.shape[0]

    def key_of(p):
        return k_ref[...] if p == 0 else bands[p - 1][0]

    def value_of(p):
        return v_ref[...] if p == 0 else bands[p - 1][1]

    places = (0,) + offsets
    top = None
    for p, offset in enumerate(places):
        s = mm(key_of(p), q, NT) * scale
        for j in range(per_dev):
            for i in range(per_dev):
                part = s[j * BLK : (j + 1) * BLK, i * BLK : (i + 1) * BLK]
                part = part + block_bias(lists_ref, run, per_dev, total_blocks, offset, i, j)
                s_ref[p * tokens + j * BLK : p * tokens + (j + 1) * BLK, i * BLK : (i + 1) * BLK] = part
    s_ref[len(places) * tokens :, :] = mm(first_ref[0], q, NT) * scale
    s = s_ref[...]
    top = jnp.max(s, axis=0, keepdims=True)
    e = jnp.exp(s - top)
    total = jnp.sum(e, axis=0, keepdims=True)
    inverse = 1.0 / total
    low = (e * inverse).astype(jnp.bfloat16)
    out = mm(first_ref[1], low[len(places) * tokens :], TN)
    for p in range(len(places)):
        out = out + mm(value_of(p), low[p * tokens : (p + 1) * tokens], TN)
    mixed_ref[...] = out.T.astype(jnp.bfloat16)
    lse_ref[0] = top + jnp.log(total)


def probs_of(lists_ref, s_ref, run, per_dev, s, offset, lse):
    if offset is None:
        return jnp.exp(s - lse)
    for j in range(per_dev):
        for i in range(per_dev):
            part = s[j * BLK : (j + 1) * BLK, i * BLK : (i + 1) * BLK]
            part = part + block_bias(lists_ref, run, per_dev, lists_ref.shape[0], offset, i, j)
            s_ref[j * BLK : (j + 1) * BLK, i * BLK : (i + 1) * BLK] = part
    return jnp.exp(s_ref[...] - lse)


def first_kernel(offsets, per_dev, scale, run_ref, lists_ref, q_ref, *rest):
    bands = rest[: len(offsets)]
    first_ref, mixed_ref, grad_ref, lse_ref, out_ref, s_ref = rest[len(offsets) :]
    q = q_ref[...]
    grad = grad_ref[...]
    lse = lse_ref[0]
    product = grad.astype(jnp.float32) * mixed_ref[...].astype(jnp.float32)
    delta = jnp.sum(product.T, axis=0, keepdims=True)
    at = 0
    for n, (offset, pair_ref) in enumerate(zip(tuple(offsets) + (None,), bands + (first_ref,))):
        p = probs_of(lists_ref, s_ref.at[n], run_ref[0], per_dev, mm(pair_ref[0], q, NT) * scale, offset, lse)
        slopes = (p * (mm(pair_ref[1], grad, NT) - delta)).astype(jnp.bfloat16)
        rows = slice(at, at + pair_ref.shape[1])
        at = rows.stop
        out_ref[0, rows, :] = mm(slopes, q, NN).astype(jnp.bfloat16)
        out_ref[1, rows, :] = mm(p.astype(jnp.bfloat16), grad, NN).astype(jnp.bfloat16)


def bwd_kernel(offsets, early, per_dev, scale, run_ref, lists_ref, q_ref, k_ref, v_ref, *rest):
    bands = rest[: len(offsets)]
    first_ref, mixed_ref, grad_ref, lse_ref = rest[len(offsets) : len(offsets) + 4]
    outs = rest[len(offsets) + 4 :]
    dq_ref, own_ref = outs[:2]
    band_outs = list(outs[2:-1])
    s_ref = outs[-1]
    q = q_ref[...]
    grad = grad_ref[...]
    lse = lse_ref[0]
    product = grad.astype(jnp.float32) * mixed_ref[...].astype(jnp.float32)
    delta = jnp.sum(product.T, axis=0, keepdims=True)
    dq = None
    plan = [(None, first_ref[0], first_ref[1], None)]
    for offset, pair_ref in zip(offsets, bands):
        plan.append((offset, pair_ref[0], pair_ref[1], None if offset in early else band_outs.pop(0)))
    plan.append((0, k_ref[...], v_ref[...], own_ref))
    for n, (offset, key, value, out_ref) in enumerate(plan):
        p = probs_of(lists_ref, s_ref.at[n], run_ref[0], per_dev, mm(key, q, NT) * scale, offset, lse)
        slopes = (p * (mm(value, grad, NT) - delta)).astype(jnp.bfloat16)
        more = mm(key, slopes, TN)
        dq = more if dq is None else dq + more
        if out_ref is not None:
            out_ref[0] = mm(slopes, q, NN).astype(out_ref.dtype)
            out_ref[1] = mm(p.astype(jnp.bfloat16), grad, NN).astype(out_ref.dtype)
    dq_ref[...] = (dq * scale).T.astype(jnp.bfloat16)


def local(queries, key_heads, value_heads, out_weight, block_lists, out_grad):
    scale = HD ** (-0.5)
    tokens, features = queries.shape
    groups = features // HD
    per_dev = tokens // BLK
    ctx = lax.axis_size("ctx")
    head = lax.axis_size("head")
    run = lax.axis_index("ctx")
    column = lax.axis_index("head")
    reach = -(-REACH // per_dev)
    length = ctx // 2
    direct = ctx == 8 and head == length and reach == 2 and out_grad.shape[1] == 2 * features
    place = run // 2
    side = run % 2
    if direct:
        offsets, early = (-2, 2, "pair", "across"), ("across",)
    else:
        offsets, early = tuple(o for o in range(-reach, reach + 1) if o != 0), ()
    places = 1 + len(offsets)
    smem = pl.BlockSpec(memory_space=pltpu.SMEM)
    whole = pl.BlockSpec(memory_space=pltpu.VMEM)
    distant = pl.BlockSpec(memory_space=pltpu.HBM)
    anywhere = pl.BlockSpec(memory_space=pl.ANY)
    width = out_weight.shape[0]

    both = jnp.stack([key_heads, value_heads])
    head_rows = both[:, :BLK]
    if direct:
        half = out_grad.shape[1] // 2
        own_half = lax.dynamic_slice_in_dim(out_grad, side * half, half, 1)
        other_half = lax.dynamic_slice_in_dim(out_grad, (1 - side) * half, half, 1)
        before, after = shifted(both, 2), shifted(both, -2)
        beside = swapped(jnp.concatenate([both, other_half[None]], axis=0), range(length))
        grad_side = lax.all_gather(jnp.concatenate([own_half, tied(beside[2], before, after)], axis=0), "head", axis=1, tiled=True)
        sent = jnp.where(side == 0, after, before)
        hop = [(2 * z, 2 * z + 1) for z in range(length - 1)] + [(2 * z + 1, 2 * z) for z in range(1, length)]
        across = lax.ppermute(sent, "ctx", hop)
        known = jnp.where(run == 1, beside[:2, :BLK], head_rows)
        known = jnp.where(run == 2, before[:, :BLK], known)
        middle_rows = lax.ppermute(head_rows, "ctx", [(0, length)])
        known = jnp.where(run == length, middle_rows, known)
        late = lax.ppermute(known, "ctx", [(1, 7), (0, 3), (4, 5), (2, 6)])
        first = jnp.where((run == 3) | (run > length), late, known)

        def between(x, places):
            return lax.ppermute(x, "ctx", [(2 * a + n, 2 * b + n) for a, b in places for n in range(2)])

        base = tied(out_weight, before, after, middle_rows)
        near = between(base, ((0, 1), (1, 0), (2, 3), (3, 2)))
        middle = between(base, ((1, 2), (2, 1)))
        far = between(near, ((1, 2), (2, 1)))
        outer = between(middle, ((1, 0), (2, 3)))
        farthest = between(far, ((1, 0), (2, 3)))
        weight_pieces = [base, near, middle, outer, far, farthest]
        bands = [before, after, beside, across]
    else:
        bands = [shifted(both, -o) for o in offsets]
        first = from_first(head_rows)
        grad_full = lax.all_gather(out_grad, "head", axis=1, tiled=True)
        full_weight = lax.all_gather(out_weight, "ctx", axis=0, tiled=True)
        rounds = ctx // head
        mine = jnp.zeros((rounds * tokens, width), jnp.bfloat16)
        for r in range(rounds):
            pairs = []
            for c in range(ctx):
                for h in range(head):
                    pairs.append((c * head + h, (rounds * h + (c + r) % rounds) * head + c // rounds))
            sent = lax.dynamic_slice_in_dim(out_grad, ((run + r) % rounds) * width, width, 1)
            got = lax.ppermute(sent, ("ctx", "head"), pairs)
            mine = lax.dynamic_update_slice_in_dim(mine, got, ((run - r) % rounds) * tokens, 0)
        grad_rows = lax.all_gather(mine, "head", axis=0, tiled=True)

    run_word = run.astype(jnp.int32).reshape(1)
    flat = pl.BlockSpec((tokens, HD), lambda h: (0, h))
    pair = pl.BlockSpec((2, tokens, HD), lambda h: (0, 0, h))
    head_pair = pl.BlockSpec((2, BLK, HD), lambda h: (0, 0, h))
    row = pl.BlockSpec((1, 1, tokens), lambda h: (h, 0, 0))
    keys = places * tokens + BLK
    mixed, lse = pl.pallas_call(
        functools.partial(fwd_kernel, offsets, per_dev, scale),
        grid=(groups,),
        in_specs=[smem, smem, flat, flat, flat] + [pair] * len(offsets) + [head_pair],
        out_specs=[flat, row],
        out_shape=[
            jax.ShapeDtypeStruct((tokens, features), jnp.bfloat16),
            jax.ShapeDtypeStruct((groups, 1, tokens), jnp.float32),
        ],
        scratch_shapes=[pltpu.VMEM((keys, tokens), jnp.float32)],
        compiler_params=pltpu.CompilerParams(vmem_limit_bytes=40 * 1024 * 1024),
        cost_estimate=CHEAP,
        name="attend",
    )(run_word, block_lists, queries, key_heads, value_heads, *bands, first)

    if direct:
        held = [pltpu.VMEM((length, width, features), jnp.bfloat16), pltpu.SemaphoreType.DMA((length,))]
        own_grad, other_grad = pl.pallas_call(
            functools.partial(grads_kernel, length),
            in_specs=[distant] + [anywhere] * 6,
            out_specs=[whole] * 2,
            out_shape=[
                jax.ShapeDtypeStruct((tokens, features), jnp.float32),
                jax.ShapeDtypeStruct((tokens, features), jnp.bfloat16),
            ],
            scratch_shapes=[pltpu.VMEM((2 * tokens, length * width), jnp.bfloat16)] + held + [pltpu.SemaphoreType.DMA],
            compiler_params=pltpu.CompilerParams(vmem_limit_bytes=32 * 1024 * 1024),
            cost_estimate=CHEAP,
            name="project_grad",
        )(grad_side, *weight_pieces)
        mixed_grad = (own_grad + swapped(other_grad, range(length)).astype(jnp.float32)).astype(jnp.bfloat16)
        mixed_other = tied(swapped(mixed, range(length)), other_grad)
        partial_out = pl.pallas_call(
            functools.partial(outs_kernel, length),
            in_specs=[whole] * 2 + [anywhere] * 6,
            out_specs=pl.BlockSpec((2 * tokens, length * width), lambda: (0, 0)),
            out_shape=jax.ShapeDtypeStruct((2 * tokens, length * width), jnp.bfloat16),
            scratch_shapes=held,
            compiler_params=pltpu.CompilerParams(vmem_limit_bytes=32 * 1024 * 1024),
            cost_estimate=CHEAP,
            name="project_out",
        )(mixed, mixed_other, *weight_pieces)
        scattered = lax.psum_scatter(partial_out, "head", scatter_dimension=1, tiled=True)
        mine, theirs = scattered[:tokens], swapped(scattered[tokens:], range(length))
        attended = jnp.where(
            side == 0, jnp.concatenate([mine, theirs], axis=1), jnp.concatenate([theirs, mine], axis=1)
        )
        own_part, *weight_parts = pl.pallas_call(
            functools.partial(weight_kernel, length),
            in_specs=[distant] + [whole] * 2,
            out_specs=[whole] * length,
            out_shape=[jax.ShapeDtypeStruct((width, features), jnp.float32)]
            + [jax.ShapeDtypeStruct((width, features), jnp.bfloat16)] * (length - 1),
            scratch_shapes=[
                pltpu.VMEM((2 * tokens, length * width), jnp.bfloat16),
                pltpu.VMEM((2 * tokens, features), jnp.bfloat16),
                pltpu.SemaphoreType.DMA,
            ],
            compiler_params=pltpu.CompilerParams(vmem_limit_bytes=32 * 1024 * 1024),
            cost_estimate=CHEAP,
            name="weight_part",
        )(grad_side, mixed, mixed_other)
        mixed_grad = tied(mixed_grad, own_part, partial_out)
        weight_turns = [turned(weight_parts[n - 1], n, length) for n in (1, 3)]
    else:
        partial_out = mm(mixed, full_weight, NT).astype(jnp.bfloat16)
        mixed_grad = mm(grad_full, full_weight, NN).astype(jnp.bfloat16)
        mixed_all = lax.all_gather(mixed, "ctx", axis=0, tiled=True)
        attended = lax.psum_scatter(partial_out, "head", scatter_dimension=1, tiled=True)
    early_bands = [band for o, band in zip(offsets, bands) if o in early]
    early_rows = len(early) * tokens + BLK
    early_grads = pl.pallas_call(
        functools.partial(first_kernel, early, per_dev, scale),
        grid=(groups,),
        in_specs=[smem, smem, flat] + [pair] * len(early) + [head_pair, flat, flat, row],
        out_specs=pl.BlockSpec((2, early_rows, HD), lambda h: (0, 0, h)),
        out_shape=jax.ShapeDtypeStruct((2, early_rows, features), jnp.bfloat16),
        scratch_shapes=[pltpu.VMEM((1 + len(early), tokens, tokens), jnp.float32)],
        compiler_params=pltpu.CompilerParams(vmem_limit_bytes=32 * 1024 * 1024),
        cost_estimate=pl.CostEstimate(flops=10_000_000_000, bytes_accessed=1, transcendentals=0),
        name="first_grad",
    )(run_word, block_lists, queries, *early_bands, first, mixed, mixed_grad, lse)

    lse_later = tied(lse, early_grads)
    results = pl.pallas_call(
        functools.partial(bwd_kernel, offsets, early, per_dev, scale),
        grid=(groups,),
        in_specs=[smem, smem, flat, flat, flat] + [pair] * len(offsets) + [head_pair, flat, flat, row],
        out_specs=[flat, pair] + [pair] * (len(offsets) - len(early)),
        out_shape=[
            jax.ShapeDtypeStruct((tokens, features), jnp.bfloat16),
            jax.ShapeDtypeStruct((2, tokens, features), jnp.float32),
        ]
        + [jax.ShapeDtypeStruct((2, tokens, features), jnp.bfloat16)] * (len(offsets) - len(early)),
        scratch_shapes=[pltpu.VMEM((1 + places, tokens, tokens), jnp.float32)],
        compiler_params=pltpu.CompilerParams(vmem_limit_bytes=40 * 1024 * 1024),
        cost_estimate=pl.CostEstimate(flops=30_000_000_000, bytes_accessed=1, transcendentals=0),
        name="attend_grad",
    )(run_word, block_lists, queries, key_heads, value_heads, *bands, first, mixed, mixed_grad, lse_later)
    query_grad, own = results[:2]
    if direct:
        to_before, to_after, to_beside = results[2:]
        swap = tied(swapped(early_grads, range(length)), query_grad)
        diagonal = swap[:, :tokens].astype(jnp.float32)
        first_sum = early_grads[:, tokens:].astype(jnp.float32) + swap[:, tokens:].astype(jnp.float32)
        folded = jnp.pad(jnp.where(run == 2, first_sum, 0.0), ((0, 0), (0, tokens - BLK), (0, 0)))
        to_before, to_after, _ = lax.optimization_barrier((to_before, to_after, weight_turns))
        to_before = to_before.astype(jnp.float32) + jnp.where(side == 1, diagonal, 0.0) + folded
        to_after = to_after.astype(jnp.float32) + jnp.where(side == 0, diagonal, 0.0)
        back_pair = swapped(to_beside, range(length))
        to_before, to_after = to_before.astype(jnp.bfloat16), to_after.astype(jnp.bfloat16)
        to_before, to_after, near, last_part = lax.optimization_barrier(
            (to_before, to_after, first_sum.astype(jnp.bfloat16), weight_parts[1])
        )
        back_down = shifted(to_before, -2)
        back_up = shifted(to_after, 2)
        for c in range(length, ctx, 2):
            got = tied(lax.ppermute(near, "ctx", [(c, 0)]), back_down, back_up)
            first_sum = first_sum + got.astype(jnp.float32)
        weight_grad = own_part
        for part in weight_turns + [turned(last_part, 2, length)]:
            weight_grad = weight_grad + part.astype(jnp.float32)
        wide = pl.BlockSpec((2, BLK, features), lambda n: (0, n, 0))
        top = pl.BlockSpec((2, BLK, features), lambda n: (0, 0, 0))
        slab = pl.BlockSpec((BLK, features), lambda n: (n, 0))
        key_grad, value_grad = pl.pallas_call(
            functools.partial(finish_kernel, scale),
            grid=(per_dev,),
            in_specs=[smem] + [wide] * 4 + [top],
            out_specs=[slab, slab],
            out_shape=[jax.ShapeDtypeStruct((tokens, features), jnp.bfloat16)] * 2,
            cost_estimate=CHEAP,
            name="finish",
        )(run_word, own, back_pair, back_down, back_up, first_sum)

    else:
        first_sum = to_first(early_grads.astype(jnp.float32))
        sums = own
        for o, part in zip(offsets, results[2:]):
            sums = sums + shifted(part, o).astype(jnp.float32)
        first_sum = jnp.where(run == 0, first_sum, 0.0)
        sums = sums + jnp.pad(first_sum, ((0, 0), (0, tokens - BLK), (0, 0)))
        key_grad = (sums[0] * scale).astype(jnp.bfloat16)
        value_grad = sums[1].astype(jnp.bfloat16)
    if not direct:
        weight_grad = mm(grad_rows, mixed_all, TN)
    return (attended, query_grad, key_grad, value_grad, weight_grad)


def solution(mesh):
    spec = P("ctx", "head")
    return jax.shard_map(
        local,
        mesh=mesh,
        in_specs=(spec, spec, spec, spec, P(), spec),
        out_specs=(spec,) * 5,
        check_vma=False,
    )
```

profile of v0, /device:TPU:0, one launch (start us, length us, event | category | flops | bytes accessed | tf_op | source)
XLA Modules:
  0.0 187.0 jit_solution(5513058792755849123)
XLA Ops:
  9.5 3.0 %collective-permute-start.2 = (bf16[3,256,512]{2,1,0:T(8,128)(2,1)S(1)}, bf16[3,256,512]{2,1,0:T(8,128)(2,1)S(1)}, u32[]{:S(2)}, u32[]{:S(2)}) collective-permute-start(bf16[3,256,512]{2,1,0:T(8,128)(2,1)S(1)} %pad_maximum_fusion), channel_id=1, source_target_pairs={{0,4},{4,0},{8,12},{12,8},{16,20},{20,16},{24,28},{28,24},{1,5},{5... | collective-permute-start | bytes 2359304 | tf_op jit(solution)/shard_map/ppermute | solution.py:62
  12.6 3.5 %collective-permute-start = (bf16[2,256,512]{2,1,0:T(8,128)(2,1)S(1)}, bf16[2,256,512]{2,1,0:T(8,128)(2,1)S(1)}, u32[]{:S(2)}, u32[]{:S(2)}) collective-permute-start(bf16[2,256,512]{2,1,0:T(8,128)(2,1)S(1)} %pad_maximum_fusion.1), channel_id=1, source_target_pairs={{0,8},{4,12},{8,16},{12,20},{16,24},{20,28},{1,9},{5,13},{9,17},{1... | collective-permute-start | bytes 1572872 | tf_op jit(solution)/shard_map/ppermute | solution.py:27
  17.4 12.7 %collective-permute-done.2.rest_2_ = bf16[3,256,512]{2,1,0:T(8,128)(2,1)S(1)} collective-permute-done((bf16[3,256,512]{2,1,0:T(8,128)(2,1)S(1)}, bf16[3,256,512]{2,1,0:T(8,128)(2,1)S(1)}, u32[]{:S(2)}, u32[]{:S(2)}) %collective-permute-start.2) | collective-permute-done | bytes 786464 | tf_op jit(solution)/shard_map/ppermute | solution.py:62
  32.1 4.5 %collective-permute-start.4 = (bf16[2,128,512]{2,1,0:T(8,128)(2,1)S(1)}, bf16[2,128,512]{2,1,0:T(8,128)(2,1)S(1)}, u32[]{:S(2)}, u32[]{:S(2)}) collective-permute-start(bf16[2,128,512]{2,1,0:T(8,128)(2,1)S(1)} %fusion.7), channel_id=1, source_target_pairs={{0,16},{1,17},{2,18},{3,19}} | collective-permute-start | bytes 786440 | tf_op jit(solution)/shard_map/ppermute | solution.py:303
  36.6 6.2 %collective-permute-done.4 = bf16[2,128,512]{2,1,0:T(8,128)(2,1)S(1)} collective-permute-done((bf16[2,128,512]{2,1,0:T(8,128)(2,1)S(1)}, bf16[2,128,512]{2,1,0:T(8,128)(2,1)S(1)}, u32[]{:S(2)}, u32[]{:S(2)}) %collective-permute-start.4) | collective-permute-done | bytes 262176 | tf_op jit(solution)/shard_map/ppermute | solution.py:303
  42.8 1.5 collective-permute-start.8
  44.3 7.9 %collective-permute-done.7.rest_1_ = bf16[512,512]{1,0:T(8,128)(2,1)} collective-permute-done((bf16[512,512]{1,0:T(8,128)(2,1)S(1)}, bf16[512,512]{1,0:T(8,128)(2,1)}, u32[]{:S(2)}, u32[]{:S(2)}) %collective-permute-start.7) | collective-permute-done | bytes 524320 | tf_op jit(solution)/shard_map/ppermute | solution.py:309
  52.2 1.4 collective-permute-start.10
  54.5 2.1 %collective-permute-start.3 = (bf16[2,256,512]{2,1,0:T(8,128)(2,1)}, bf16[2,256,512]{2,1,0:T(8,128)(2,1)}, u32[]{:S(2)}, u32[]{:S(2)}) collective-permute-start(bf16[2,256,512]{2,1,0:T(8,128)(2,1)} %broadcast_select_fusion), channel_id=1, source_target_pairs={{0,4},{8,12},{16,20},{12,8},{20,16},{28,24},{1,5},{9,13},{17,21},{... | collective-permute-start | bytes 1572872 | tf_op jit(solution)/shard_map/ppermute | solution.py:300
  57.9 1.3 collective-permute-start.11
  59.3 9.9 %collective-permute-start.5 = (bf16[2,128,512]{2,1,0:T(8,128)(2,1)S(1)}, bf16[2,128,512]{2,1,0:T(8,128)(2,1)}, u32[]{:S(2)}, u32[]{:S(2)}) collective-permute-start(bf16[2,128,512]{2,1,0:T(8,128)(2,1)S(1)} %fusion.9), channel_id=1, source_target_pairs={{4,28},{0,12},{16,20},{8,24},{5,29},{1,13},{17,21},{9,25},{6,30},{... | collective-permute-start | bytes 786440 | tf_op jit(solution)/shard_map/ppermute | solution.py:305
  69.3 3.1 %collective-permute-done.5 = bf16[2,128,512]{2,1,0:T(8,128)(2,1)} collective-permute-done((bf16[2,128,512]{2,1,0:T(8,128)(2,1)S(1)}, bf16[2,128,512]{2,1,0:T(8,128)(2,1)}, u32[]{:S(2)}, u32[]{:S(2)}) %collective-permute-start.5) | collective-permute-done | bytes 262176 | tf_op jit(solution)/shard_map/ppermute | solution.py:305
  73.5 6.2 %attend.1 = (bf16[256,512]{1,0:T(8,128)(2,1)S(1)}, f32[4,1,256]{2,1,0:T(1,128)S(1)}) custom-call(s32[1]{0:T(128)} %bitcast.run_ref, s32[16,3]{1,0:T(8,128)S(1)} %copy.11.lists_ref, bf16[256,512]{1,0:T(8,128)(2,1)S(1)} %copy-done.19, bf16[256,512]{1,0:T(8,128)(2,1)S(1)} %copy-done.4, bf16[256,512]{1,0:T(8,128)(2,1)S(1)} %copy-done.3, ...), custom_call_target="tpu_custom_call" | custom-call | flops 1 | bytes 1 | tf_op jit(solution)/shard_map/attend/pallas_call | solution.py:342
  79.8 1.3 collective-permute-done.11.rest_5_
  81.1 1.6 copy-done
  82.7 3.4 %project_grad.1 = (f32[256,512]{1,0:T(8,128)S(1)}, bf16[256,512]{1,0:T(8,128)(2,1)}) custom-call(bf16[512,2048]{1,0:T(8,128)(2,1)S(1)} %copy-done, bf16[512,512]{1,0:T(8,128)(2,1)S(1)} %copy-done.9, bf16[512,512]{1,0:T(8,128)(2,1)} %collective-permute-done.7.rest_1_, bf16[512,512]{1,0:T(8,128)(2,1)} %collective-permute-done.8.rest_2_, ...), custom_call_target="tpu_custom_call" | custom-call | flops 1 | bytes 1 | tf_op jit(solution)/shard_map/project_grad/pallas_call | solution.py:359
  86.9 1.7 collective-permute-start.13
  88.7 2.5 %project_out.1 = bf16[512,2048]{1,0:T(8,128)(2,1)S(1)} custom-call(bf16[256,512]{1,0:T(8,128)(2,1)S(1)} %get-tuple-element.34.mixed_ref.rest_2_.rest_5_, bf16[256,512]{1,0:T(8,128)(2,1)S(1)} %collective-permute-done.6.other_ref, bf16[512,512]{1,0:T(8,128)(2,1)S(1)} %copy-done.9, bf16[512,512]{1,0:T(8,128)(2,1)} %collective-permute-done.7.rest_1_, ...), custom_call_target="tpu_custom_call" | custom-call | flops 1 | bytes 1 | tf_op jit(solution)/shard_map/project_out/pallas_call | solution.py:374
  91.2 1.4 copy-done.2
  93.3 1.6 copy-done.1
  95.8 2.0 %weight_part.1 = (f32[512,512]{1,0:T(8,128)S(1)}, bf16[512,512]{1,0:T(8,128)(2,1)S(1)}, bf16[512,512]{1,0:T(8,128)(2,1)}, bf16[512,512]{1,0:T(8,128)(2,1)S(1)}) custom-call(bf16[512,2048]{1,0:T(8,128)(2,1)S(1)} %copy-done.1, bf16[256,512]{1,0:T(8,128)(2,1)S(1)} %get-tuple-element.34.mixed_ref.rest_2_.rest_5_, bf16[256,512]{1,0:T(8,128)(2,1)S(1)} %copy-done.13), custom_call_target="tpu_custom_call" | custom-call | flops 1 | bytes 1 | tf_op jit(solution)/shard_map/weight_part/pallas_call | solution.py:389
  97.8 3.2 %collective-permute-start.15 = (bf16[512,512]{1,0:T(8,128)(2,1)S(1)}, bf16[512,512]{1,0:T(8,128)(2,1)S(1)}, u32[]{:S(2)}, u32[]{:S(2)}) collective-permute-start(bf16[512,512]{1,0:T(8,128)(2,1)S(1)} %get-tuple-element.49), channel_id=1, source_target_pairs={{0,8},{4,12},{8,16},{12,20},{16,24},{20,28},{24,0},{28,4},{1,9},{5... | collective-permute-start | bytes 1572872 | tf_op jit(solution)/shard_map/ppermute | solution.py:58
  101.1 6.3 %collective-permute-start.16 = (bf16[512,512]{1,0:T(8,128)(2,1)S(1)}, bf16[512,512]{1,0:T(8,128)(2,1)S(1)}, u32[]{:S(2)}, u32[]{:S(2)}) collective-permute-start(bf16[512,512]{1,0:T(8,128)(2,1)S(1)} %get-tuple-element.50), channel_id=1, source_target_pairs={{0,24},{4,28},{8,0},{12,4},{16,8},{20,12},{24,16},{28,20},{1,25},{... | collective-permute-start | bytes 1572872 | tf_op jit(solution)/shard_map/ppermute | solution.py:58
  108.5 3.8 %first_grad.1 = bf16[2,384,512]{2,1,0:T(8,128)(2,1)S(1)} custom-call(s32[1]{0:T(128)} %bitcast.run_ref, s32[16,3]{1,0:T(8,128)S(1)} %copy.11.lists_ref, bf16[256,512]{1,0:T(8,128)(2,1)S(1)} %copy-done.20, bf16[2,256,512]{2,1,0:T(8,128)(2,1)} %collective-permute-done.3.rest_3_.rest_0_, bf16[2,128,512]{2,1,0:T(8,128)(2,1)S(1)} %copy-done.16, ...), custom_call_target="tpu_custom_call" | custom-call | flops 10000000000 | bytes 1 | tf_op jit(solution)/shard_map/first_grad/pallas_call | solution.py:413
  112.7 9.0 %attend_grad.1 = (bf16[256,512]{1,0:T(8,128)(2,1)}, f32[2,256,512]{2,1,0:T(8,128)S(1)}, bf16[2,256,512]{2,1,0:T(8,128)(2,1)S(1)}, bf16[2,256,512]{2,1,0:T(8,128)(2,1)S(1)}, bf16[2,256,512]{2,1,0:T(8,128)(2,1)S(1)}) custom-call(s32[1]{0:T(128)} %bitcast.run_ref, s32[16,3]{1,0:T(8,128)S(1)} %copy.11.lists_ref, bf16[256,512]{1,0:T(8,128)(2,1)S(1)} %copy-done.20, ...), custom_call_target="tpu_custom_call" | custom-call | flops 30000001024 | bytes 1 | tf_op jit(solution)/shard_map/attend_grad/pallas_call | solution.py:426
  121.7 3.9 %collective-permute-done.16 = bf16[512,512]{1,0:T(8,128)(2,1)S(1)} collective-permute-done((bf16[512,512]{1,0:T(8,128)(2,1)S(1)}, bf16[512,512]{1,0:T(8,128)(2,1)S(1)}, u32[]{:S(2)}, u32[]{:S(2)}) %collective-permute-start.16) | collective-permute-done | bytes 524320 | tf_op jit(solution)/shard_map/ppermute | solution.py:58
  125.7 2.6 %collective-permute-done.17 = bf16[2,384,512]{2,1,0:T(8,128)(2,1)S(1)} collective-permute-done((bf16[2,384,512]{2,1,0:T(8,128)(2,1)S(1)}, bf16[2,384,512]{2,1,0:T(8,128)(2,1)S(1)}, u32[]{:S(2)}, u32[]{:S(2)}) %collective-permute-start.17) | collective-permute-done | bytes 786464 | tf_op jit(solution)/shard_map/ppermute | solution.py:62
  130.0 4.6 %collective-permute-start.19 = (bf16[2,256,512]{2,1,0:T(8,128)(2,1)S(1)}, bf16[2,256,512]{2,1,0:T(8,128)(2,1)S(1)}, u32[]{:S(2)}, u32[]{:S(2)}) collective-permute-start(bf16[2,256,512]{2,1,0:T(8,128)(2,1)S(1)} %get-tuple-element.56), channel_id=1, source_target_pairs={{0,8},{4,12},{8,16},{12,20},{16,24},{20,28},{1,9},{5,13},{9,17},{1... | collective-permute-start | bytes 1572872 | tf_op jit(solution)/shard_map/ppermute | solution.py:27
  137.3 13.0 %collective-permute-done.21 = bf16[2,128,512]{2,1,0:T(8,128)(2,1)S(1)} collective-permute-done((bf16[2,128,512]{2,1,0:T(8,128)(2,1)S(1)}, bf16[2,128,512]{2,1,0:T(8,128)(2,1)S(1)}, u32[]{:S(2)}, u32[]{:S(2)}) %collective-permute-start.21) | collective-permute-done | bytes 262176 | tf_op jit(solution)/shard_map/ppermute | solution.py:459
  150.3 16.6 %collective-permute-done.20 = bf16[2,128,512]{2,1,0:T(8,128)(2,1)S(1)} collective-permute-done((bf16[2,128,512]{2,1,0:T(8,128)(2,1)S(1)}, bf16[2,128,512]{2,1,0:T(8,128)(2,1)S(1)}, u32[]{:S(2)}, u32[]{:S(2)}) %collective-permute-start.20) | collective-permute-done | bytes 262176 | tf_op jit(solution)/shard_map/ppermute | solution.py:459
  168.6 2.7 %finish.1 = (bf16[256,512]{1,0:T(8,128)(2,1)}, bf16[256,512]{1,0:T(8,128)(2,1)}) custom-call(s32[1]{0:T(128)} %bitcast.run_ref, f32[2,256,512]{2,1,0:T(8,128)} %copy-done.14, bf16[2,256,512]{2,1,0:T(8,128)(2,1)} %copy-done.23, bf16[2,256,512]{2,1,0:T(8,128)(2,1)} %copy-done.21, bf16[2,256,512]{2,1,0:T(8,128)(2,1)} %copy-done.22, ...), custom_call_target="tpu_custom_call" | custom-call | flops 1 | bytes 1 | tf_op jit(solution)/shard_map/finish/pallas_call | solution.py:467
  172.5 4.8 %collective-permute-done.22 = bf16[512,512]{1,0:T(8,128)(2,1)S(1)} collective-permute-done((bf16[512,512]{1,0:T(8,128)(2,1)}, bf16[512,512]{1,0:T(8,128)(2,1)S(1)}, u32[]{:S(2)}, u32[]{:S(2)}) %collective-permute-start.22) | collective-permute-done | bytes 524320 | tf_op jit(solution)/shard_map/ppermute | solution.py:58
  (94 shorter events, 23.0 us)
Async XLA Ops:
  7.2 73.9 %all-gather.2.cloned.1.call-start = ((), (), s32[]{:S(2)}) async-start(), calls=%async_computation.1 | async-start | bytes 2621440 | tf_op jit(solution)/shard_map/all_gather | solution.py:297
  9.5 33.3 %copy-start.9 = (bf16[512,512]{1,0:T(8,128)(2,1)S(1)}, bf16[512,512]{1,0:T(8,128)(2,1)}, u32[]{:S(2)}) copy-start(bf16[512,512]{1,0:T(8,128)(2,1)} %rest_0_.1) | copy-start | bytes 1572868
  9.5 20.5 %collective-permute-start.2 = (bf16[3,256,512]{2,1,0:T(8,128)(2,1)S(1)}, bf16[3,256,512]{2,1,0:T(8,128)(2,1)S(1)}, u32[]{:S(2)}, u32[]{:S(2)}) collective-permute-start(bf16[3,256,512]{2,1,0:T(8,128)(2,1)S(1)} %pad_maximum_fusion), channel_id=1, source_target_pairs={{0,4},{4,0},{8,12},{12,8},{16,20},{20,16},{24,28},{28,24},{1,5},{5... | collective-permute-start | bytes 2359304 | tf_op jit(solution)/shard_map/ppermute | solution.py:62
  12.6 17.5 %collective-permute-start = (bf16[2,256,512]{2,1,0:T(8,128)(2,1)S(1)}, bf16[2,256,512]{2,1,0:T(8,128)(2,1)S(1)}, u32[]{:S(2)}, u32[]{:S(2)}) collective-permute-start(bf16[2,256,512]{2,1,0:T(8,128)(2,1)S(1)} %pad_maximum_fusion.1), channel_id=1, source_target_pairs={{0,8},{4,12},{8,16},{12,20},{16,24},{20,28},{1,9},{5,13},{9,17},{1... | collective-permute-start | bytes 1572872 | tf_op jit(solution)/shard_map/ppermute | solution.py:27
  16.1 15.0 %collective-permute-start.1 = (bf16[2,256,512]{2,1,0:T(8,128)(2,1)S(1)}, bf16[2,256,512]{2,1,0:T(8,128)(2,1)S(1)}, u32[]{:S(2)}, u32[]{:S(2)}) collective-permute-start(bf16[2,256,512]{2,1,0:T(8,128)(2,1)S(1)} %pad_maximum_fusion.1), channel_id=1, source_target_pairs={{8,0},{12,4},{16,8},{20,12},{24,16},{28,20},{9,1},{13,5},{17,9},{2... | collective-permute-start | bytes 1572872 | tf_op jit(solution)/shard_map/ppermute | solution.py:27
  30.1 42.4 %copy-start.5 = (bf16[3,256,512]{2,1,0:T(8,128)(2,1)}, bf16[3,256,512]{2,1,0:T(8,128)(2,1)S(1)}, u32[]{:S(2)}) copy-start(bf16[3,256,512]{2,1,0:T(8,128)(2,1)S(1)} %collective-permute-done.2.rest_2_) | copy-start | bytes 2359300
  31.1 41.4 %copy-start.7 = (bf16[2,256,512]{2,1,0:T(8,128)(2,1)}, bf16[2,256,512]{2,1,0:T(8,128)(2,1)S(1)}, u32[]{:S(2)}) copy-start(bf16[2,256,512]{2,1,0:T(8,128)(2,1)S(1)} %collective-permute-done.1.rest_1_) | copy-start | bytes 1572868
  32.0 37.2 %copy-start.24 = (s32[16,3]{0,1:T(4,128)S(1)}, s32[16,3]{0,1:T(4,128)}, u32[]{:S(2)}) copy-start(s32[16,3]{0,1:T(4,128)} %param.10) | copy-start | bytes 580
  32.0 139.3 %reduce-scatter.2.cloned.1.call-start = ((), (), s32[]{:S(2)}) async-start(), calls=%async_computation.2 | async-start | bytes 2621440 | tf_op jit(solution)/shard_map/reduce_scatter | solution.py:384
  32.1 10.7 %collective-permute-start.4 = (bf16[2,128,512]{2,1,0:T(8,128)(2,1)S(1)}, bf16[2,128,512]{2,1,0:T(8,128)(2,1)S(1)}, u32[]{:S(2)}, u32[]{:S(2)}) collective-permute-start(bf16[2,128,512]{2,1,0:T(8,128)(2,1)S(1)} %fusion.7), channel_id=1, source_target_pairs={{0,16},{1,17},{2,18},{3,19}} | collective-permute-start | bytes 786440 | tf_op jit(solution)/shard_map/ppermute | solution.py:303
  42.8 9.4 %collective-permute-start.7 = (bf16[512,512]{1,0:T(8,128)(2,1)S(1)}, bf16[512,512]{1,0:T(8,128)(2,1)}, u32[]{:S(2)}, u32[]{:S(2)}) collective-permute-start(bf16[512,512]{1,0:T(8,128)(2,1)S(1)} %copy-done.9), channel_id=1, source_target_pairs={{0,8},{4,12},{8,0},{12,4},{16,24},{20,28},{24,16},{28,20},{1,9},{5... | collective-permute-start | bytes 1572872 | tf_op jit(solution)/shard_map/ppermute | solution.py:309
  42.8 13.8 %collective-permute-start.8 = (bf16[512,512]{1,0:T(8,128)(2,1)S(1)}, bf16[512,512]{1,0:T(8,128)(2,1)}, u32[]{:S(2)}, u32[]{:S(2)}) collective-permute-start(bf16[512,512]{1,0:T(8,128)(2,1)S(1)} %copy-done.9), channel_id=1, source_target_pairs={{8,16},{12,20},{16,8},{20,12},{9,17},{13,21},{17,9},{21,13},{10,18... | collective-permute-start | bytes 1572872 | tf_op jit(solution)/shard_map/ppermute | solution.py:309
  52.2 5.7 %collective-permute-start.10 = (bf16[512,512]{1,0:T(8,128)(2,1)}, bf16[512,512]{1,0:T(8,128)(2,1)}, u32[]{:S(2)}, u32[]{:S(2)}) collective-permute-start(bf16[512,512]{1,0:T(8,128)(2,1)} %collective-permute-done.7.rest_1_), channel_id=1, source_target_pairs={{8,16},{12,20},{16,8},{20,12},{9,17},{13,21},{17,9},{21,13},{10,18... | collective-permute-start | bytes 1572872 | tf_op jit(solution)/shard_map/ppermute | solution.py:309
  54.5 17.9 %collective-permute-start.3 = (bf16[2,256,512]{2,1,0:T(8,128)(2,1)}, bf16[2,256,512]{2,1,0:T(8,128)(2,1)}, u32[]{:S(2)}, u32[]{:S(2)}) collective-permute-start(bf16[2,256,512]{2,1,0:T(8,128)(2,1)} %broadcast_select_fusion), channel_id=1, source_target_pairs={{0,4},{8,12},{16,20},{12,8},{20,16},{28,24},{1,5},{9,13},{17,21},{... | collective-permute-start | bytes 1572872 | tf_op jit(solution)/shard_map/ppermute | solution.py:300
  56.6 23.2 %collective-permute-start.9 = (bf16[512,512]{1,0:T(8,128)(2,1)}, bf16[512,512]{1,0:T(8,128)(2,1)}, u32[]{:S(2)}, u32[]{:S(2)}) collective-permute-start(bf16[512,512]{1,0:T(8,128)(2,1)} %collective-permute-done.8.rest_2_), channel_id=1, source_target_pairs={{8,0},{12,4},{16,24},{20,28},{9,1},{13,5},{17,25},{21,29},{10,2},{... | collective-permute-start | bytes 1572872 | tf_op jit(solution)/shard_map/ppermute | solution.py:309
  57.9 23.2 %collective-permute-start.11 = (bf16[512,512]{1,0:T(8,128)(2,1)}, bf16[512,512]{1,0:T(8,128)(2,1)}, u32[]{:S(2)}, u32[]{:S(2)}) collective-permute-start(bf16[512,512]{1,0:T(8,128)(2,1)} %collective-permute-done.10.rest_4_), channel_id=1, source_target_pairs={{8,0},{12,4},{16,24},{20,28},{9,1},{13,5},{17,25},{21,29},{10,2},{... | collective-permute-start | bytes 1572872 | tf_op jit(solution)/shard_map/ppermute | solution.py:309
  59.3 13.1 %collective-permute-start.5 = (bf16[2,128,512]{2,1,0:T(8,128)(2,1)S(1)}, bf16[2,128,512]{2,1,0:T(8,128)(2,1)}, u32[]{:S(2)}, u32[]{:S(2)}) collective-permute-start(bf16[2,128,512]{2,1,0:T(8,128)(2,1)S(1)} %fusion.9), channel_id=1, source_target_pairs={{4,28},{0,12},{16,20},{8,24},{5,29},{1,13},{17,21},{9,25},{6,30},{... | collective-permute-start | bytes 786440 | tf_op jit(solution)/shard_map/ppermute | solution.py:305
  79.7 8.9 %collective-permute-start.6 = (bf16[256,512]{1,0:T(8,128)(2,1)S(1)}, bf16[256,512]{1,0:T(8,128)(2,1)S(1)}, u32[]{:S(2)}, u32[]{:S(2)}) collective-permute-start(bf16[256,512]{1,0:T(8,128)(2,1)S(1)} %get-tuple-element.34.mixed_ref.rest_2_.rest_5_), channel_id=1, source_target_pairs={{0,4},{4,0},{8,12},{12,8},{16,20},{20,16},{24,28},{28,24},{1,5},{5... | collective-permute-start | bytes 786440 | tf_op jit(solution)/shard_map/ppermute | solution.py:62
  86.9 20.5 %collective-permute-start.13 = (bf16[256,512]{1,0:T(8,128)(2,1)}, bf16[256,512]{1,0:T(8,128)(2,1)}, u32[]{:S(2)}, u32[]{:S(2)}) collective-permute-start(bf16[256,512]{1,0:T(8,128)(2,1)} %get-tuple-element.37), channel_id=1, source_target_pairs={{0,4},{4,0},{8,12},{12,8},{16,20},{20,16},{24,28},{28,24},{1,5},{5... | collective-permute-start | bytes 786440 | tf_op jit(solution)/shard_map/ppermute | solution.py:62
  95.8 12.7 %copy-start.20 = (bf16[256,512]{1,0:T(8,128)(2,1)S(1)}, bf16[256,512]{1,0:T(8,128)(2,1)}, u32[]{:S(2)}) copy-start(bf16[256,512]{1,0:T(8,128)(2,1)} %q_ref.5) | copy-start | bytes 786436
  97.8 23.9 %collective-permute-start.15 = (bf16[512,512]{1,0:T(8,128)(2,1)S(1)}, bf16[512,512]{1,0:T(8,128)(2,1)S(1)}, u32[]{:S(2)}, u32[]{:S(2)}) collective-permute-start(bf16[512,512]{1,0:T(8,128)(2,1)S(1)} %get-tuple-element.49), channel_id=1, source_target_pairs={{0,8},{4,12},{8,16},{12,20},{16,24},{20,28},{24,0},{28,4},{1,9},{5... | collective-permute-start | bytes 1572872 | tf_op jit(solution)/shard_map/ppermute | solution.py:58
  101.1 24.6 %collective-permute-start.16 = (bf16[512,512]{1,0:T(8,128)(2,1)S(1)}, bf16[512,512]{1,0:T(8,128)(2,1)S(1)}, u32[]{:S(2)}, u32[]{:S(2)}) collective-permute-start(bf16[512,512]{1,0:T(8,128)(2,1)S(1)} %get-tuple-element.50), channel_id=1, source_target_pairs={{0,24},{4,28},{8,0},{12,4},{16,8},{20,12},{24,16},{28,20},{1,25},{... | collective-permute-start | bytes 1572872 | tf_op jit(solution)/shard_map/ppermute | solution.py:58
  112.4 15.9 %collective-permute-start.17 = (bf16[2,384,512]{2,1,0:T(8,128)(2,1)S(1)}, bf16[2,384,512]{2,1,0:T(8,128)(2,1)S(1)}, u32[]{:S(2)}, u32[]{:S(2)}) collective-permute-start(bf16[2,384,512]{2,1,0:T(8,128)(2,1)S(1)} %first_grad.1), channel_id=1, source_target_pairs={{0,4},{4,0},{8,12},{12,8},{16,20},{20,16},{24,28},{28,24},{1,5},{5... | collective-permute-start | bytes 2359304 | tf_op jit(solution)/shard_map/ppermute | solution.py:62
  128.7 21.6 %collective-permute-start.18 = (bf16[2,256,512]{2,1,0:T(8,128)(2,1)S(1)}, bf16[2,256,512]{2,1,0:T(8,128)(2,1)S(1)}, u32[]{:S(2)}, u32[]{:S(2)}) collective-permute-start(bf16[2,256,512]{2,1,0:T(8,128)(2,1)S(1)} %get-tuple-element.55), channel_id=1, source_target_pairs={{8,0},{12,4},{16,8},{20,12},{24,16},{28,20},{9,1},{13,5},{17,9},{2... | collective-permute-start | bytes 1572872 | tf_op jit(solution)/shard_map/ppermute | solution.py:27
  130.0 20.3 %collective-permute-start.19 = (bf16[2,256,512]{2,1,0:T(8,128)(2,1)S(1)}, bf16[2,256,512]{2,1,0:T(8,128)(2,1)S(1)}, u32[]{:S(2)}, u32[]{:S(2)}) collective-permute-start(bf16[2,256,512]{2,1,0:T(8,128)(2,1)S(1)} %get-tuple-element.56), channel_id=1, source_target_pairs={{0,8},{4,12},{8,16},{12,20},{16,24},{20,28},{1,9},{5,13},{9,17},{1... | collective-permute-start | bytes 1572872 | tf_op jit(solution)/shard_map/ppermute | solution.py:27
  134.6 15.7 %collective-permute-start.21 = (bf16[2,128,512]{2,1,0:T(8,128)(2,1)S(1)}, bf16[2,128,512]{2,1,0:T(8,128)(2,1)S(1)}, u32[]{:S(2)}, u32[]{:S(2)}) collective-permute-start(bf16[2,128,512]{2,1,0:T(8,128)(2,1)S(1)} %get-tuple-element.57), channel_id=1, source_target_pairs={{24,0},{25,1},{26,2},{27,3}} | collective-permute-start | bytes 786440 | tf_op jit(solution)/shard_map/ppermute | solution.py:459
  135.9 31.0 %collective-permute-start.20 = (bf16[2,128,512]{2,1,0:T(8,128)(2,1)S(1)}, bf16[2,128,512]{2,1,0:T(8,128)(2,1)S(1)}, u32[]{:S(2)}, u32[]{:S(2)}) collective-permute-start(bf16[2,128,512]{2,1,0:T(8,128)(2,1)S(1)} %get-tuple-element.57), channel_id=1, source_target_pairs={{16,0},{17,1},{18,2},{19,3}} | collective-permute-start | bytes 786440 | tf_op jit(solution)/shard_map/ppermute | solution.py:459
  137.2 30.6 %collective-permute-start.14 = (bf16[2,256,512]{2,1,0:T(8,128)(2,1)S(1)}, bf16[2,256,512]{2,1,0:T(8,128)(2,1)S(1)}, u32[]{:S(2)}, u32[]{:S(2)}) collective-permute-start(bf16[2,256,512]{2,1,0:T(8,128)(2,1)S(1)} %get-tuple-element.46), channel_id=1, source_target_pairs={{0,4},{4,0},{8,12},{12,8},{16,20},{20,16},{24,28},{28,24},{1,5},{5... | collective-permute-start | bytes 1572872 | tf_op jit(solution)/shard_map/ppermute | solution.py:62
  150.3 27.0 %collective-permute-start.22 = (bf16[512,512]{1,0:T(8,128)(2,1)}, bf16[512,512]{1,0:T(8,128)(2,1)S(1)}, u32[]{:S(2)}, u32[]{:S(2)}) collective-permute-start(bf16[512,512]{1,0:T(8,128)(2,1)} %get-tuple-element.62), channel_id=1, source_target_pairs={{0,16},{4,20},{8,24},{12,28},{16,0},{20,4},{24,8},{28,12},{1,17},{... | collective-permute-start | bytes 1572872 | tf_op jit(solution)/shard_map/ppermute | solution.py:58
  150.3 18.3 %copy-start.21 = (bf16[2,256,512]{2,1,0:T(8,128)(2,1)}, bf16[2,256,512]{2,1,0:T(8,128)(2,1)S(1)}, u32[]{:S(2)}) copy-start(bf16[2,256,512]{2,1,0:T(8,128)(2,1)S(1)} %collective-permute-done.18.b_ref) | copy-start | bytes 1572868
  150.3 17.5 %copy-start.22 = (bf16[2,256,512]{2,1,0:T(8,128)(2,1)}, bf16[2,256,512]{2,1,0:T(8,128)(2,1)S(1)}, u32[]{:S(2)}) copy-start(bf16[2,256,512]{2,1,0:T(8,128)(2,1)S(1)} %collective-permute-done.19.c_ref) | copy-start | bytes 1572868
  172.4 6.7 %collective-permute-start.12 = (bf16[256,512]{1,0:T(8,128)(2,1)S(1)}, bf16[256,512]{1,0:T(8,128)(2,1)S(1)}, u32[]{:S(2)}, u32[]{:S(2)}) collective-permute-start(bf16[256,512]{1,0:T(8,128)(2,1)S(1)} %get-tuple-element.68), channel_id=1, source_target_pairs={{0,4},{4,0},{8,12},{12,8},{16,20},{20,16},{24,28},{28,24},{1,5},{5... | collective-permute-start | bytes 786440 | tf_op jit(solution)/shard_map/ppermute | solution.py:62
  (18 other events, 85.7 us)
Sparse Core Ops, SparseCore 0:
  32.1 23.1 all-gather.1
  93.4 37.5 reduce-scatter.1
where the time goes:
time: 188 us; the launch traced here: 187 us
  waiting for transfers between devices  73.8 us (39%)
  starting transfers between devices  50.2 us (27%)
  Pallas kernels  29.7 us (16%)
  between operations  14.5 us (8%)
  local copies, waits for them, and re-layouts  11.1 us (6%)
  other arithmetic  7.63 us (4%)
    ppermute x2, waiting for transfers between devices, local(): got = tied(lax.ppermute(near, 'ctx', [(c, 0)]), back_down, back_up)  29.6 us
    ppermute x6, waiting for transfers between devices, swapped(): lax.ppermute(piece, 'ctx', [(2 * z + n, 2 * z + 1 - n) for z in places fo...  15.9 us
    ppermute x4, starting transfers between devices, shifted(): lax.ppermute(x, 'ctx', [(i, i + by) for i in range(peers) if 0 <= i + by...  10.7 us
    ppermute x1, starting transfers between devices, local(): late = lax.ppermute(known, 'ctx', [(1, 7), (0, 3), (4, 5), (2, 6)])  9.93 us
    ppermute x3, starting transfers between devices, turned(): lax.ppermute(x, 'ctx', [(2 * z + n, 2 * ((z + by) % length) + n) for z in...  9.55 us
    ppermute x5, waiting for transfers between devices, between(): lax.ppermute(x, 'ctx', [(2 * a + n, 2 * b + n) for a, b in places for n i...  9.26 us
    pallas_call x1, Pallas kernels, local(): pl.pallas_call(functools.partial(bwd_kernel, offsets, early, per_dev, sca...  9.04 us
    unnamed x51, local copies, waits for them, and re-layouts  8.94 us
  transfers between devices with their start and end apart: 25, of which 12 were waited for; matrix products, arithmetic and copies ran while one was open for 3% of the time, Pallas kernels for 16%

commit v1 on v0

--- a/solution.py
+++ b/solution.py
@@ -94,15 +94,12 @@
     return held_ref[b]
 
 
-def grads_kernel(length, rows_hbm_ref, *rest):
+def grads_kernel(length, rows_ref, *rest):
     pieces = rest[:6]
-    grad_ref, other_ref, rows_ref, held_ref, sems, row_sem = rest[6:]
+    grad_ref, other_ref, held_ref, sems = rest[6:]
     tokens = grad_ref.shape[0]
     width = rows_ref.shape[1] // length
-    rows = pltpu.make_async_copy(rows_hbm_ref, rows_ref, row_sem)
-    rows.start()
     start_weights(pieces, held_ref, sems)
-    rows.wait()
     total = None
     for b in range(length):
         part = mm(rows_ref[:, b * width : (b + 1) * width], weight_at(held_ref, sems, b), NN)
@@ -124,17 +121,14 @@
         out_ref[tokens:, columns] = mm(other_ref[...], weight, NT).astype(jnp.bfloat16)
 
 
-def weight_kernel(length, rows_hbm_ref, mixed_ref, other_ref, own_ref, *rest):
+def weight_kernel(length, rows_ref, mixed_ref, other_ref, own_ref, *rest):
     sends = rest[: length - 1]
-    rows_ref, both_ref, row_sem = rest[length - 1 :]
+    (both_ref,) = rest[length - 1 :]
     width = own_ref.shape[0]
     tokens = mixed_ref.shape[0]
     place = lax.div(lax.axis_index("ctx"), 2)
-    rows = pltpu.make_async_copy(rows_hbm_ref, rows_ref, row_sem)
-    rows.start()
     both_ref[:tokens, :] = mixed_ref[...]
     both_ref[tokens:, :] = other_ref[...]
-    rows.wait()
     for n, out_ref in enumerate((own_ref,) + sends):
         column = pl.multiple_of(lax.rem(place + n, length) * width, 128)
         out_ref[...] = mm(rows_ref[:, pl.ds(column, width)], both_ref[...], TN).astype(out_ref.dtype)
@@ -282,7 +276,6 @@
     places = 1 + len(offsets)
     smem = pl.BlockSpec(memory_space=pltpu.SMEM)
     whole = pl.BlockSpec(memory_space=pltpu.VMEM)
-    distant = pl.BlockSpec(memory_space=pltpu.HBM)
     anywhere = pl.BlockSpec(memory_space=pl.ANY)
     width = out_weight.shape[0]
 
@@ -298,19 +291,18 @@
         sent = jnp.where(side == 0, after, before)
         hop = [(2 * z, 2 * z + 1) for z in range(length - 1)] + [(2 * z + 1, 2 * z) for z in range(1, length)]
         across = lax.ppermute(sent, "ctx", hop)
-        known = jnp.where(run == 1, beside[:2, :BLK], head_rows)
-        known = jnp.where(run == 2, before[:, :BLK], known)
-        middle_rows = lax.ppermute(head_rows, "ctx", [(0, length)])
-        known = jnp.where(run == length, middle_rows, known)
-        late = lax.ppermute(known, "ctx", [(1, 7), (0, 3), (4, 5), (2, 6)])
-        first = jnp.where((run == 3) | (run > length), late, known)
+        known = jnp.where(run == 2, before[:, :BLK], head_rows)
+        known = jnp.where((run == 3) | (run == 4), lax.ppermute(known, "ctx", [(2, 4), (0, 3)]), known)
+        known = jnp.where(run == 1, beside[:2, :BLK], known)
+        first = jnp.where(run > length, lax.ppermute(known, "ctx", [(4, 6), (3, 5), (2, 7)]), known)
 
         def between(x, places):
             return lax.ppermute(x, "ctx", [(2 * a + n, 2 * b + n) for a, b in places for n in range(2)])
 
-        base = tied(out_weight, before, after, middle_rows)
+        base = tied(out_weight, before, after)
         near = between(base, ((0, 1), (1, 0), (2, 3), (3, 2)))
         middle = between(base, ((1, 2), (2, 1)))
+        near, middle, across, first = lax.optimization_barrier((near, middle, across, first))
         far = between(near, ((1, 2), (2, 1)))
         outer = between(middle, ((1, 0), (2, 3)))
         farthest = between(far, ((1, 0), (2, 3)))
@@ -356,21 +348,32 @@
 
     if direct:
         held = [pltpu.VMEM((length, width, features), jnp.bfloat16), pltpu.SemaphoreType.DMA((length,))]
+        mixed_other = swapped(mixed, range(length))
+        own_part, *weight_parts = pl.pallas_call(
+            functools.partial(weight_kernel, length),
+            in_specs=[whole] + [whole] * 2,
+            out_specs=[whole] * length,
+            out_shape=[jax.ShapeDtypeStruct((width, features), jnp.float32)]
+            + [jax.ShapeDtypeStruct((width, features), jnp.bfloat16)] * (length - 1),
+            scratch_shapes=[pltpu.VMEM((2 * tokens, features), jnp.bfloat16)],
+            compiler_params=pltpu.CompilerParams(vmem_limit_bytes=32 * 1024 * 1024),
+            cost_estimate=CHEAP,
+            name="weight_part",
+        )(grad_side, mixed, mixed_other)
         own_grad, other_grad = pl.pallas_call(
             functools.partial(grads_kernel, length),
-            in_specs=[distant] + [anywhere] * 6,
+            in_specs=[whole] + [anywhere] * 6,
             out_specs=[whole] * 2,
             out_shape=[
                 jax.ShapeDtypeStruct((tokens, features), jnp.float32),
                 jax.ShapeDtypeStruct((tokens, features), jnp.bfloat16),
             ],
-            scratch_shapes=[pltpu.VMEM((2 * tokens, length * width), jnp.bfloat16)] + held + [pltpu.SemaphoreType.DMA],
+            scratch_shapes=held,
             compiler_params=pltpu.CompilerParams(vmem_limit_bytes=32 * 1024 * 1024),
             cost_estimate=CHEAP,
             name="project_grad",
-        )(grad_side, *weight_pieces)
+        )(tied(grad_side, own_part), *weight_pieces)
         mixed_grad = (own_grad + swapped(other_grad, range(length)).astype(jnp.float32)).astype(jnp.bfloat16)
-        mixed_other = tied(swapped(mixed, range(length)), other_grad)
         partial_out = pl.pallas_call(
             functools.partial(outs_kernel, length),
             in_specs=[whole] * 2 + [anywhere] * 6,
@@ -380,28 +383,13 @@
             compiler_params=pltpu.CompilerParams(vmem_limit_bytes=32 * 1024 * 1024),
             cost_estimate=CHEAP,
             name="project_out",
-        )(mixed, mixed_other, *weight_pieces)
+        )(mixed, tied(mixed_other, other_grad), *weight_pieces)
         scattered = lax.psum_scatter(partial_out, "head", scatter_dimension=1, tiled=True)
         mine, theirs = scattered[:tokens], swapped(scattered[tokens:], range(length))
         attended = jnp.where(
             side == 0, jnp.concatenate([mine, theirs], axis=1), jnp.concatenate([theirs, mine], axis=1)
         )
-        own_part, *weight_parts = pl.pallas_call(
-            functools.partial(weight_kernel, length),
-            in_specs=[distant] + [whole] * 2,
-            out_specs=[whole] * length,
-            out_shape=[jax.ShapeDtypeStruct((width, features), jnp.float32)]
-            + [jax.ShapeDtypeStruct((width, features), jnp.bfloat16)] * (length - 1),
-            scratch_shapes=[
-                pltpu.VMEM((2 * tokens, length * width), jnp.bfloat16),
-                pltpu.VMEM((2 * tokens, features), jnp.bfloat16),
-                pltpu.SemaphoreType.DMA,
-            ],
-            compiler_params=pltpu.CompilerParams(vmem_limit_bytes=32 * 1024 * 1024),
-            cost_estimate=CHEAP,
-            name="weight_part",
-        )(grad_side, mixed, mixed_other)
-        mixed_grad = tied(mixed_grad, own_part, partial_out)
+        mixed_grad = tied(mixed_grad, partial_out)
         weight_turns = [turned(weight_parts[n - 1], n, length) for n in (1, 3)]
     else:
         partial_out = mm(mixed, full_weight, NT).astype(jnp.bfloat16)
@@ -472,7 +460,7 @@
             out_shape=[jax.ShapeDtypeStruct((tokens, features), jnp.bfloat16)] * 2,
             cost_estimate=CHEAP,
             name="finish",
-        )(run_word, own, back_pair, back_down, back_up, first_sum)
+        )(run_word, tied(own, theirs), back_pair, back_down, back_up, first_sum)
 
     else:
         first_sum = to_first(early_grads.astype(jnp.float32))

time: 188 us -> 212 us (1.13)
  waiting for transfers between devices: 73.8 us -> 88.7 us
  local copies, waits for them, and re-layouts: 11.1 us -> 15.7 us
  other arithmetic: 7.63 us -> 11.1 us
    ppermute x2, starting transfers between devices: 14.4 us -> 4.22 us  [the longest x1 2.87 us: local(): lax.ppermute(known, 'ctx', [(2, 4), (0, 3)])]
    ppermute x6, waiting for transfers between devices: 15.9 us -> 23.6 us  [swapped(): lax.ppermute(piece, 'ctx', [(2 * z + n, 2 * z + 1 - n) for z in places fo...]
    ppermute x2, waiting for transfers between devices: 29.6 us -> 36.6 us  [local(): got = tied(lax.ppermute(near, 'ctx', [(c, 0)]), back_down, back_up)]
    ppermute x3, starting transfers between devices: 9.55 us -> 15.4 us  [turned(): lax.ppermute(x, 'ctx', [(2 * z + n, 2 * ((z + by) % length) + n) for z in...]
    unnamed x51 -> x69, local copies, waits for them, and re-layouts: 8.94 us -> 13.5 us
    ppermute x5, waiting for transfers between devices: 9.26 us -> 13.8 us  [between(): lax.ppermute(x, 'ctx', [(2 * a + n, 2 * b + n) for a, b in places for n i...]
    ppermute x5, starting transfers between devices: 5.48 us -> 9.42 us  [between(): lax.ppermute(x, 'ctx', [(2 * a + n, 2 * b + n) for a, b in places for n i...]
    ppermute x3, waiting for transfers between devices: 8.71 us -> 4.86 us  [turned(): lax.ppermute(x, 'ctx', [(2 * z + n, 2 * ((z + by) % length) + n) for z in...]
  transfers between devices with their start and end apart: 25 -> 25, of which waited for: 12 -> 10; matrix products, arithmetic and copies ran while one was open for 3% -> 5% of each run, Pallas kernels for 16% -> 11%
where the time goes in v1:
time: 212 us; the launch traced here: 211 us
  waiting for transfers between devices  88.7 us (42%)
  starting transfers between devices  50.4 us (24%)
  Pallas kernels  30.1 us (14%)
  local copies, waits for them, and re-layouts  15.7 us (7%)
  between operations  14.5 us (7%)
  other arithmetic  11.1 us (5%)
    ppermute x2, waiting for transfers between devices, local(): got = tied(lax.ppermute(near, 'ctx', [(c, 0)]), back_down, back_up)  36.6 us
    ppermute x6, waiting for transfers between devices, swapped(): lax.ppermute(piece, 'ctx', [(2 * z + n, 2 * z + 1 - n) for z in places fo...  23.6 us
    ppermute x3, starting transfers between devices, turned(): lax.ppermute(x, 'ctx', [(2 * z + n, 2 * ((z + by) % length) + n) for z in...  15.4 us
    ppermute x5, waiting for transfers between devices, between(): lax.ppermute(x, 'ctx', [(2 * a + n, 2 * b + n) for a, b in places for n i...  13.8 us
    unnamed x69, local copies, waits for them, and re-layouts  13.5 us
    ppermute x4, starting transfers between devices, shifted(): lax.ppermute(x, 'ctx', [(i, i + by) for i in range(peers) if 0 <= i + by...  11.7 us
    ppermute x1, waiting for transfers between devices, local(): lax.ppermute(known, 'ctx', [(2, 4), (0, 3)])  9.83 us
    ppermute x5, starting transfers between devices, between(): lax.ppermute(x, 'ctx', [(2 * a + n, 2 * b + n) for a, b in places for n i...  9.42 us
  transfers between devices with their start and end apart: 25, of which 10 were waited for; matrix products, arithmetic and copies ran while one was open for 5% of the time, Pallas kernels for 11%

profile of v1, /device:TPU:0, one launch (start us, length us, event | category | flops | bytes accessed | tf_op | source)
XLA Modules:
  0.0 210.6 jit_solution(12838080155746324146)
XLA Ops:
  9.6 3.0 %collective-permute-start.2 = (bf16[3,256,512]{2,1,0:T(8,128)(2,1)S(1)}, bf16[3,256,512]{2,1,0:T(8,128)(2,1)S(1)}, u32[]{:S(2)}, u32[]{:S(2)}) collective-permute-start(bf16[3,256,512]{2,1,0:T(8,128)(2,1)S(1)} %pad_maximum_fusion), channel_id=1, source_target_pairs={{0,4},{4,0},{8,12},{12,8},{16,20},{20,16},{24,28},{28,24},{1,5},{5... | collective-permute-start | bytes 2359304 | tf_op jit(solution)/shard_map/ppermute | solution.py:62
  13.9 4.6 %collective-permute-start = (bf16[2,256,512]{2,1,0:T(8,128)(2,1)S(1)}, bf16[2,256,512]{2,1,0:T(8,128)(2,1)S(1)}, u32[]{:S(2)}, u32[]{:S(2)}) collective-permute-start(bf16[2,256,512]{2,1,0:T(8,128)(2,1)S(1)} %pad_maximum_fusion.1), channel_id=1, source_target_pairs={{0,8},{4,12},{8,16},{12,20},{16,24},{20,28},{1,9},{5,13},{9,17},{1... | collective-permute-start | bytes 1572872 | tf_op jit(solution)/shard_map/ppermute | solution.py:27
  18.5 11.6 %collective-permute-done.2.rest_2_ = bf16[3,256,512]{2,1,0:T(8,128)(2,1)S(1)} collective-permute-done((bf16[3,256,512]{2,1,0:T(8,128)(2,1)S(1)}, bf16[3,256,512]{2,1,0:T(8,128)(2,1)S(1)}, u32[]{:S(2)}, u32[]{:S(2)}) %collective-permute-start.2) | collective-permute-done | bytes 786464 | tf_op jit(solution)/shard_map/ppermute | solution.py:62
  31.8 4.7 %collective-permute-start.3 = (bf16[512,512]{1,0:T(8,128)(2,1)S(1)}, bf16[512,512]{1,0:T(8,128)(2,1)}, u32[]{:S(2)}, u32[]{:S(2)}) collective-permute-start(bf16[512,512]{1,0:T(8,128)(2,1)S(1)} %copy-done.4), channel_id=1, source_target_pairs={{0,8},{4,12},{8,0},{12,4},{16,24},{20,28},{24,16},{28,20},{1,9},{5... | collective-permute-start | bytes 1572872 | tf_op jit(solution)/shard_map/ppermute | solution.py:300
  36.5 2.9 %collective-permute-start.6 = (bf16[2,128,512]{2,1,0:T(8,128)(2,1)S(1)}, bf16[2,128,512]{2,1,0:T(8,128)(2,1)S(1)}, u32[]{:S(2)}, u32[]{:S(2)}) collective-permute-start(bf16[2,128,512]{2,1,0:T(8,128)(2,1)S(1)} %fusion.8), channel_id=1, source_target_pairs={{8,16},{0,12},{9,17},{1,13},{10,18},{2,14},{11,19},{3,15}} | collective-permute-start | bytes 786440 | tf_op jit(solution)/shard_map/ppermute | solution.py:295
  40.3 2.1 collective-permute-start.5
  42.3 9.8 %collective-permute-done.6 = bf16[2,128,512]{2,1,0:T(8,128)(2,1)S(1)} collective-permute-done((bf16[2,128,512]{2,1,0:T(8,128)(2,1)S(1)}, bf16[2,128,512]{2,1,0:T(8,128)(2,1)S(1)}, u32[]{:S(2)}, u32[]{:S(2)}) %collective-permute-start.6) | collective-permute-done | bytes 262176 | tf_op jit(solution)/shard_map/ppermute | solution.py:295
  52.9 1.4 collective-permute-start.7
  54.3 1.7 broadcast_select_fusion.1.rest_4_.rest_1_
  56.0 1.5 collective-permute-start.10
  58.7 1.3 collective-permute-start.11
  62.0 6.2 %attend.1 = (bf16[256,512]{1,0:T(8,128)(2,1)S(1)}, f32[4,1,256]{2,1,0:T(1,128)S(1)}) custom-call(s32[1]{0:T(128)} %bitcast.run_ref, s32[16,3]{1,0:T(8,128)S(1)} %copy.11.lists_ref, bf16[256,512]{1,0:T(8,128)(2,1)S(1)} %copy-done.20, bf16[256,512]{1,0:T(8,128)(2,1)S(1)} %copy-done.3, bf16[256,512]{1,0:T(8,128)(2,1)S(1)} %copy-done.2, ...), custom_call_target="tpu_custom_call" | custom-call | flops 1 | bytes 1 | tf_op jit(solution)/shard_map/attend/pallas_call | solution.py:334
  69.0 5.7 %collective-permute-done.8.other_ref = bf16[256,512]{1,0:T(8,128)(2,1)S(1)} collective-permute-done((bf16[256,512]{1,0:T(8,128)(2,1)S(1)}, bf16[256,512]{1,0:T(8,128)(2,1)S(1)}, u32[]{:S(2)}, u32[]{:S(2)}) %collective-permute-start.8) | collective-permute-done | bytes 262176 | tf_op jit(solution)/shard_map/ppermute | solution.py:62
  75.4 1.6 copy-done
  78.9 1.3 weight_part.1
  81.2 1.4 collective-permute-done.9.rest_3_
  82.6 12.4 %collective-permute-done.11.rest_5_ = bf16[512,512]{1,0:T(8,128)(2,1)} collective-permute-done((bf16[512,512]{1,0:T(8,128)(2,1)}, bf16[512,512]{1,0:T(8,128)(2,1)}, u32[]{:S(2)}, u32[]{:S(2)}) %collective-permute-start.11) | collective-permute-done | bytes 524320 | tf_op jit(solution)/shard_map/ppermute | solution.py:300
  95.0 3.3 %project_grad.1 = (f32[256,512]{1,0:T(8,128)S(1)}, bf16[256,512]{1,0:T(8,128)(2,1)}) custom-call(bf16[512,2048]{1,0:T(8,128)(2,1)S(1)} %copy-done.1, bf16[512,512]{1,0:T(8,128)(2,1)S(1)} %copy-done.4, bf16[512,512]{1,0:T(8,128)(2,1)} %collective-permute-done.3.rest_1_, bf16[512,512]{1,0:T(8,128)(2,1)S(1)} %collective-permute-done.4.rest_2_, ...), custom_call_target="tpu_custom_call" | custom-call | flops 1 | bytes 1 | tf_op jit(solution)/shard_map/project_grad/pallas_call | solution.py:363
  101.0 3.9 %project_out.1 = bf16[512,2048]{1,0:T(8,128)(2,1)} custom-call(bf16[256,512]{1,0:T(8,128)(2,1)S(1)} %copy-done.9, bf16[256,512]{1,0:T(8,128)(2,1)S(1)} %copy-done.13, bf16[512,512]{1,0:T(8,128)(2,1)S(1)} %copy-done.4, bf16[512,512]{1,0:T(8,128)(2,1)} %collective-permute-done.3.rest_1_, bf16[512,512]{1,0:T(8,128)(2,1)S(1)} %collective-permute-done.4.rest_2_, ...), custom_call_target="tpu_custom_call" | custom-call | flops 1 | bytes 1 | tf_op jit(solution)/shard_map/project_out/pallas_call | solution.py:377
  104.9 12.7 %collective-permute-start.15 = (bf16[512,512]{1,0:T(8,128)(2,1)}, bf16[512,512]{1,0:T(8,128)(2,1)S(1)}, u32[]{:S(2)}, u32[]{:S(2)}) collective-permute-start(bf16[512,512]{1,0:T(8,128)(2,1)} %copy-done.26), channel_id=1, source_target_pairs={{0,8},{4,12},{8,16},{12,20},{16,24},{20,28},{24,0},{28,4},{1,9},{5... | collective-permute-start | bytes 1572872 | tf_op jit(solution)/shard_map/ppermute | solution.py:58
  119.6 3.8 %first_grad.1 = bf16[2,384,512]{2,1,0:T(8,128)(2,1)S(1)} custom-call(s32[1]{0:T(128)} %bitcast.run_ref, s32[16,3]{1,0:T(8,128)S(1)} %copy.11.lists_ref, bf16[256,512]{1,0:T(8,128)(2,1)S(1)} %copy-done.21, bf16[2,256,512]{2,1,0:T(8,128)(2,1)} %collective-permute-done.5.rest_3_.rest_0_, bf16[2,128,512]{2,1,0:T(8,128)(2,1)S(1)} %copy-done.16, ...), custom_call_target="tpu_custom_call" | custom-call | flops 10000000000 | bytes 1 | tf_op jit(solution)/shard_map/first_grad/pallas_call | solution.py:401
  123.4 1.8 collective-permute-start.17
  125.2 9.0 %attend_grad.1 = (bf16[256,512]{1,0:T(8,128)(2,1)}, f32[2,256,512]{2,1,0:T(8,128)S(1)}, bf16[2,256,512]{2,1,0:T(8,128)(2,1)S(1)}, bf16[2,256,512]{2,1,0:T(8,128)(2,1)S(1)}, bf16[2,256,512]{2,1,0:T(8,128)(2,1)S(1)}) custom-call(s32[1]{0:T(128)} %bitcast.run_ref, s32[16,3]{1,0:T(8,128)S(1)} %copy.11.lists_ref, bf16[256,512]{1,0:T(8,128)(2,1)S(1)} %copy-done.22, ...), custom_call_target="tpu_custom_call" | custom-call | flops 30000001024 | bytes 1 | tf_op jit(solution)/shard_map/attend_grad/pallas_call | solution.py:414
  134.2 4.9 %collective-permute-done.16 = bf16[512,512]{1,0:T(8,128)(2,1)S(1)} collective-permute-done((bf16[512,512]{1,0:T(8,128)(2,1)}, bf16[512,512]{1,0:T(8,128)(2,1)S(1)}, u32[]{:S(2)}, u32[]{:S(2)}) %collective-permute-start.16) | collective-permute-done | bytes 524320 | tf_op jit(solution)/shard_map/ppermute | solution.py:58
  139.1 2.1 %collective-permute-done.17 = bf16[2,384,512]{2,1,0:T(8,128)(2,1)S(1)} collective-permute-done((bf16[2,384,512]{2,1,0:T(8,128)(2,1)S(1)}, bf16[2,384,512]{2,1,0:T(8,128)(2,1)S(1)}, u32[]{:S(2)}, u32[]{:S(2)}) %collective-permute-start.17) | collective-permute-done | bytes 786464 | tf_op jit(solution)/shard_map/ppermute | solution.py:62
  143.4 4.6 %collective-permute-start.19 = (bf16[2,256,512]{2,1,0:T(8,128)(2,1)S(1)}, bf16[2,256,512]{2,1,0:T(8,128)(2,1)S(1)}, u32[]{:S(2)}, u32[]{:S(2)}) collective-permute-start(bf16[2,256,512]{2,1,0:T(8,128)(2,1)S(1)} %get-tuple-element.68), channel_id=1, source_target_pairs={{0,8},{4,12},{8,16},{12,20},{16,24},{20,28},{1,9},{5,13},{9,17},{1... | collective-permute-start | bytes 1572872 | tf_op jit(solution)/shard_map/ppermute | solution.py:27
  148.0 2.7 %collective-permute-start.22 = (bf16[512,512]{1,0:T(8,128)(2,1)S(1)}, bf16[512,512]{1,0:T(8,128)(2,1)S(1)}, u32[]{:S(2)}, u32[]{:S(2)}) collective-permute-start(bf16[512,512]{1,0:T(8,128)(2,1)S(1)} %copy-done.24), channel_id=1, source_target_pairs={{0,16},{4,20},{8,24},{12,28},{16,0},{20,4},{24,8},{28,12},{1,17},{... | collective-permute-start | bytes 1572872 | tf_op jit(solution)/shard_map/ppermute | solution.py:58
  153.3 20.4 %collective-permute-done.21 = bf16[2,128,512]{2,1,0:T(8,128)(2,1)S(1)} collective-permute-done((bf16[2,128,512]{2,1,0:T(8,128)(2,1)S(1)}, bf16[2,128,512]{2,1,0:T(8,128)(2,1)S(1)}, u32[]{:S(2)}, u32[]{:S(2)}) %collective-permute-start.21) | collective-permute-done | bytes 262176 | tf_op jit(solution)/shard_map/ppermute | solution.py:447
  173.7 16.1 %collective-permute-done.20 = bf16[2,128,512]{2,1,0:T(8,128)(2,1)S(1)} collective-permute-done((bf16[2,128,512]{2,1,0:T(8,128)(2,1)S(1)}, bf16[2,128,512]{2,1,0:T(8,128)(2,1)S(1)}, u32[]{:S(2)}, u32[]{:S(2)}) %collective-permute-start.20) | collective-permute-done | bytes 262176 | tf_op jit(solution)/shard_map/ppermute | solution.py:447
  193.0 2.1 %convert_add_fusion.1.first_ref = f32[2,128,512]{2,1,0:T(8,128)} fusion(bf16[2,128,512]{2,1,0:T(8,128)(2,1)} %copy-done.31, bf16[2,128,512]{2,1,0:T(8,128)(2,1)} %copy-done.32, bf16[2,384,512]{2,1,0:T(8,128)(2,1)} %copy-done.19, bf16[2,384,512]{2,1,0:T(8,128)(2,1)} %copy-done.27), kind=kLoop, calls=%fused_computation.14 | loop fusion | flops 917504 | bytes 1572864 | tf_op jit(solution)/shard_map/add | solution.py:448
  195.1 4.2 %collective-permute-done.12 = bf16[256,512]{1,0:T(8,128)(2,1)S(1)} collective-permute-done((bf16[256,512]{1,0:T(8,128)(2,1)S(1)}, bf16[256,512]{1,0:T(8,128)(2,1)S(1)}, u32[]{:S(2)}, u32[]{:S(2)}) %collective-permute-start.12) | collective-permute-done | bytes 262176 | tf_op jit(solution)/shard_map/ppermute | solution.py:62
  201.1 2.6 %finish.1 = (bf16[256,512]{1,0:T(8,128)(2,1)}, bf16[256,512]{1,0:T(8,128)(2,1)}) custom-call(s32[1]{0:T(128)} %bitcast.run_ref, f32[2,256,512]{2,1,0:T(8,128)} %copy-done.14, bf16[2,256,512]{2,1,0:T(8,128)(2,1)} %copy-done.30, bf16[2,256,512]{2,1,0:T(8,128)(2,1)} %copy-done.28, bf16[2,256,512]{2,1,0:T(8,128)(2,1)} %copy-done.29, ...), custom_call_target="tpu_custom_call" | custom-call | flops 1 | bytes 1 | tf_op jit(solution)/shard_map/finish/pallas_call | solution.py:455
  (112 shorter events, 28.8 us)
Async XLA Ops:
  7.2 68.2 %all-gather.2.cloned.1.call-start = ((), (), s32[]{:S(2)}) async-start(), calls=%async_computation.1 | async-start | bytes 2621440 | tf_op jit(solution)/shard_map/all_gather | solution.py:290
  8.4 22.7 %copy-start.4 = (bf16[512,512]{1,0:T(8,128)(2,1)S(1)}, bf16[512,512]{1,0:T(8,128)(2,1)}, u32[]{:S(2)}) copy-start(bf16[512,512]{1,0:T(8,128)(2,1)} %rest_0_.1) | copy-start | bytes 1572868
  9.6 20.5 %collective-permute-start.2 = (bf16[3,256,512]{2,1,0:T(8,128)(2,1)S(1)}, bf16[3,256,512]{2,1,0:T(8,128)(2,1)S(1)}, u32[]{:S(2)}, u32[]{:S(2)}) collective-permute-start(bf16[3,256,512]{2,1,0:T(8,128)(2,1)S(1)} %pad_maximum_fusion), channel_id=1, source_target_pairs={{0,4},{4,0},{8,12},{12,8},{16,20},{20,16},{24,28},{28,24},{1,5},{5... | collective-permute-start | bytes 2359304 | tf_op jit(solution)/shard_map/ppermute | solution.py:62
  12.6 17.5 %collective-permute-start.1 = (bf16[2,256,512]{2,1,0:T(8,128)(2,1)S(1)}, bf16[2,256,512]{2,1,0:T(8,128)(2,1)S(1)}, u32[]{:S(2)}, u32[]{:S(2)}) collective-permute-start(bf16[2,256,512]{2,1,0:T(8,128)(2,1)S(1)} %pad_maximum_fusion.1), channel_id=1, source_target_pairs={{8,0},{12,4},{16,8},{20,12},{24,16},{28,20},{9,1},{13,5},{17,9},{2... | collective-permute-start | bytes 1572872 | tf_op jit(solution)/shard_map/ppermute | solution.py:27
  13.9 16.2 %collective-permute-start = (bf16[2,256,512]{2,1,0:T(8,128)(2,1)S(1)}, bf16[2,256,512]{2,1,0:T(8,128)(2,1)S(1)}, u32[]{:S(2)}, u32[]{:S(2)}) collective-permute-start(bf16[2,256,512]{2,1,0:T(8,128)(2,1)S(1)} %pad_maximum_fusion.1), channel_id=1, source_target_pairs={{0,8},{4,12},{8,16},{12,20},{16,24},{20,28},{1,9},{5,13},{9,17},{1... | collective-permute-start | bytes 1572872 | tf_op jit(solution)/shard_map/ppermute | solution.py:27
  31.0 160.8 %reduce-scatter.2.cloned.1.call-start = ((), (), s32[]{:S(2)}) async-start(), calls=%async_computation.2 | async-start | bytes 2621440 | tf_op jit(solution)/shard_map/reduce_scatter | solution.py:387
  31.1 24.9 %collective-permute-start.4 = (bf16[512,512]{1,0:T(8,128)(2,1)S(1)}, bf16[512,512]{1,0:T(8,128)(2,1)S(1)}, u32[]{:S(2)}, u32[]{:S(2)}) collective-permute-start(bf16[512,512]{1,0:T(8,128)(2,1)S(1)} %copy-done.4), channel_id=1, source_target_pairs={{8,16},{12,20},{16,8},{20,12},{9,17},{13,21},{17,9},{21,13},{10,18... | collective-permute-start | bytes 1572872 | tf_op jit(solution)/shard_map/ppermute | solution.py:300
  31.8 24.2 %collective-permute-start.3 = (bf16[512,512]{1,0:T(8,128)(2,1)S(1)}, bf16[512,512]{1,0:T(8,128)(2,1)}, u32[]{:S(2)}, u32[]{:S(2)}) collective-permute-start(bf16[512,512]{1,0:T(8,128)(2,1)S(1)} %copy-done.4), channel_id=1, source_target_pairs={{0,8},{4,12},{8,0},{12,4},{16,24},{20,28},{24,16},{28,20},{1,9},{5... | collective-permute-start | bytes 1572872 | tf_op jit(solution)/shard_map/ppermute | solution.py:300
  36.5 23.5 %copy-start.33 = (s32[16,3]{0,1:T(4,128)S(1)}, s32[16,3]{0,1:T(4,128)}, u32[]{:S(2)}) copy-start(s32[16,3]{0,1:T(4,128)} %param.10) | copy-start | bytes 580
  36.5 15.6 %collective-permute-start.6 = (bf16[2,128,512]{2,1,0:T(8,128)(2,1)S(1)}, bf16[2,128,512]{2,1,0:T(8,128)(2,1)S(1)}, u32[]{:S(2)}, u32[]{:S(2)}) collective-permute-start(bf16[2,128,512]{2,1,0:T(8,128)(2,1)S(1)} %fusion.8), channel_id=1, source_target_pairs={{8,16},{0,12},{9,17},{1,13},{10,18},{2,14},{11,19},{3,15}} | collective-permute-start | bytes 786440 | tf_op jit(solution)/shard_map/ppermute | solution.py:295
  40.3 15.7 %collective-permute-start.5 = (bf16[2,256,512]{2,1,0:T(8,128)(2,1)}, bf16[2,256,512]{2,1,0:T(8,128)(2,1)}, u32[]{:S(2)}, u32[]{:S(2)}) collective-permute-start(bf16[2,256,512]{2,1,0:T(8,128)(2,1)} %broadcast_select_fusion), channel_id=1, source_target_pairs={{0,4},{8,12},{16,20},{12,8},{20,16},{28,24},{1,5},{9,13},{17,21},{... | collective-permute-start | bytes 1572872 | tf_op jit(solution)/shard_map/ppermute | solution.py:293
  52.9 1.4 collective-permute-start.7
  56.0 2.8 %collective-permute-start.10 = (bf16[512,512]{1,0:T(8,128)(2,1)}, bf16[512,512]{1,0:T(8,128)(2,1)}, u32[]{:S(2)}, u32[]{:S(2)}) collective-permute-start(bf16[512,512]{1,0:T(8,128)(2,1)} %collective-permute-done.3.rest_1_), channel_id=1, source_target_pairs={{8,16},{12,20},{16,8},{20,12},{9,17},{13,21},{17,9},{21,13},{10,18... | collective-permute-start | bytes 1572872 | tf_op jit(solution)/shard_map/ppermute | solution.py:300
  57.4 25.2 %collective-permute-start.9 = (bf16[512,512]{1,0:T(8,128)(2,1)S(1)}, bf16[512,512]{1,0:T(8,128)(2,1)}, u32[]{:S(2)}, u32[]{:S(2)}) collective-permute-start(bf16[512,512]{1,0:T(8,128)(2,1)S(1)} %collective-permute-done.4.rest_2_), channel_id=1, source_target_pairs={{8,0},{12,4},{16,24},{20,28},{9,1},{13,5},{17,25},{21,29},{10,2},{... | collective-permute-start | bytes 1572872 | tf_op jit(solution)/shard_map/ppermute | solution.py:300
  58.7 36.2 %collective-permute-start.11 = (bf16[512,512]{1,0:T(8,128)(2,1)}, bf16[512,512]{1,0:T(8,128)(2,1)}, u32[]{:S(2)}, u32[]{:S(2)}) collective-permute-start(bf16[512,512]{1,0:T(8,128)(2,1)} %collective-permute-done.10.rest_4_), channel_id=1, source_target_pairs={{8,0},{12,4},{16,24},{20,28},{9,1},{13,5},{17,25},{21,29},{10,2},{... | collective-permute-start | bytes 1572872 | tf_op jit(solution)/shard_map/ppermute | solution.py:300
  68.2 6.4 %collective-permute-start.8 = (bf16[256,512]{1,0:T(8,128)(2,1)S(1)}, bf16[256,512]{1,0:T(8,128)(2,1)S(1)}, u32[]{:S(2)}, u32[]{:S(2)}) collective-permute-start(bf16[256,512]{1,0:T(8,128)(2,1)S(1)} %get-tuple-element.43.mixed_ref.rest_2_.rest_5_), channel_id=1, source_target_pairs={{0,4},{4,0},{8,12},{12,8},{16,20},{20,16},{24,28},{28,24},{1,5},{5... | collective-permute-start | bytes 786440 | tf_op jit(solution)/shard_map/ppermute | solution.py:62
  81.2 17.1 %copy-start.26 = (bf16[512,512]{1,0:T(8,128)(2,1)}, bf16[512,512]{1,0:T(8,128)(2,1)S(1)}, u32[]{:S(2)}) copy-start(bf16[512,512]{1,0:T(8,128)(2,1)S(1)} %get-tuple-element.61) | copy-start | bytes 1572868
  99.1 18.5 %collective-permute-start.13 = (bf16[256,512]{1,0:T(8,128)(2,1)}, bf16[256,512]{1,0:T(8,128)(2,1)}, u32[]{:S(2)}, u32[]{:S(2)}) collective-permute-start(bf16[256,512]{1,0:T(8,128)(2,1)} %get-tuple-element.49), channel_id=1, source_target_pairs={{0,4},{4,0},{8,12},{12,8},{16,20},{20,16},{24,28},{28,24},{1,5},{5... | collective-permute-start | bytes 786440 | tf_op jit(solution)/shard_map/ppermute | solution.py:62
  104.9 29.3 %collective-permute-start.15 = (bf16[512,512]{1,0:T(8,128)(2,1)}, bf16[512,512]{1,0:T(8,128)(2,1)S(1)}, u32[]{:S(2)}, u32[]{:S(2)}) collective-permute-start(bf16[512,512]{1,0:T(8,128)(2,1)} %copy-done.26), channel_id=1, source_target_pairs={{0,8},{4,12},{8,16},{12,20},{16,24},{20,28},{24,0},{28,4},{1,9},{5... | collective-permute-start | bytes 1572872 | tf_op jit(solution)/shard_map/ppermute | solution.py:58
  117.6 21.5 %collective-permute-start.16 = (bf16[512,512]{1,0:T(8,128)(2,1)}, bf16[512,512]{1,0:T(8,128)(2,1)S(1)}, u32[]{:S(2)}, u32[]{:S(2)}) collective-permute-start(bf16[512,512]{1,0:T(8,128)(2,1)} %copy-done.25), channel_id=1, source_target_pairs={{0,24},{4,28},{8,0},{12,4},{16,8},{20,12},{24,16},{28,20},{1,25},{... | collective-permute-start | bytes 1572872 | tf_op jit(solution)/shard_map/ppermute | solution.py:58
  123.4 17.8 %copy-start.19 = (bf16[2,384,512]{2,1,0:T(8,128)(2,1)}, bf16[2,384,512]{2,1,0:T(8,128)(2,1)S(1)}, u32[]{:S(2)}) copy-start(bf16[2,384,512]{2,1,0:T(8,128)(2,1)S(1)} %first_grad.1) | copy-start | bytes 2359300
  123.4 17.8 %collective-permute-start.17 = (bf16[2,384,512]{2,1,0:T(8,128)(2,1)S(1)}, bf16[2,384,512]{2,1,0:T(8,128)(2,1)S(1)}, u32[]{:S(2)}, u32[]{:S(2)}) collective-permute-start(bf16[2,384,512]{2,1,0:T(8,128)(2,1)S(1)} %first_grad.1), channel_id=1, source_target_pairs={{0,4},{4,0},{8,12},{12,8},{16,20},{20,16},{24,28},{28,24},{1,5},{5... | collective-permute-start | bytes 2359304 | tf_op jit(solution)/shard_map/ppermute | solution.py:62
  141.2 49.4 %copy-start.6 = (f32[512,512]{1,0:T(8,128)S(1)}, f32[512,512]{1,0:T(8,128)}, u32[]{:S(2)}) copy-start(f32[512,512]{1,0:T(8,128)} %copy-done.5) | copy-start | bytes 3145732
  142.1 31.6 %collective-permute-start.18 = (bf16[2,256,512]{2,1,0:T(8,128)(2,1)S(1)}, bf16[2,256,512]{2,1,0:T(8,128)(2,1)S(1)}, u32[]{:S(2)}, u32[]{:S(2)}) collective-permute-start(bf16[2,256,512]{2,1,0:T(8,128)(2,1)S(1)} %get-tuple-element.67), channel_id=1, source_target_pairs={{8,0},{12,4},{16,8},{20,12},{24,16},{28,20},{9,1},{13,5},{17,9},{2... | collective-permute-start | bytes 1572872 | tf_op jit(solution)/shard_map/ppermute | solution.py:27
  143.4 30.4 %collective-permute-start.19 = (bf16[2,256,512]{2,1,0:T(8,128)(2,1)S(1)}, bf16[2,256,512]{2,1,0:T(8,128)(2,1)S(1)}, u32[]{:S(2)}, u32[]{:S(2)}) collective-permute-start(bf16[2,256,512]{2,1,0:T(8,128)(2,1)S(1)} %get-tuple-element.68), channel_id=1, source_target_pairs={{0,8},{4,12},{8,16},{12,20},{16,24},{20,28},{1,9},{5,13},{9,17},{1... | collective-permute-start | bytes 1572872 | tf_op jit(solution)/shard_map/ppermute | solution.py:27
  148.0 41.9 %collective-permute-start.22 = (bf16[512,512]{1,0:T(8,128)(2,1)S(1)}, bf16[512,512]{1,0:T(8,128)(2,1)S(1)}, u32[]{:S(2)}, u32[]{:S(2)}) collective-permute-start(bf16[512,512]{1,0:T(8,128)(2,1)S(1)} %copy-done.24), channel_id=1, source_target_pairs={{0,16},{4,20},{8,24},{12,28},{16,0},{20,4},{24,8},{28,12},{1,17},{... | collective-permute-start | bytes 1572872 | tf_op jit(solution)/shard_map/ppermute | solution.py:58
  150.7 23.0 %collective-permute-start.21 = (bf16[2,128,512]{2,1,0:T(8,128)(2,1)S(1)}, bf16[2,128,512]{2,1,0:T(8,128)(2,1)S(1)}, u32[]{:S(2)}, u32[]{:S(2)}) collective-permute-start(bf16[2,128,512]{2,1,0:T(8,128)(2,1)S(1)} %get-tuple-element.69), channel_id=1, source_target_pairs={{24,0},{25,1},{26,2},{27,3}} | collective-permute-start | bytes 786440 | tf_op jit(solution)/shard_map/ppermute | solution.py:447
  152.0 37.9 %collective-permute-start.20 = (bf16[2,128,512]{2,1,0:T(8,128)(2,1)S(1)}, bf16[2,128,512]{2,1,0:T(8,128)(2,1)S(1)}, u32[]{:S(2)}, u32[]{:S(2)}) collective-permute-start(bf16[2,128,512]{2,1,0:T(8,128)(2,1)S(1)} %get-tuple-element.69), channel_id=1, source_target_pairs={{16,0},{17,1},{18,2},{19,3}} | collective-permute-start | bytes 786440 | tf_op jit(solution)/shard_map/ppermute | solution.py:447
  173.7 26.6 %collective-permute-start.14 = (bf16[2,256,512]{2,1,0:T(8,128)(2,1)S(1)}, bf16[2,256,512]{2,1,0:T(8,128)(2,1)S(1)}, u32[]{:S(2)}, u32[]{:S(2)}) collective-permute-start(bf16[2,256,512]{2,1,0:T(8,128)(2,1)S(1)} %get-tuple-element.58), channel_id=1, source_target_pairs={{0,4},{4,0},{8,12},{12,8},{16,20},{20,16},{24,28},{28,24},{1,5},{5... | collective-permute-start | bytes 1572872 | tf_op jit(solution)/shard_map/ppermute | solution.py:62
  173.7 19.2 %copy-start.28 = (bf16[2,256,512]{2,1,0:T(8,128)(2,1)}, bf16[2,256,512]{2,1,0:T(8,128)(2,1)S(1)}, u32[]{:S(2)}) copy-start(bf16[2,256,512]{2,1,0:T(8,128)(2,1)S(1)} %collective-permute-done.18.b_ref) | copy-start | bytes 1572868
  173.7 19.2 %copy-start.29 = (bf16[2,256,512]{2,1,0:T(8,128)(2,1)}, bf16[2,256,512]{2,1,0:T(8,128)(2,1)S(1)}, u32[]{:S(2)}) copy-start(bf16[2,256,512]{2,1,0:T(8,128)(2,1)S(1)} %collective-permute-done.19.c_ref) | copy-start | bytes 1572868
  192.9 6.4 %collective-permute-start.12 = (bf16[256,512]{1,0:T(8,128)(2,1)S(1)}, bf16[256,512]{1,0:T(8,128)(2,1)S(1)}, u32[]{:S(2)}, u32[]{:S(2)}) collective-permute-start(bf16[256,512]{1,0:T(8,128)(2,1)S(1)} %get-tuple-element.80), channel_id=1, source_target_pairs={{0,4},{4,0},{8,12},{12,8},{16,20},{20,16},{24,28},{28,24},{1,5},{5... | collective-permute-start | bytes 786440 | tf_op jit(solution)/shard_map/ppermute | solution.py:62
  (27 other events, 151.1 us)
Sparse Core Ops, SparseCore 0:
  31.1 24.0 all-gather.1
  105.0 43.2 reduce-scatter.1

commit v2 on v1

--- a/solution.py
+++ b/solution.py
@@ -291,18 +291,19 @@
         sent = jnp.where(side == 0, after, before)
         hop = [(2 * z, 2 * z + 1) for z in range(length - 1)] + [(2 * z + 1, 2 * z) for z in range(1, length)]
         across = lax.ppermute(sent, "ctx", hop)
-        known = jnp.where(run == 2, before[:, :BLK], head_rows)
-        known = jnp.where((run == 3) | (run == 4), lax.ppermute(known, "ctx", [(2, 4), (0, 3)]), known)
-        known = jnp.where(run == 1, beside[:2, :BLK], known)
-        first = jnp.where(run > length, lax.ppermute(known, "ctx", [(4, 6), (3, 5), (2, 7)]), known)
+        known = jnp.where(run == 1, beside[:2, :BLK], head_rows)
+        known = jnp.where(run == 2, before[:, :BLK], known)
+        middle_rows = lax.ppermute(head_rows, "ctx", [(0, length)])
+        known = jnp.where(run == length, middle_rows, known)
+        late = lax.ppermute(known, "ctx", [(1, 7), (0, 3), (4, 5), (2, 6)])
+        first = jnp.where((run == 3) | (run > length), late, known)
 
         def between(x, places):
             return lax.ppermute(x, "ctx", [(2 * a + n, 2 * b + n) for a, b in places for n in range(2)])
 
-        base = tied(out_weight, before, after)
+        base = tied(out_weight, before, after, middle_rows)
         near = between(base, ((0, 1), (1, 0), (2, 3), (3, 2)))
         middle = between(base, ((1, 2), (2, 1)))
-        near, middle, across, first = lax.optimization_barrier((near, middle, across, first))
         far = between(near, ((1, 2), (2, 1)))
         outer = between(middle, ((1, 0), (2, 3)))
         farthest = between(far, ((1, 0), (2, 3)))
@@ -348,18 +349,6 @@
 
     if direct:
         held = [pltpu.VMEM((length, width, features), jnp.bfloat16), pltpu.SemaphoreType.DMA((length,))]
-        mixed_other = swapped(mixed, range(length))
-        own_part, *weight_parts = pl.pallas_call(
-            functools.partial(weight_kernel, length),
-            in_specs=[whole] + [whole] * 2,
-            out_specs=[whole] * length,
-            out_shape=[jax.ShapeDtypeStruct((width, features), jnp.float32)]
-            + [jax.ShapeDtypeStruct((width, features), jnp.bfloat16)] * (length - 1),
-            scratch_shapes=[pltpu.VMEM((2 * tokens, features), jnp.bfloat16)],
-            compiler_params=pltpu.CompilerParams(vmem_limit_bytes=32 * 1024 * 1024),
-            cost_estimate=CHEAP,
-            name="weight_part",
-        )(grad_side, mixed, mixed_other)
         own_grad, other_grad = pl.pallas_call(
             functools.partial(grads_kernel, length),
             in_specs=[whole] + [anywhere] * 6,
@@ -372,8 +361,20 @@
             compiler_params=pltpu.CompilerParams(vmem_limit_bytes=32 * 1024 * 1024),
             cost_estimate=CHEAP,
             name="project_grad",
-        )(tied(grad_side, own_part), *weight_pieces)
+        )(grad_side, *weight_pieces)
         mixed_grad = (own_grad + swapped(other_grad, range(length)).astype(jnp.float32)).astype(jnp.bfloat16)
+        mixed_other = tied(swapped(mixed, range(length)), other_grad)
+        own_part, *weight_parts = pl.pallas_call(
+            functools.partial(weight_kernel, length),
+            in_specs=[whole] + [whole] * 2,
+            out_specs=[whole] * length,
+            out_shape=[jax.ShapeDtypeStruct((width, features), jnp.float32)]
+            + [jax.ShapeDtypeStruct((width, features), jnp.bfloat16)] * (length - 1),
+            scratch_shapes=[pltpu.VMEM((2 * tokens, features), jnp.bfloat16)],
+            compiler_params=pltpu.CompilerParams(vmem_limit_bytes=32 * 1024 * 1024),
+            cost_estimate=CHEAP,
+            name="weight_part",
+        )(grad_side, mixed, mixed_other)
         partial_out = pl.pallas_call(
             functools.partial(outs_kernel, length),
             in_specs=[whole] * 2 + [anywhere] * 6,
@@ -383,13 +384,9 @@
             compiler_params=pltpu.CompilerParams(vmem_limit_bytes=32 * 1024 * 1024),
             cost_estimate=CHEAP,
             name="project_out",
-        )(mixed, tied(mixed_other, other_grad), *weight_pieces)
+        )(mixed, tied(mixed_other, own_part), *weight_pieces)
         scattered = lax.psum_scatter(partial_out, "head", scatter_dimension=1, tiled=True)
-        mine, theirs = scattered[:tokens], swapped(scattered[tokens:], range(length))
-        attended = jnp.where(
-            side == 0, jnp.concatenate([mine, theirs], axis=1), jnp.concatenate([theirs, mine], axis=1)
-        )
-        mixed_grad = tied(mixed_grad, partial_out)
+        mixed_grad = tied(mixed_grad, own_part)
         weight_turns = [turned(weight_parts[n - 1], n, length) for n in (1, 3)]
     else:
         partial_out = mm(mixed, full_weight, NT).astype(jnp.bfloat16)
@@ -410,7 +407,7 @@
         name="first_grad",
     )(run_word, block_lists, queries, *early_bands, first, mixed, mixed_grad, lse)
 
-    lse_later = tied(lse, early_grads)
+    lse_later = tied(lse, early_grads, partial_out)
     results = pl.pallas_call(
         functools.partial(bwd_kernel, offsets, early, per_dev, scale),
         grid=(groups,),
@@ -443,12 +440,17 @@
         )
         back_down = shifted(to_before, -2)
         back_up = shifted(to_after, 2)
-        for c in range(length, ctx, 2):
-            got = tied(lax.ppermute(near, "ctx", [(c, 0)]), back_down, back_up)
-            first_sum = first_sum + got.astype(jnp.float32)
+        scattered = tied(scattered, back_pair)
+        mine, theirs = scattered[:tokens], swapped(scattered[tokens:], range(length))
+        attended = jnp.where(
+            side == 0, jnp.concatenate([mine, theirs], axis=1), jnp.concatenate([theirs, mine], axis=1)
+        )
         weight_grad = own_part
         for part in weight_turns + [turned(last_part, 2, length)]:
             weight_grad = weight_grad + part.astype(jnp.float32)
+        for c in range(length, ctx, 2):
+            got = tied(lax.ppermute(near, "ctx", [(c, 0)]), back_down, back_up, attended)
+            first_sum = first_sum + got.astype(jnp.float32)
         wide = pl.BlockSpec((2, BLK, features), lambda n: (0, n, 0))
         top = pl.BlockSpec((2, BLK, features), lambda n: (0, 0, 0))
         slab = pl.BlockSpec((BLK, features), lambda n: (n, 0))
@@ -460,7 +462,7 @@
             out_shape=[jax.ShapeDtypeStruct((tokens, features), jnp.bfloat16)] * 2,
             cost_estimate=CHEAP,
             name="finish",
-        )(run_word, tied(own, theirs), back_pair, back_down, back_up, first_sum)
+        )(run_word, own, back_pair, back_down, back_up, first_sum)
 
     else:
         first_sum = to_first(early_grads.astype(jnp.float32))

time: 212 us -> 187 us (0.88)
  the two profiles are of different devices: /device:TPU:0 before, /device:TPU:12 now
where the time goes in v2:
time: 187 us; the launch traced here: 186 us
  waiting for transfers between devices  59.6 us (32%)
  starting transfers between devices  56.7 us (30%)
  Pallas kernels  33.6 us (18%)
  between operations  14.5 us (8%)
  other arithmetic  10.9 us (6%)
  local copies, waits for them, and re-layouts  10.5 us (6%)
    ppermute x5, starting transfers between devices, between(): lax.ppermute(x, 'ctx', [(2 * a + n, 2 * b + n) for a, b in places for n i...  21.7 us
    ppermute x6, waiting for transfers between devices, swapped(): lax.ppermute(piece, 'ctx', [(2 * z + n, 2 * z + 1 - n) for z in places fo...  19.9 us
    ppermute x4, starting transfers between devices, shifted(): lax.ppermute(x, 'ctx', [(i, i + by) for i in range(peers) if 0 <= i + by...  13.3 us
    ppermute x4, waiting for transfers between devices, shifted(): lax.ppermute(x, 'ctx', [(i, i + by) for i in range(peers) if 0 <= i + by...  12.8 us
    ppermute x3, waiting for transfers between devices, turned(): lax.ppermute(x, 'ctx', [(2 * z + n, 2 * ((z + by) % length) + n) for z in...  11.9 us
    ppermute x5, waiting for transfers between devices, between(): lax.ppermute(x, 'ctx', [(2 * a + n, 2 * b + n) for a, b in places for n i...  11.8 us
    pallas_call x1, Pallas kernels, local(): pl.pallas_call(functools.partial(bwd_kernel, offsets, early, per_dev, sca...  9.04 us
    ppermute x3, starting transfers between devices, turned(): lax.ppermute(x, 'ctx', [(2 * z + n, 2 * ((z + by) % length) + n) for z in...  8.72 us
  transfers between devices with their start and end apart: 25, of which 10 were waited for; matrix products, arithmetic and copies ran while one was open for 4% of the time, Pallas kernels for 17%

profile of v2, /device:TPU:12, one launch (start us, length us, event | category | flops | bytes accessed | tf_op | source)
XLA Modules:
  0.0 185.8 jit_solution(13560839258201702453)
XLA Ops:
  11.1 2.4 %collective-permute-start.1 = (bf16[2,256,512]{2,1,0:T(8,128)(2,1)S(1)}, bf16[2,256,512]{2,1,0:T(8,128)(2,1)S(1)}, u32[]{:S(2)}, u32[]{:S(2)}) collective-permute-start(bf16[2,256,512]{2,1,0:T(8,128)(2,1)S(1)} %pad_maximum_fusion.1), channel_id=1, source_target_pairs={{8,0},{12,4},{16,8},{20,12},{24,16},{28,20},{9,1},{13,5},{17,9},{2... | collective-permute-start | bytes 1572872 | tf_op jit(solution)/shard_map/ppermute | solution.py:27
  13.5 3.5 %collective-permute-start = (bf16[2,256,512]{2,1,0:T(8,128)(2,1)S(1)}, bf16[2,256,512]{2,1,0:T(8,128)(2,1)S(1)}, u32[]{:S(2)}, u32[]{:S(2)}) collective-permute-start(bf16[2,256,512]{2,1,0:T(8,128)(2,1)S(1)} %pad_maximum_fusion.1), channel_id=1, source_target_pairs={{0,8},{4,12},{8,16},{12,20},{16,24},{20,28},{1,9},{5,13},{9,17},{1... | collective-permute-start | bytes 1572872 | tf_op jit(solution)/shard_map/ppermute | solution.py:27
  17.0 11.9 %collective-permute-done.2.rest_2_ = bf16[3,256,512]{2,1,0:T(8,128)(2,1)S(1)} collective-permute-done((bf16[3,256,512]{2,1,0:T(8,128)(2,1)S(1)}, bf16[3,256,512]{2,1,0:T(8,128)(2,1)S(1)}, u32[]{:S(2)}, u32[]{:S(2)}) %collective-permute-start.2) | collective-permute-done | bytes 786464 | tf_op jit(solution)/shard_map/ppermute | solution.py:62
  30.7 10.4 %collective-permute-start.7 = (bf16[512,512]{1,0:T(8,128)(2,1)S(1)}, bf16[512,512]{1,0:T(8,128)(2,1)}, u32[]{:S(2)}, u32[]{:S(2)}) collective-permute-start(bf16[512,512]{1,0:T(8,128)(2,1)S(1)} %copy-done.8), channel_id=1, source_target_pairs={{0,8},{4,12},{8,0},{12,4},{16,24},{20,28},{24,16},{28,20},{1,9},{5... | collective-permute-start | bytes 1572872 | tf_op jit(solution)/shard_map/ppermute | solution.py:302
  41.1 3.8 %collective-permute-start.8 = (bf16[512,512]{1,0:T(8,128)(2,1)S(1)}, bf16[512,512]{1,0:T(8,128)(2,1)}, u32[]{:S(2)}, u32[]{:S(2)}) collective-permute-start(bf16[512,512]{1,0:T(8,128)(2,1)S(1)} %copy-done.8), channel_id=1, source_target_pairs={{8,16},{12,20},{16,8},{20,12},{9,17},{13,21},{17,9},{21,13},{10,18... | collective-permute-start | bytes 1572872 | tf_op jit(solution)/shard_map/ppermute | solution.py:302
  44.9 6.5 %collective-permute-done.7.rest_1_ = bf16[512,512]{1,0:T(8,128)(2,1)} collective-permute-done((bf16[512,512]{1,0:T(8,128)(2,1)S(1)}, bf16[512,512]{1,0:T(8,128)(2,1)}, u32[]{:S(2)}, u32[]{:S(2)}) %collective-permute-start.7) | collective-permute-done | bytes 524320 | tf_op jit(solution)/shard_map/ppermute | solution.py:302
  51.4 4.0 %collective-permute-start.10 = (bf16[512,512]{1,0:T(8,128)(2,1)}, bf16[512,512]{1,0:T(8,128)(2,1)}, u32[]{:S(2)}, u32[]{:S(2)}) collective-permute-start(bf16[512,512]{1,0:T(8,128)(2,1)} %collective-permute-done.7.rest_1_), channel_id=1, source_target_pairs={{8,16},{12,20},{16,8},{20,12},{9,17},{13,21},{17,9},{21,13},{10,18... | collective-permute-start | bytes 1572872 | tf_op jit(solution)/shard_map/ppermute | solution.py:302
  56.3 1.9 %collective-permute-start.3 = (bf16[2,256,512]{2,1,0:T(8,128)(2,1)}, bf16[2,256,512]{2,1,0:T(8,128)(2,1)}, u32[]{:S(2)}, u32[]{:S(2)}) collective-permute-start(bf16[2,256,512]{2,1,0:T(8,128)(2,1)} %broadcast_select_fusion), channel_id=1, source_target_pairs={{0,4},{8,12},{16,20},{12,8},{20,16},{28,24},{1,5},{9,13},{17,21},{... | collective-permute-start | bytes 1572872 | tf_op jit(solution)/shard_map/ppermute | solution.py:293
  59.5 5.4 %collective-permute-done.10.rest_4_ = bf16[512,512]{1,0:T(8,128)(2,1)} collective-permute-done((bf16[512,512]{1,0:T(8,128)(2,1)}, bf16[512,512]{1,0:T(8,128)(2,1)}, u32[]{:S(2)}, u32[]{:S(2)}) %collective-permute-start.10) | collective-permute-done | bytes 524320 | tf_op jit(solution)/shard_map/ppermute | solution.py:302
  64.9 2.1 %collective-permute-start.11 = (bf16[512,512]{1,0:T(8,128)(2,1)}, bf16[512,512]{1,0:T(8,128)(2,1)}, u32[]{:S(2)}, u32[]{:S(2)}) collective-permute-start(bf16[512,512]{1,0:T(8,128)(2,1)} %collective-permute-done.10.rest_4_), channel_id=1, source_target_pairs={{8,0},{12,4},{16,24},{20,28},{9,1},{13,5},{17,25},{21,29},{10,2},{... | collective-permute-start | bytes 1572872 | tf_op jit(solution)/shard_map/ppermute | solution.py:302
  67.1 2.0 %collective-permute-start.5 = (bf16[2,128,512]{2,1,0:T(8,128)(2,1)S(1)}, bf16[2,128,512]{2,1,0:T(8,128)(2,1)}, u32[]{:S(2)}, u32[]{:S(2)}) collective-permute-start(bf16[2,128,512]{2,1,0:T(8,128)(2,1)S(1)} %fusion.9), channel_id=1, source_target_pairs={{4,28},{0,12},{16,20},{8,24},{5,29},{1,13},{17,21},{9,25},{6,30},{... | collective-permute-start | bytes 786440 | tf_op jit(solution)/shard_map/ppermute | solution.py:298
  69.2 3.1 %collective-permute-done.5 = bf16[2,128,512]{2,1,0:T(8,128)(2,1)} collective-permute-done((bf16[2,128,512]{2,1,0:T(8,128)(2,1)S(1)}, bf16[2,128,512]{2,1,0:T(8,128)(2,1)}, u32[]{:S(2)}, u32[]{:S(2)}) %collective-permute-start.5) | collective-permute-done | bytes 262176 | tf_op jit(solution)/shard_map/ppermute | solution.py:298
  73.4 6.2 %attend.1 = (bf16[256,512]{1,0:T(8,128)(2,1)S(1)}, f32[4,1,256]{2,1,0:T(1,128)S(1)}) custom-call(s32[1]{0:T(128)} %bitcast.run_ref, s32[16,3]{1,0:T(8,128)S(1)} %copy.11.lists_ref, bf16[256,512]{1,0:T(8,128)(2,1)S(1)} %copy-done.22, bf16[256,512]{1,0:T(8,128)(2,1)S(1)} %copy-done.3, bf16[256,512]{1,0:T(8,128)(2,1)S(1)} %copy-done.2, ...), custom_call_target="tpu_custom_call" | custom-call | flops 1 | bytes 1 | tf_op jit(solution)/shard_map/attend/pallas_call | solution.py:335
  79.6 1.8 collective-permute-start.6
  85.9 3.5 %project_grad.1 = (f32[256,512]{1,0:T(8,128)S(1)}, bf16[256,512]{1,0:T(8,128)(2,1)}) custom-call(bf16[512,2048]{1,0:T(8,128)(2,1)S(1)} %copy-done, bf16[512,512]{1,0:T(8,128)(2,1)S(1)} %copy-done.9, bf16[512,512]{1,0:T(8,128)(2,1)} %collective-permute-done.7.rest_1_, bf16[512,512]{1,0:T(8,128)(2,1)} %collective-permute-done.8.rest_2_, ...), custom_call_target="tpu_custom_call" | custom-call | flops 1 | bytes 1 | tf_op jit(solution)/shard_map/project_grad/pallas_call | solution.py:352
  90.5 3.2 %weight_part.1 = (f32[512,512]{1,0:T(8,128)S(1)}, bf16[512,512]{1,0:T(8,128)(2,1)}, bf16[512,512]{1,0:T(8,128)(2,1)S(1)}, bf16[512,512]{1,0:T(8,128)(2,1)}) custom-call(bf16[512,2048]{1,0:T(8,128)(2,1)S(1)} %copy-done.1, bf16[256,512]{1,0:T(8,128)(2,1)S(1)} %get-tuple-element.36.mixed_ref.rest_2_.rest_5_, bf16[256,512]{1,0:T(8,128)(2,1)} %collective-permute-done.6.other_ref), custom_call_target="tpu_custom_call" | custom-call | flops 1 | bytes 1 | tf_op jit(solution)/shard_map/weight_part/pallas_call | solution.py:367
  95.4 5.3 %project_out.1 = bf16[512,2048]{1,0:T(8,128)(2,1)} custom-call(bf16[256,512]{1,0:T(8,128)(2,1)S(1)} %get-tuple-element.36.mixed_ref.rest_2_.rest_5_, bf16[256,512]{1,0:T(8,128)(2,1)} %collective-permute-done.6.other_ref, bf16[512,512]{1,0:T(8,128)(2,1)S(1)} %copy-done.10, bf16[512,512]{1,0:T(8,128)(2,1)} %collective-permute-done.7.rest_1_, ...), custom_call_target="tpu_custom_call" | custom-call | flops 1 | bytes 1 | tf_op jit(solution)/shard_map/project_out/pallas_call | solution.py:378
  100.8 5.3 %collective-permute-start.15 = (bf16[512,512]{1,0:T(8,128)(2,1)}, bf16[512,512]{1,0:T(8,128)(2,1)S(1)}, u32[]{:S(2)}, u32[]{:S(2)}) collective-permute-start(bf16[512,512]{1,0:T(8,128)(2,1)} %get-tuple-element.53), channel_id=1, source_target_pairs={{0,8},{4,12},{8,16},{12,20},{16,24},{20,28},{24,0},{28,4},{1,9},{5... | collective-permute-start | bytes 1572872 | tf_op jit(solution)/shard_map/ppermute | solution.py:58
  107.1 3.8 %first_grad.1 = bf16[2,384,512]{2,1,0:T(8,128)(2,1)S(1)} custom-call(s32[1]{0:T(128)} %bitcast.run_ref, s32[16,3]{1,0:T(8,128)S(1)} %copy.11.lists_ref, bf16[256,512]{1,0:T(8,128)(2,1)S(1)} %copy-done.23, bf16[2,256,512]{2,1,0:T(8,128)(2,1)} %collective-permute-done.3.rest_3_.rest_0_, bf16[2,128,512]{2,1,0:T(8,128)(2,1)S(1)} %copy-done.18, ...), custom_call_target="tpu_custom_call" | custom-call | flops 10000000000 | bytes 1 | tf_op jit(solution)/shard_map/first_grad/pallas_call | solution.py:398
  111.6 9.0 %attend_grad.1 = (bf16[256,512]{1,0:T(8,128)(2,1)}, f32[2,256,512]{2,1,0:T(8,128)S(1)}, bf16[2,256,512]{2,1,0:T(8,128)(2,1)S(1)}, bf16[2,256,512]{2,1,0:T(8,128)(2,1)S(1)}, bf16[2,256,512]{2,1,0:T(8,128)(2,1)S(1)}) custom-call(s32[1]{0:T(128)} %bitcast.run_ref, s32[16,3]{1,0:T(8,128)S(1)} %copy.11.lists_ref, bf16[256,512]{1,0:T(8,128)(2,1)S(1)} %copy-done.23, ...), custom_call_target="tpu_custom_call" | custom-call | flops 30000001024 | bytes 1 | tf_op jit(solution)/shard_map/attend_grad/pallas_call | solution.py:411
  122.1 2.5 %collective-permute-done.15 = bf16[512,512]{1,0:T(8,128)(2,1)S(1)} collective-permute-done((bf16[512,512]{1,0:T(8,128)(2,1)}, bf16[512,512]{1,0:T(8,128)(2,1)S(1)}, u32[]{:S(2)}, u32[]{:S(2)}) %collective-permute-start.15) | collective-permute-done | bytes 524320 | tf_op jit(solution)/shard_map/ppermute | solution.py:58
  124.6 2.2 %collective-permute-done.16 = bf16[512,512]{1,0:T(8,128)(2,1)S(1)} collective-permute-done((bf16[512,512]{1,0:T(8,128)(2,1)}, bf16[512,512]{1,0:T(8,128)(2,1)S(1)}, u32[]{:S(2)}, u32[]{:S(2)}) %collective-permute-start.16) | collective-permute-done | bytes 524320 | tf_op jit(solution)/shard_map/ppermute | solution.py:58
  126.9 4.6 %collective-permute-done.17 = bf16[2,384,512]{2,1,0:T(8,128)(2,1)S(1)} collective-permute-done((bf16[2,384,512]{2,1,0:T(8,128)(2,1)S(1)}, bf16[2,384,512]{2,1,0:T(8,128)(2,1)S(1)}, u32[]{:S(2)}, u32[]{:S(2)}) %collective-permute-start.17) | collective-permute-done | bytes 786464 | tf_op jit(solution)/shard_map/ppermute | solution.py:62
  132.9 3.4 %collective-permute-start.22 = (bf16[512,512]{1,0:T(8,128)(2,1)S(1)}, bf16[512,512]{1,0:T(8,128)(2,1)S(1)}, u32[]{:S(2)}, u32[]{:S(2)}) collective-permute-start(bf16[512,512]{1,0:T(8,128)(2,1)S(1)} %copy-done.25), channel_id=1, source_target_pairs={{0,16},{4,20},{8,24},{12,28},{16,0},{20,4},{24,8},{28,12},{1,17},{... | collective-permute-start | bytes 1572872 | tf_op jit(solution)/shard_map/ppermute | solution.py:58
  138.4 2.7 %collective-permute-start.18 = (bf16[2,256,512]{2,1,0:T(8,128)(2,1)}, bf16[2,256,512]{2,1,0:T(8,128)(2,1)}, u32[]{:S(2)}, u32[]{:S(2)}) collective-permute-start(bf16[2,256,512]{2,1,0:T(8,128)(2,1)} %get-tuple-element.59), channel_id=1, source_target_pairs={{8,0},{12,4},{16,8},{20,12},{24,16},{28,20},{9,1},{13,5},{17,9},{2... | collective-permute-start | bytes 1572872 | tf_op jit(solution)/shard_map/ppermute | solution.py:27
  141.2 4.7 %collective-permute-start.19 = (bf16[2,256,512]{2,1,0:T(8,128)(2,1)}, bf16[2,256,512]{2,1,0:T(8,128)(2,1)}, u32[]{:S(2)}, u32[]{:S(2)}) collective-permute-start(bf16[2,256,512]{2,1,0:T(8,128)(2,1)} %get-tuple-element.60), channel_id=1, source_target_pairs={{0,8},{4,12},{8,16},{12,20},{16,24},{20,28},{1,9},{5,13},{9,17},{1... | collective-permute-start | bytes 1572872 | tf_op jit(solution)/shard_map/ppermute | solution.py:27
  147.0 7.2 %collective-permute-done.22 = bf16[512,512]{1,0:T(8,128)(2,1)S(1)} collective-permute-done((bf16[512,512]{1,0:T(8,128)(2,1)S(1)}, bf16[512,512]{1,0:T(8,128)(2,1)S(1)}, u32[]{:S(2)}, u32[]{:S(2)}) %collective-permute-start.22) | collective-permute-done | bytes 524320 | tf_op jit(solution)/shard_map/ppermute | solution.py:58
  154.8 2.4 %convert_add_fusion = f32[512,512]{1,0:T(8,128)} fusion(bf16[512,512]{1,0:T(8,128)(2,1)S(1)} %collective-permute-done.22, bf16[512,512]{1,0:T(8,128)(2,1)} %copy-done.28, f32[512,512]{1,0:T(8,128)S(1)} %copy-done.15, bf16[512,512]{1,0:T(8,128)(2,1)} %copy-done.27), kind=kLoop, calls=%fused_computation.7 | loop fusion | flops 1572864 | bytes 3670016 | tf_op jit(solution)/shard_map/add | solution.py:450
  157.2 3.4 %collective-permute-done.14 = bf16[256,512]{1,0:T(8,128)(2,1)S(1)} collective-permute-done((bf16[256,512]{1,0:T(8,128)(2,1)S(1)}, bf16[256,512]{1,0:T(8,128)(2,1)S(1)}, u32[]{:S(2)}, u32[]{:S(2)}) %collective-permute-start.14) | collective-permute-done | bytes 262176 | tf_op jit(solution)/shard_map/ppermute | solution.py:62
  161.5 12.8 %collective-permute-done.18.b_ref = bf16[2,256,512]{2,1,0:T(8,128)(2,1)} collective-permute-done((bf16[2,256,512]{2,1,0:T(8,128)(2,1)}, bf16[2,256,512]{2,1,0:T(8,128)(2,1)}, u32[]{:S(2)}, u32[]{:S(2)}) %collective-permute-start.18) | collective-permute-done | bytes 524320 | tf_op jit(solution)/shard_map/ppermute | solution.py:27
  174.3 2.0 %convert_add_fusion.1.first_ref = f32[2,128,512]{2,1,0:T(8,128)} fusion(bf16[2,128,512]{2,1,0:T(8,128)(2,1)S(1)} %collective-permute-done.21, bf16[2,128,512]{2,1,0:T(8,128)(2,1)} %collective-permute-done.20, bf16[2,384,512]{2,1,0:T(8,128)(2,1)} %copy-done.21, bf16[2,384,512]{2,1,0:T(8,128)(2,1)} %copy-done.26), kind=kLoop, calls=%fused_computation.14 | loop fusion | flops 917504 | bytes 1572864 | tf_op jit(solution)/shard_map/add | solution.py:453
  176.3 2.6 %finish.1 = (bf16[256,512]{1,0:T(8,128)(2,1)}, bf16[256,512]{1,0:T(8,128)(2,1)}) custom-call(s32[1]{0:T(128)} %bitcast.run_ref, f32[2,256,512]{2,1,0:T(8,128)} %copy-done.16, bf16[2,256,512]{2,1,0:T(8,128)(2,1)} %copy-done.29, bf16[2,256,512]{2,1,0:T(8,128)(2,1)} %collective-permute-done.18.b_ref, bf16[2,256,512]{2,1,0:T(8,128)(2,1)} %collective-permute-done.19.c_ref, ...), custom_call_target="tpu_custom_call" | custom-call | flops 1 | bytes 1 | tf_op jit(solution)/shard_map/finish/pallas_call | solution.py:457
  (106 shorter events, 25.6 us)
Async XLA Ops:
  7.2 75.1 %all-gather.2.cloned.1.call-start = ((), (), s32[]{:S(2)}) async-start(), calls=%async_computation.1 | async-start | bytes 2621440 | tf_op jit(solution)/shard_map/all_gather | solution.py:290
  9.5 21.2 %copy-start.8 = (bf16[512,512]{1,0:T(8,128)(2,1)S(1)}, bf16[512,512]{1,0:T(8,128)(2,1)}, u32[]{:S(2)}) copy-start(bf16[512,512]{1,0:T(8,128)(2,1)} %rest_0_.1) | copy-start | bytes 1572868
  9.5 19.3 %collective-permute-start.2 = (bf16[3,256,512]{2,1,0:T(8,128)(2,1)S(1)}, bf16[3,256,512]{2,1,0:T(8,128)(2,1)S(1)}, u32[]{:S(2)}, u32[]{:S(2)}) collective-permute-start(bf16[3,256,512]{2,1,0:T(8,128)(2,1)S(1)} %pad_maximum_fusion), channel_id=1, source_target_pairs={{0,4},{4,0},{8,12},{12,8},{16,20},{20,16},{24,28},{28,24},{1,5},{5... | collective-permute-start | bytes 2359304 | tf_op jit(solution)/shard_map/ppermute | solution.py:62
  11.1 17.8 %collective-permute-start.1 = (bf16[2,256,512]{2,1,0:T(8,128)(2,1)S(1)}, bf16[2,256,512]{2,1,0:T(8,128)(2,1)S(1)}, u32[]{:S(2)}, u32[]{:S(2)}) collective-permute-start(bf16[2,256,512]{2,1,0:T(8,128)(2,1)S(1)} %pad_maximum_fusion.1), channel_id=1, source_target_pairs={{8,0},{12,4},{16,8},{20,12},{24,16},{28,20},{9,1},{13,5},{17,9},{2... | collective-permute-start | bytes 1572872 | tf_op jit(solution)/shard_map/ppermute | solution.py:27
  13.5 15.4 %collective-permute-start = (bf16[2,256,512]{2,1,0:T(8,128)(2,1)S(1)}, bf16[2,256,512]{2,1,0:T(8,128)(2,1)S(1)}, u32[]{:S(2)}, u32[]{:S(2)}) collective-permute-start(bf16[2,256,512]{2,1,0:T(8,128)(2,1)S(1)} %pad_maximum_fusion.1), channel_id=1, source_target_pairs={{0,8},{4,12},{8,16},{12,20},{16,24},{20,28},{1,9},{5,13},{9,17},{1... | collective-permute-start | bytes 1572872 | tf_op jit(solution)/shard_map/ppermute | solution.py:27
  28.9 43.5 %copy-start.4 = (bf16[3,256,512]{2,1,0:T(8,128)(2,1)}, bf16[3,256,512]{2,1,0:T(8,128)(2,1)S(1)}, u32[]{:S(2)}) copy-start(bf16[3,256,512]{2,1,0:T(8,128)(2,1)S(1)} %collective-permute-done.2.rest_2_) | copy-start | bytes 2359300
  28.9 43.5 %copy-start.6 = (bf16[2,256,512]{2,1,0:T(8,128)(2,1)}, bf16[2,256,512]{2,1,0:T(8,128)(2,1)S(1)}, u32[]{:S(2)}) copy-start(bf16[2,256,512]{2,1,0:T(8,128)(2,1)S(1)} %collective-permute-done.1.rest_1_) | copy-start | bytes 1572868
  29.9 39.2 %copy-start.30 = (s32[16,3]{0,1:T(4,128)S(1)}, s32[16,3]{0,1:T(4,128)}, u32[]{:S(2)}) copy-start(s32[16,3]{0,1:T(4,128)} %param.10) | copy-start | bytes 580
  29.9 116.0 %reduce-scatter.2.cloned.1.call-start = ((), (), s32[]{:S(2)}) async-start(), calls=%async_computation.2 | async-start | bytes 2621440 | tf_op jit(solution)/shard_map/reduce_scatter | solution.py:388
  30.0 0.7 collective-permute-start.4
  30.7 20.7 %collective-permute-start.7 = (bf16[512,512]{1,0:T(8,128)(2,1)S(1)}, bf16[512,512]{1,0:T(8,128)(2,1)}, u32[]{:S(2)}, u32[]{:S(2)}) collective-permute-start(bf16[512,512]{1,0:T(8,128)(2,1)S(1)} %copy-done.8), channel_id=1, source_target_pairs={{0,8},{4,12},{8,0},{12,4},{16,24},{20,28},{24,16},{28,20},{1,9},{5... | collective-permute-start | bytes 1572872 | tf_op jit(solution)/shard_map/ppermute | solution.py:302
  41.1 17.1 %collective-permute-start.8 = (bf16[512,512]{1,0:T(8,128)(2,1)S(1)}, bf16[512,512]{1,0:T(8,128)(2,1)}, u32[]{:S(2)}, u32[]{:S(2)}) collective-permute-start(bf16[512,512]{1,0:T(8,128)(2,1)S(1)} %copy-done.8), channel_id=1, source_target_pairs={{8,16},{12,20},{16,8},{20,12},{9,17},{13,21},{17,9},{21,13},{10,18... | collective-permute-start | bytes 1572872 | tf_op jit(solution)/shard_map/ppermute | solution.py:302
  51.4 13.5 %collective-permute-start.10 = (bf16[512,512]{1,0:T(8,128)(2,1)}, bf16[512,512]{1,0:T(8,128)(2,1)}, u32[]{:S(2)}, u32[]{:S(2)}) collective-permute-start(bf16[512,512]{1,0:T(8,128)(2,1)} %collective-permute-done.7.rest_1_), channel_id=1, source_target_pairs={{8,16},{12,20},{16,8},{20,12},{9,17},{13,21},{17,9},{21,13},{10,18... | collective-permute-start | bytes 1572872 | tf_op jit(solution)/shard_map/ppermute | solution.py:302
  56.3 16.1 %collective-permute-start.3 = (bf16[2,256,512]{2,1,0:T(8,128)(2,1)}, bf16[2,256,512]{2,1,0:T(8,128)(2,1)}, u32[]{:S(2)}, u32[]{:S(2)}) collective-permute-start(bf16[2,256,512]{2,1,0:T(8,128)(2,1)} %broadcast_select_fusion), channel_id=1, source_target_pairs={{0,4},{8,12},{16,20},{12,8},{20,16},{28,24},{1,5},{9,13},{17,21},{... | collective-permute-start | bytes 1572872 | tf_op jit(solution)/shard_map/ppermute | solution.py:293
  58.2 23.2 %collective-permute-start.9 = (bf16[512,512]{1,0:T(8,128)(2,1)}, bf16[512,512]{1,0:T(8,128)(2,1)S(1)}, u32[]{:S(2)}, u32[]{:S(2)}) collective-permute-start(bf16[512,512]{1,0:T(8,128)(2,1)} %collective-permute-done.8.rest_2_), channel_id=1, source_target_pairs={{8,0},{12,4},{16,24},{20,28},{9,1},{13,5},{17,25},{21,29},{10,2},{... | collective-permute-start | bytes 1572872 | tf_op jit(solution)/shard_map/ppermute | solution.py:302
  64.9 17.3 %collective-permute-start.11 = (bf16[512,512]{1,0:T(8,128)(2,1)}, bf16[512,512]{1,0:T(8,128)(2,1)}, u32[]{:S(2)}, u32[]{:S(2)}) collective-permute-start(bf16[512,512]{1,0:T(8,128)(2,1)} %collective-permute-done.10.rest_4_), channel_id=1, source_target_pairs={{8,0},{12,4},{16,24},{20,28},{9,1},{13,5},{17,25},{21,29},{10,2},{... | collective-permute-start | bytes 1572872 | tf_op jit(solution)/shard_map/ppermute | solution.py:302
  67.1 5.2 %collective-permute-start.5 = (bf16[2,128,512]{2,1,0:T(8,128)(2,1)S(1)}, bf16[2,128,512]{2,1,0:T(8,128)(2,1)}, u32[]{:S(2)}, u32[]{:S(2)}) collective-permute-start(bf16[2,128,512]{2,1,0:T(8,128)(2,1)S(1)} %fusion.9), channel_id=1, source_target_pairs={{4,28},{0,12},{16,20},{8,24},{5,29},{1,13},{17,21},{9,25},{6,30},{... | collective-permute-start | bytes 786440 | tf_op jit(solution)/shard_map/ppermute | solution.py:298
  79.6 10.9 %collective-permute-start.6 = (bf16[256,512]{1,0:T(8,128)(2,1)S(1)}, bf16[256,512]{1,0:T(8,128)(2,1)}, u32[]{:S(2)}, u32[]{:S(2)}) collective-permute-start(bf16[256,512]{1,0:T(8,128)(2,1)S(1)} %get-tuple-element.36.mixed_ref.rest_2_.rest_5_), channel_id=1, source_target_pairs={{0,4},{4,0},{8,12},{12,8},{16,20},{20,16},{24,28},{28,24},{1,5},{5... | collective-permute-start | bytes 786440 | tf_op jit(solution)/shard_map/ppermute | solution.py:62
  90.2 15.8 %collective-permute-start.12 = (bf16[256,512]{1,0:T(8,128)(2,1)}, bf16[256,512]{1,0:T(8,128)(2,1)}, u32[]{:S(2)}, u32[]{:S(2)}) collective-permute-start(bf16[256,512]{1,0:T(8,128)(2,1)} %get-tuple-element.39), channel_id=1, source_target_pairs={{0,4},{4,0},{8,12},{12,8},{16,20},{20,16},{24,28},{28,24},{1,5},{5... | collective-permute-start | bytes 786440 | tf_op jit(solution)/shard_map/ppermute | solution.py:62
  100.8 23.9 %collective-permute-start.15 = (bf16[512,512]{1,0:T(8,128)(2,1)}, bf16[512,512]{1,0:T(8,128)(2,1)S(1)}, u32[]{:S(2)}, u32[]{:S(2)}) collective-permute-start(bf16[512,512]{1,0:T(8,128)(2,1)} %get-tuple-element.53), channel_id=1, source_target_pairs={{0,8},{4,12},{8,16},{12,20},{16,24},{20,28},{24,0},{28,4},{1,9},{5... | collective-permute-start | bytes 1572872 | tf_op jit(solution)/shard_map/ppermute | solution.py:58
  106.1 20.8 %collective-permute-start.16 = (bf16[512,512]{1,0:T(8,128)(2,1)}, bf16[512,512]{1,0:T(8,128)(2,1)S(1)}, u32[]{:S(2)}, u32[]{:S(2)}) collective-permute-start(bf16[512,512]{1,0:T(8,128)(2,1)} %get-tuple-element.54), channel_id=1, source_target_pairs={{0,24},{4,28},{8,0},{12,4},{16,8},{20,12},{24,16},{28,20},{1,25},{... | collective-permute-start | bytes 1572872 | tf_op jit(solution)/shard_map/ppermute | solution.py:58
  111.0 20.5 %copy-start.21 = (bf16[2,384,512]{2,1,0:T(8,128)(2,1)}, bf16[2,384,512]{2,1,0:T(8,128)(2,1)S(1)}, u32[]{:S(2)}) copy-start(bf16[2,384,512]{2,1,0:T(8,128)(2,1)S(1)} %first_grad.1) | copy-start | bytes 2359300
  111.0 20.5 %collective-permute-start.17 = (bf16[2,384,512]{2,1,0:T(8,128)(2,1)S(1)}, bf16[2,384,512]{2,1,0:T(8,128)(2,1)S(1)}, u32[]{:S(2)}, u32[]{:S(2)}) collective-permute-start(bf16[2,384,512]{2,1,0:T(8,128)(2,1)S(1)} %first_grad.1), channel_id=1, source_target_pairs={{0,4},{4,0},{8,12},{12,8},{16,20},{20,16},{24,28},{28,24},{1,5},{5... | collective-permute-start | bytes 2359304 | tf_op jit(solution)/shard_map/ppermute | solution.py:62
  120.7 20.5 %collective-permute-start.13 = (bf16[2,256,512]{2,1,0:T(8,128)(2,1)S(1)}, bf16[2,256,512]{2,1,0:T(8,128)(2,1)S(1)}, u32[]{:S(2)}, u32[]{:S(2)}) collective-permute-start(bf16[2,256,512]{2,1,0:T(8,128)(2,1)S(1)} %get-tuple-element.47), channel_id=1, source_target_pairs={{0,4},{4,0},{8,12},{12,8},{16,20},{20,16},{24,28},{28,24},{1,5},{5... | collective-permute-start | bytes 1572872 | tf_op jit(solution)/shard_map/ppermute | solution.py:62
  124.6 16.5 %copy-start.27 = (bf16[512,512]{1,0:T(8,128)(2,1)}, bf16[512,512]{1,0:T(8,128)(2,1)S(1)}, u32[]{:S(2)}) copy-start(bf16[512,512]{1,0:T(8,128)(2,1)S(1)} %collective-permute-done.15) | copy-start | bytes 1572868
  131.6 23.2 %copy-start.15 = (f32[512,512]{1,0:T(8,128)S(1)}, f32[512,512]{1,0:T(8,128)}, u32[]{:S(2)}) copy-start(f32[512,512]{1,0:T(8,128)} %copy-done.14) | copy-start | bytes 3145732
  132.9 21.3 %collective-permute-start.22 = (bf16[512,512]{1,0:T(8,128)(2,1)S(1)}, bf16[512,512]{1,0:T(8,128)(2,1)S(1)}, u32[]{:S(2)}, u32[]{:S(2)}) collective-permute-start(bf16[512,512]{1,0:T(8,128)(2,1)S(1)} %copy-done.25), channel_id=1, source_target_pairs={{0,16},{4,20},{8,24},{12,28},{16,0},{20,4},{24,8},{28,12},{1,17},{... | collective-permute-start | bytes 1572872 | tf_op jit(solution)/shard_map/ppermute | solution.py:58
  136.3 25.2 %collective-permute-start.21 = (bf16[2,128,512]{2,1,0:T(8,128)(2,1)S(1)}, bf16[2,128,512]{2,1,0:T(8,128)(2,1)S(1)}, u32[]{:S(2)}, u32[]{:S(2)}) collective-permute-start(bf16[2,128,512]{2,1,0:T(8,128)(2,1)S(1)} %get-tuple-element.61), channel_id=1, source_target_pairs={{24,0},{25,1},{26,2},{27,3}} | collective-permute-start | bytes 786440 | tf_op jit(solution)/shard_map/ppermute | solution.py:452
  137.0 37.3 %collective-permute-start.20 = (bf16[2,128,512]{2,1,0:T(8,128)(2,1)S(1)}, bf16[2,128,512]{2,1,0:T(8,128)(2,1)}, u32[]{:S(2)}, u32[]{:S(2)}) collective-permute-start(bf16[2,128,512]{2,1,0:T(8,128)(2,1)S(1)} %get-tuple-element.61), channel_id=1, source_target_pairs={{16,0},{17,1},{18,2},{19,3}} | collective-permute-start | bytes 786440 | tf_op jit(solution)/shard_map/ppermute | solution.py:452
  138.4 35.9 %collective-permute-start.18 = (bf16[2,256,512]{2,1,0:T(8,128)(2,1)}, bf16[2,256,512]{2,1,0:T(8,128)(2,1)}, u32[]{:S(2)}, u32[]{:S(2)}) collective-permute-start(bf16[2,256,512]{2,1,0:T(8,128)(2,1)} %get-tuple-element.59), channel_id=1, source_target_pairs={{8,0},{12,4},{16,8},{20,12},{24,16},{28,20},{9,1},{13,5},{17,9},{2... | collective-permute-start | bytes 1572872 | tf_op jit(solution)/shard_map/ppermute | solution.py:27
  141.2 33.1 %collective-permute-start.19 = (bf16[2,256,512]{2,1,0:T(8,128)(2,1)}, bf16[2,256,512]{2,1,0:T(8,128)(2,1)}, u32[]{:S(2)}, u32[]{:S(2)}) collective-permute-start(bf16[2,256,512]{2,1,0:T(8,128)(2,1)} %get-tuple-element.60), channel_id=1, source_target_pairs={{0,8},{4,12},{8,16},{12,20},{16,24},{20,28},{1,9},{5,13},{9,17},{1... | collective-permute-start | bytes 1572872 | tf_op jit(solution)/shard_map/ppermute | solution.py:27
  154.2 6.4 %collective-permute-start.14 = (bf16[256,512]{1,0:T(8,128)(2,1)S(1)}, bf16[256,512]{1,0:T(8,128)(2,1)S(1)}, u32[]{:S(2)}, u32[]{:S(2)}) collective-permute-start(bf16[256,512]{1,0:T(8,128)(2,1)S(1)} %get-tuple-element.72), channel_id=1, source_target_pairs={{0,4},{4,0},{8,12},{12,8},{16,20},{20,16},{24,28},{28,24},{1,5},{5... | collective-permute-start | bytes 786440 | tf_op jit(solution)/shard_map/ppermute | solution.py:62
  (24 other events, 112.9 us)
Sparse Core Ops, SparseCore 0:
  30.0 22.7 all-gather.1
  100.9 34.9 reduce-scatter.1

commit v3 on v2

--- a/solution.py
+++ b/solution.py
@@ -375,19 +375,8 @@
             cost_estimate=CHEAP,
             name="weight_part",
         )(grad_side, mixed, mixed_other)
-        partial_out = pl.pallas_call(
-            functools.partial(outs_kernel, length),
-            in_specs=[whole] * 2 + [anywhere] * 6,
-            out_specs=pl.BlockSpec((2 * tokens, length * width), lambda: (0, 0)),
-            out_shape=jax.ShapeDtypeStruct((2 * tokens, length * width), jnp.bfloat16),
-            scratch_shapes=held,
-            compiler_params=pltpu.CompilerParams(vmem_limit_bytes=32 * 1024 * 1024),
-            cost_estimate=CHEAP,
-            name="project_out",
-        )(mixed, tied(mixed_other, own_part), *weight_pieces)
-        scattered = lax.psum_scatter(partial_out, "head", scatter_dimension=1, tiled=True)
         mixed_grad = tied(mixed_grad, own_part)
-        weight_turns = [turned(weight_parts[n - 1], n, length) for n in (1, 3)]
+        weight_turns = [turned(weight_parts[n - 1], n, length) for n in range(1, length)]
     else:
         partial_out = mm(mixed, full_weight, NT).astype(jnp.bfloat16)
         mixed_grad = mm(grad_full, full_weight, NN).astype(jnp.bfloat16)
@@ -407,7 +396,21 @@
         name="first_grad",
     )(run_word, block_lists, queries, *early_bands, first, mixed, mixed_grad, lse)
 
-    lse_later = tied(lse, early_grads, partial_out)
+    if direct:
+        partial_out = pl.pallas_call(
+            functools.partial(outs_kernel, length),
+            in_specs=[whole] * 2 + [anywhere] * 6,
+            out_specs=pl.BlockSpec((2 * tokens, length * width), lambda: (0, 0)),
+            out_shape=jax.ShapeDtypeStruct((2 * tokens, length * width), jnp.bfloat16),
+            scratch_shapes=held,
+            compiler_params=pltpu.CompilerParams(vmem_limit_bytes=32 * 1024 * 1024),
+            cost_estimate=CHEAP,
+            name="project_out",
+        )(mixed, tied(mixed_other, early_grads), *weight_pieces)
+        scattered = lax.psum_scatter(partial_out, "head", scatter_dimension=1, tiled=True)
+        lse_later = tied(lse, early_grads, partial_out)
+    else:
+        lse_later = tied(lse, early_grads)
     results = pl.pallas_call(
         functools.partial(bwd_kernel, offsets, early, per_dev, scale),
         grid=(groups,),
@@ -435,9 +438,7 @@
         to_after = to_after.astype(jnp.float32) + jnp.where(side == 0, diagonal, 0.0)
         back_pair = swapped(to_beside, range(length))
         to_before, to_after = to_before.astype(jnp.bfloat16), to_after.astype(jnp.bfloat16)
-        to_before, to_after, near, last_part = lax.optimization_barrier(
-            (to_before, to_after, first_sum.astype(jnp.bfloat16), weight_parts[1])
-        )
+        to_before, to_after, near = lax.optimization_barrier((to_before, to_after, first_sum.astype(jnp.bfloat16)))
         back_down = shifted(to_before, -2)
         back_up = shifted(to_after, 2)
         scattered = tied(scattered, back_pair)
@@ -446,7 +447,7 @@
             side == 0, jnp.concatenate([mine, theirs], axis=1), jnp.concatenate([theirs, mine], axis=1)
         )
         weight_grad = own_part
-        for part in weight_turns + [turned(last_part, 2, length)]:
+        for part in weight_turns:
             weight_grad = weight_grad + part.astype(jnp.float32)
         for c in range(length, ctx, 2):
             got = tied(lax.ppermute(near, "ctx", [(c, 0)]), back_down, back_up, attended)

time: 187 us -> 193 us (1.032); the launches traced: 186 us -> 190 us
  waiting for transfers between devices: 59.6 us -> 67.2 us
  starting transfers between devices: 56.7 us -> 53.6 us
  Pallas kernels: 33.6 us -> 31.3 us
    ppermute x3, waiting for transfers between devices: 11.9 us -> 27.8 us  [turned(): lax.ppermute(x, 'ctx', [(2 * z + n, 2 * ((z + by) % length) + n) for z in...]
    ppermute x4, waiting for transfers between devices: 12.8 us -> 5.39 us  [shifted(): lax.ppermute(x, 'ctx', [(i, i + by) for i in range(peers) if 0 <= i + by...]
    ppermute x3, starting transfers between devices: 8.72 us -> 6.35 us  [turned(): lax.ppermute(x, 'ctx', [(2 * z + n, 2 * ((z + by) % length) + n) for z in...]
    unnamed x63 -> x59, local copies, waits for them, and re-layouts: 8.27 us -> 8.69 us
  transfers between devices with their start and end apart: 25 -> 25, of which waited for: 10 -> 10; matrix products, arithmetic and copies ran while one was open for 4% -> 5% of each run, Pallas kernels for 17% -> 11%
where the time goes in v3:
time: 193 us; the launch traced here: 190 us
  waiting for transfers between devices  67.2 us (35%)
  starting transfers between devices  53.6 us (28%)
  Pallas kernels  31.3 us (16%)
  between operations  14.5 us (8%)
  other arithmetic  11.9 us (6%)
  local copies, waits for them, and re-layouts  11.1 us (6%)
    ppermute x3, waiting for transfers between devices, turned(): lax.ppermute(x, 'ctx', [(2 * z + n, 2 * ((z + by) % length) + n) for z in...  27.8 us
    ppermute x5, starting transfers between devices, between(): lax.ppermute(x, 'ctx', [(2 * a + n, 2 * b + n) for a, b in places for n i...  22.4 us
    ppermute x6, waiting for transfers between devices, swapped(): lax.ppermute(piece, 'ctx', [(2 * z + n, 2 * z + 1 - n) for z in places fo...  19.4 us
    ppermute x4, starting transfers between devices, shifted(): lax.ppermute(x, 'ctx', [(i, i + by) for i in range(peers) if 0 <= i + by...  11.7 us
    ppermute x5, waiting for transfers between devices, between(): lax.ppermute(x, 'ctx', [(2 * a + n, 2 * b + n) for a, b in places for n i...  11.1 us
    pallas_call x1, Pallas kernels, local(): pl.pallas_call(functools.partial(bwd_kernel, offsets, early, per_dev, sca...  9.01 us
    unnamed x59, local copies, waits for them, and re-layouts  8.69 us
    pallas_call x1, Pallas kernels, local(): pl.pallas_call(functools.partial(fwd_kernel, offsets, per_dev, scale), gr...  6.76 us
  transfers between devices with their start and end apart: 25, of which 10 were waited for; matrix products, arithmetic and copies ran while one was open for 5% of the time, Pallas kernels for 11%

profile of v3, /device:TPU:12, one launch (start us, length us, event | category | flops | bytes accessed | tf_op | source)
XLA Modules:
  0.0 189.6 jit_solution(12587933495708545929)
XLA Ops:
  11.1 2.4 %collective-permute-start.1 = (bf16[2,256,512]{2,1,0:T(8,128)(2,1)S(1)}, bf16[2,256,512]{2,1,0:T(8,128)(2,1)S(1)}, u32[]{:S(2)}, u32[]{:S(2)}) collective-permute-start(bf16[2,256,512]{2,1,0:T(8,128)(2,1)S(1)} %pad_maximum_fusion.1), channel_id=1, source_target_pairs={{8,0},{12,4},{16,8},{20,12},{24,16},{28,20},{9,1},{13,5},{17,9},{2... | collective-permute-start | bytes 1572872 | tf_op jit(solution)/shard_map/ppermute | solution.py:27
  13.5 3.5 %collective-permute-start = (bf16[2,256,512]{2,1,0:T(8,128)(2,1)S(1)}, bf16[2,256,512]{2,1,0:T(8,128)(2,1)S(1)}, u32[]{:S(2)}, u32[]{:S(2)}) collective-permute-start(bf16[2,256,512]{2,1,0:T(8,128)(2,1)S(1)} %pad_maximum_fusion.1), channel_id=1, source_target_pairs={{0,8},{4,12},{8,16},{12,20},{16,24},{20,28},{1,9},{5,13},{9,17},{1... | collective-permute-start | bytes 1572872 | tf_op jit(solution)/shard_map/ppermute | solution.py:27
  17.0 11.9 %collective-permute-done.2.rest_2_ = bf16[3,256,512]{2,1,0:T(8,128)(2,1)S(1)} collective-permute-done((bf16[3,256,512]{2,1,0:T(8,128)(2,1)S(1)}, bf16[3,256,512]{2,1,0:T(8,128)(2,1)S(1)}, u32[]{:S(2)}, u32[]{:S(2)}) %collective-permute-start.2) | collective-permute-done | bytes 786464 | tf_op jit(solution)/shard_map/ppermute | solution.py:62
  30.6 10.4 %collective-permute-start.7 = (bf16[512,512]{1,0:T(8,128)(2,1)S(1)}, bf16[512,512]{1,0:T(8,128)(2,1)S(1)}, u32[]{:S(2)}, u32[]{:S(2)}) collective-permute-start(bf16[512,512]{1,0:T(8,128)(2,1)S(1)} %copy-done.4), channel_id=1, source_target_pairs={{0,8},{4,12},{8,0},{12,4},{16,24},{20,28},{24,16},{28,20},{1,9},{5... | collective-permute-start | bytes 1572872 | tf_op jit(solution)/shard_map/ppermute | solution.py:302
  41.0 3.8 %collective-permute-start.8 = (bf16[512,512]{1,0:T(8,128)(2,1)S(1)}, bf16[512,512]{1,0:T(8,128)(2,1)}, u32[]{:S(2)}, u32[]{:S(2)}) collective-permute-start(bf16[512,512]{1,0:T(8,128)(2,1)S(1)} %copy-done.4), channel_id=1, source_target_pairs={{8,16},{12,20},{16,8},{20,12},{9,17},{13,21},{17,9},{21,13},{10,18... | collective-permute-start | bytes 1572872 | tf_op jit(solution)/shard_map/ppermute | solution.py:302
  44.8 6.4 %collective-permute-done.7.rest_1_ = bf16[512,512]{1,0:T(8,128)(2,1)S(1)} collective-permute-done((bf16[512,512]{1,0:T(8,128)(2,1)S(1)}, bf16[512,512]{1,0:T(8,128)(2,1)S(1)}, u32[]{:S(2)}, u32[]{:S(2)}) %collective-permute-start.7) | collective-permute-done | bytes 524320 | tf_op jit(solution)/shard_map/ppermute | solution.py:302
  51.2 4.0 %collective-permute-start.10 = (bf16[512,512]{1,0:T(8,128)(2,1)S(1)}, bf16[512,512]{1,0:T(8,128)(2,1)}, u32[]{:S(2)}, u32[]{:S(2)}) collective-permute-start(bf16[512,512]{1,0:T(8,128)(2,1)S(1)} %collective-permute-done.7.rest_1_), channel_id=1, source_target_pairs={{8,16},{12,20},{16,8},{20,12},{9,17},{13,21},{17,9},{21,13},{10,18... | collective-permute-start | bytes 1572872 | tf_op jit(solution)/shard_map/ppermute | solution.py:302
  56.1 1.9 %collective-permute-start.3 = (bf16[2,256,512]{2,1,0:T(8,128)(2,1)}, bf16[2,256,512]{2,1,0:T(8,128)(2,1)}, u32[]{:S(2)}, u32[]{:S(2)}) collective-permute-start(bf16[2,256,512]{2,1,0:T(8,128)(2,1)} %broadcast_select_fusion), channel_id=1, source_target_pairs={{0,4},{8,12},{16,20},{12,8},{20,16},{28,24},{1,5},{9,13},{17,21},{... | collective-permute-start | bytes 1572872 | tf_op jit(solution)/shard_map/ppermute | solution.py:293
  58.0 2.1 %collective-permute-start.9 = (bf16[512,512]{1,0:T(8,128)(2,1)}, bf16[512,512]{1,0:T(8,128)(2,1)}, u32[]{:S(2)}, u32[]{:S(2)}) collective-permute-start(bf16[512,512]{1,0:T(8,128)(2,1)} %collective-permute-done.8.rest_2_), channel_id=1, source_target_pairs={{8,0},{12,4},{16,24},{20,28},{9,1},{13,5},{17,25},{21,29},{10,2},{... | collective-permute-start | bytes 1572872 | tf_op jit(solution)/shard_map/ppermute | solution.py:302
  60.1 4.7 %collective-permute-done.10.rest_4_ = bf16[512,512]{1,0:T(8,128)(2,1)} collective-permute-done((bf16[512,512]{1,0:T(8,128)(2,1)S(1)}, bf16[512,512]{1,0:T(8,128)(2,1)}, u32[]{:S(2)}, u32[]{:S(2)}) %collective-permute-start.10) | collective-permute-done | bytes 524320 | tf_op jit(solution)/shard_map/ppermute | solution.py:302
  64.8 2.1 %collective-permute-start.11 = (bf16[512,512]{1,0:T(8,128)(2,1)}, bf16[512,512]{1,0:T(8,128)(2,1)}, u32[]{:S(2)}, u32[]{:S(2)}) collective-permute-start(bf16[512,512]{1,0:T(8,128)(2,1)} %collective-permute-done.10.rest_4_), channel_id=1, source_target_pairs={{8,0},{12,4},{16,24},{20,28},{9,1},{13,5},{17,25},{21,29},{10,2},{... | collective-permute-start | bytes 1572872 | tf_op jit(solution)/shard_map/ppermute | solution.py:302
  67.6 2.0 %collective-permute-start.5 = (bf16[2,128,512]{2,1,0:T(8,128)(2,1)}, bf16[2,128,512]{2,1,0:T(8,128)(2,1)}, u32[]{:S(2)}, u32[]{:S(2)}) collective-permute-start(bf16[2,128,512]{2,1,0:T(8,128)(2,1)} %fusion.9), channel_id=1, source_target_pairs={{4,28},{0,12},{16,20},{8,24},{5,29},{1,13},{17,21},{9,25},{6,30},{... | collective-permute-start | bytes 786440 | tf_op jit(solution)/shard_map/ppermute | solution.py:298
  69.7 3.4 %collective-permute-done.5 = bf16[2,128,512]{2,1,0:T(8,128)(2,1)} collective-permute-done((bf16[2,128,512]{2,1,0:T(8,128)(2,1)}, bf16[2,128,512]{2,1,0:T(8,128)(2,1)}, u32[]{:S(2)}, u32[]{:S(2)}) %collective-permute-start.5) | collective-permute-done | bytes 262176 | tf_op jit(solution)/shard_map/ppermute | solution.py:298
  75.1 6.8 %attend.1 = (bf16[256,512]{1,0:T(8,128)(2,1)}, f32[4,1,256]{2,1,0:T(1,128)S(1)}) custom-call(s32[1]{0:T(128)} %bitcast.run_ref, s32[16,3]{1,0:T(8,128)S(1)} %copy.11.lists_ref, bf16[256,512]{1,0:T(8,128)(2,1)S(1)} %copy-done.13, bf16[256,512]{1,0:T(8,128)(2,1)S(1)} %copy-done.3, bf16[256,512]{1,0:T(8,128)(2,1)S(1)} %copy-done.2, ...), custom_call_target="tpu_custom_call" | custom-call | flops 1 | bytes 1 | tf_op jit(solution)/shard_map/attend/pallas_call | solution.py:335
  85.4 2.1 %project_grad.1 = (f32[256,512]{1,0:T(8,128)S(1)}, bf16[256,512]{1,0:T(8,128)(2,1)S(1)}) custom-call(bf16[512,2048]{1,0:T(8,128)(2,1)S(1)} %copy-done, bf16[512,512]{1,0:T(8,128)(2,1)S(1)} %copy-done.4, bf16[512,512]{1,0:T(8,128)(2,1)S(1)} %collective-permute-done.7.rest_1_, bf16[512,512]{1,0:T(8,128)(2,1)} %collective-permute-done.8.rest_2_, ...), custom_call_target="tpu_custom_call" | custom-call | flops 1 | bytes 1 | tf_op jit(solution)/shard_map/project_grad/pallas_call | solution.py:352
  88.4 2.5 %collective-permute-done.6.other_ref = bf16[256,512]{1,0:T(8,128)(2,1)} collective-permute-done((bf16[256,512]{1,0:T(8,128)(2,1)}, bf16[256,512]{1,0:T(8,128)(2,1)}, u32[]{:S(2)}, u32[]{:S(2)}) %collective-permute-start.6) | collective-permute-done | bytes 262176 | tf_op jit(solution)/shard_map/ppermute | solution.py:62
  90.9 2.3 %weight_part.1 = (f32[512,512]{1,0:T(8,128)S(1)}, bf16[512,512]{1,0:T(8,128)(2,1)S(1)}, bf16[512,512]{1,0:T(8,128)(2,1)S(1)}, bf16[512,512]{1,0:T(8,128)(2,1)S(1)}) custom-call(bf16[512,2048]{1,0:T(8,128)(2,1)S(1)} %copy-done.1, bf16[256,512]{1,0:T(8,128)(2,1)} %get-tuple-element.35.mixed_ref.rest_2_.rest_5_, bf16[256,512]{1,0:T(8,128)(2,1)} %collective-permute-done.6.other_ref), custom_call_target="tpu_custom_call" | custom-call | flops 1 | bytes 1 | tf_op jit(solution)/shard_map/weight_part/pallas_call | solution.py:367
  95.1 4.0 %first_grad.1 = bf16[2,384,512]{2,1,0:T(8,128)(2,1)S(1)} custom-call(s32[1]{0:T(128)} %bitcast.run_ref, s32[16,3]{1,0:T(8,128)S(1)} %copy.11.lists_ref, bf16[256,512]{1,0:T(8,128)(2,1)S(1)} %copy-done.14, bf16[2,256,512]{2,1,0:T(8,128)(2,1)} %collective-permute-done.3.rest_3_.rest_0_, bf16[2,128,512]{2,1,0:T(8,128)(2,1)S(1)} %copy-done.9, ...), custom_call_target="tpu_custom_call" | custom-call | flops 10000000000 | bytes 1 | tf_op jit(solution)/shard_map/first_grad/pallas_call | solution.py:387
  100.7 4.5 %project_out.1 = bf16[512,2048]{1,0:T(8,128)(2,1)} custom-call(bf16[256,512]{1,0:T(8,128)(2,1)} %get-tuple-element.35.mixed_ref.rest_2_.rest_5_, bf16[256,512]{1,0:T(8,128)(2,1)} %collective-permute-done.6.other_ref, bf16[512,512]{1,0:T(8,128)(2,1)S(1)} %copy-done.4, bf16[512,512]{1,0:T(8,128)(2,1)S(1)} %collective-permute-done.7.rest_1_, ...), custom_call_target="tpu_custom_call" | custom-call | flops 1 | bytes 1 | tf_op jit(solution)/shard_map/project_out/pallas_call | solution.py:400
  105.2 4.6 %collective-permute-start.15 = (bf16[512,512]{1,0:T(8,128)(2,1)}, bf16[512,512]{1,0:T(8,128)(2,1)S(1)}, u32[]{:S(2)}, u32[]{:S(2)}) collective-permute-start(bf16[512,512]{1,0:T(8,128)(2,1)} %copy-done.20), channel_id=1, source_target_pairs={{0,8},{4,12},{8,16},{12,20},{16,24},{20,28},{24,0},{28,4},{1,9},{5... | collective-permute-start | bytes 1572872 | tf_op jit(solution)/shard_map/ppermute | solution.py:58
  109.8 1.7 collective-permute-start.17
  111.6 1.7 collective-permute-start.18
  115.3 9.0 %attend_grad.1 = (bf16[256,512]{1,0:T(8,128)(2,1)}, f32[2,256,512]{2,1,0:T(8,128)S(1)}, bf16[2,256,512]{2,1,0:T(8,128)(2,1)S(1)}, bf16[2,256,512]{2,1,0:T(8,128)(2,1)S(1)}, bf16[2,256,512]{2,1,0:T(8,128)(2,1)S(1)}) custom-call(s32[1]{0:T(128)} %bitcast.run_ref, s32[16,3]{1,0:T(8,128)S(1)} %copy.11.lists_ref, bf16[256,512]{1,0:T(8,128)(2,1)S(1)} %copy-done.15, ...), custom_call_target="tpu_custom_call" | custom-call | flops 30000001024 | bytes 1 | tf_op jit(solution)/shard_map/attend_grad/pallas_call | solution.py:414
  124.5 18.7 %collective-permute-done.15 = bf16[512,512]{1,0:T(8,128)(2,1)S(1)} collective-permute-done((bf16[512,512]{1,0:T(8,128)(2,1)}, bf16[512,512]{1,0:T(8,128)(2,1)S(1)}, u32[]{:S(2)}, u32[]{:S(2)}) %collective-permute-start.15) | collective-permute-done | bytes 524320 | tf_op jit(solution)/shard_map/ppermute | solution.py:58
  143.3 8.1 %collective-permute-done.16 = bf16[512,512]{1,0:T(8,128)(2,1)S(1)} collective-permute-done((bf16[512,512]{1,0:T(8,128)(2,1)}, bf16[512,512]{1,0:T(8,128)(2,1)S(1)}, u32[]{:S(2)}, u32[]{:S(2)}) %collective-permute-start.16) | collective-permute-done | bytes 524320 | tf_op jit(solution)/shard_map/ppermute | solution.py:58
  156.6 1.9 %collective-permute-start.19 = (bf16[2,256,512]{2,1,0:T(8,128)(2,1)}, bf16[2,256,512]{2,1,0:T(8,128)(2,1)S(1)}, u32[]{:S(2)}, u32[]{:S(2)}) collective-permute-start(bf16[2,256,512]{2,1,0:T(8,128)(2,1)} %get-tuple-element.58), channel_id=1, source_target_pairs={{8,0},{12,4},{16,8},{20,12},{24,16},{28,20},{9,1},{13,5},{17,9},{2... | collective-permute-start | bytes 1572872 | tf_op jit(solution)/shard_map/ppermute | solution.py:27
  158.5 3.9 %collective-permute-start.20 = (bf16[2,256,512]{2,1,0:T(8,128)(2,1)}, bf16[2,256,512]{2,1,0:T(8,128)(2,1)}, u32[]{:S(2)}, u32[]{:S(2)}) collective-permute-start(bf16[2,256,512]{2,1,0:T(8,128)(2,1)} %get-tuple-element.59), channel_id=1, source_target_pairs={{0,8},{4,12},{8,16},{12,20},{16,24},{20,28},{1,9},{5,13},{9,17},{1... | collective-permute-start | bytes 1572872 | tf_op jit(solution)/shard_map/ppermute | solution.py:27
  163.8 2.6 %convert_add_fusion = f32[512,512]{1,0:T(8,128)} fusion(bf16[512,512]{1,0:T(8,128)(2,1)} %copy-done.24, bf16[512,512]{1,0:T(8,128)(2,1)} %copy-done.23, f32[512,512]{1,0:T(8,128)S(1)} %copy-done.6, bf16[512,512]{1,0:T(8,128)(2,1)} %copy-done.22), kind=kLoop, calls=%fused_computation.7 | loop fusion | flops 1572864 | bytes 3670016 | tf_op jit(solution)/shard_map/add | solution.py:451
  166.5 5.0 %collective-permute-done.14 = bf16[256,512]{1,0:T(8,128)(2,1)S(1)} collective-permute-done((bf16[256,512]{1,0:T(8,128)(2,1)S(1)}, bf16[256,512]{1,0:T(8,128)(2,1)S(1)}, u32[]{:S(2)}, u32[]{:S(2)}) %collective-permute-start.14) | collective-permute-done | bytes 262176 | tf_op jit(solution)/shard_map/ppermute | solution.py:62
  172.4 5.4 %collective-permute-done.19.b_ref = bf16[2,256,512]{2,1,0:T(8,128)(2,1)S(1)} collective-permute-done((bf16[2,256,512]{2,1,0:T(8,128)(2,1)}, bf16[2,256,512]{2,1,0:T(8,128)(2,1)S(1)}, u32[]{:S(2)}, u32[]{:S(2)}) %collective-permute-start.19) | collective-permute-done | bytes 524320 | tf_op jit(solution)/shard_map/ppermute | solution.py:27
  177.8 2.2 %convert_add_fusion.1.first_ref = f32[2,128,512]{2,1,0:T(8,128)} fusion(bf16[2,128,512]{2,1,0:T(8,128)(2,1)} %collective-permute-done.22, bf16[2,128,512]{2,1,0:T(8,128)(2,1)} %collective-permute-done.21, bf16[2,384,512]{2,1,0:T(8,128)(2,1)S(1)} %copy-done.12, bf16[2,384,512]{2,1,0:T(8,128)(2,1)} %copy-done.21), kind=kLoop, calls=%fused_computation.14 | loop fusion | flops 917504 | bytes 1572864 | tf_op jit(solution)/shard_map/add | solution.py:454
  180.1 2.7 %finish.1 = (bf16[256,512]{1,0:T(8,128)(2,1)}, bf16[256,512]{1,0:T(8,128)(2,1)}) custom-call(s32[1]{0:T(128)} %bitcast.run_ref, f32[2,256,512]{2,1,0:T(8,128)} %copy-done.7, bf16[2,256,512]{2,1,0:T(8,128)(2,1)} %copy-done.25, bf16[2,256,512]{2,1,0:T(8,128)(2,1)} %copy-done.26, bf16[2,256,512]{2,1,0:T(8,128)(2,1)} %collective-permute-done.20.c_ref, ...), custom_call_target="tpu_custom_call" | custom-call | flops 1 | bytes 1 | tf_op jit(solution)/shard_map/finish/pallas_call | solution.py:458
  (102 shorter events, 26.7 us)
Async XLA Ops:
  7.2 76.6 %all-gather.2.cloned.1.call-start = ((), (), s32[]{:S(2)}) async-start(), calls=%async_computation.1 | async-start | bytes 2621440 | tf_op jit(solution)/shard_map/all_gather | solution.py:290
  9.5 21.0 %copy-start.4 = (bf16[512,512]{1,0:T(8,128)(2,1)S(1)}, bf16[512,512]{1,0:T(8,128)(2,1)}, u32[]{:S(2)}) copy-start(bf16[512,512]{1,0:T(8,128)(2,1)} %rest_0_.1) | copy-start | bytes 1572868
  9.5 19.3 %collective-permute-start.2 = (bf16[3,256,512]{2,1,0:T(8,128)(2,1)S(1)}, bf16[3,256,512]{2,1,0:T(8,128)(2,1)S(1)}, u32[]{:S(2)}, u32[]{:S(2)}) collective-permute-start(bf16[3,256,512]{2,1,0:T(8,128)(2,1)S(1)} %pad_maximum_fusion), channel_id=1, source_target_pairs={{0,4},{4,0},{8,12},{12,8},{16,20},{20,16},{24,28},{28,24},{1,5},{5... | collective-permute-start | bytes 2359304 | tf_op jit(solution)/shard_map/ppermute | solution.py:62
  11.1 17.8 %collective-permute-start.1 = (bf16[2,256,512]{2,1,0:T(8,128)(2,1)S(1)}, bf16[2,256,512]{2,1,0:T(8,128)(2,1)S(1)}, u32[]{:S(2)}, u32[]{:S(2)}) collective-permute-start(bf16[2,256,512]{2,1,0:T(8,128)(2,1)S(1)} %pad_maximum_fusion.1), channel_id=1, source_target_pairs={{8,0},{12,4},{16,8},{20,12},{24,16},{28,20},{9,1},{13,5},{17,9},{2... | collective-permute-start | bytes 1572872 | tf_op jit(solution)/shard_map/ppermute | solution.py:27
  13.5 15.4 %collective-permute-start = (bf16[2,256,512]{2,1,0:T(8,128)(2,1)S(1)}, bf16[2,256,512]{2,1,0:T(8,128)(2,1)S(1)}, u32[]{:S(2)}, u32[]{:S(2)}) collective-permute-start(bf16[2,256,512]{2,1,0:T(8,128)(2,1)S(1)} %pad_maximum_fusion.1), channel_id=1, source_target_pairs={{0,8},{4,12},{8,16},{12,20},{16,24},{20,28},{1,9},{5,13},{9,17},{1... | collective-permute-start | bytes 1572872 | tf_op jit(solution)/shard_map/ppermute | solution.py:27
  29.8 39.8 %copy-start.28 = (s32[16,3]{0,1:T(4,128)S(1)}, s32[16,3]{0,1:T(4,128)}, u32[]{:S(2)}) copy-start(s32[16,3]{0,1:T(4,128)} %param.10) | copy-start | bytes 580
  29.8 132.7 %reduce-scatter.2.cloned.1.call-start = ((), (), s32[]{:S(2)}) async-start(), calls=%async_computation.2 | async-start | bytes 2621440 | tf_op jit(solution)/shard_map/reduce_scatter | solution.py:410
  29.9 0.7 collective-permute-start.4
  30.6 20.6 %copy-start.27 = (bf16[2,128,512]{2,1,0:T(8,128)(2,1)}, bf16[2,128,512]{2,1,0:T(8,128)(2,1)S(1)}, u32[]{:S(2)}) copy-start(bf16[2,128,512]{2,1,0:T(8,128)(2,1)S(1)} %collective-permute-done.4) | copy-start | bytes 786436
  30.6 20.6 %collective-permute-start.7 = (bf16[512,512]{1,0:T(8,128)(2,1)S(1)}, bf16[512,512]{1,0:T(8,128)(2,1)S(1)}, u32[]{:S(2)}, u32[]{:S(2)}) collective-permute-start(bf16[512,512]{1,0:T(8,128)(2,1)S(1)} %copy-done.4), channel_id=1, source_target_pairs={{0,8},{4,12},{8,0},{12,4},{16,24},{20,28},{24,16},{28,20},{1,9},{5... | collective-permute-start | bytes 1572872 | tf_op jit(solution)/shard_map/ppermute | solution.py:302
  41.0 17.0 %collective-permute-start.8 = (bf16[512,512]{1,0:T(8,128)(2,1)S(1)}, bf16[512,512]{1,0:T(8,128)(2,1)}, u32[]{:S(2)}, u32[]{:S(2)}) collective-permute-start(bf16[512,512]{1,0:T(8,128)(2,1)S(1)} %copy-done.4), channel_id=1, source_target_pairs={{8,16},{12,20},{16,8},{20,12},{9,17},{13,21},{17,9},{21,13},{10,18... | collective-permute-start | bytes 1572872 | tf_op jit(solution)/shard_map/ppermute | solution.py:302
  51.2 13.6 %collective-permute-start.10 = (bf16[512,512]{1,0:T(8,128)(2,1)S(1)}, bf16[512,512]{1,0:T(8,128)(2,1)}, u32[]{:S(2)}, u32[]{:S(2)}) collective-permute-start(bf16[512,512]{1,0:T(8,128)(2,1)S(1)} %collective-permute-done.7.rest_1_), channel_id=1, source_target_pairs={{8,16},{12,20},{16,8},{20,12},{9,17},{13,21},{17,9},{21,13},{10,18... | collective-permute-start | bytes 1572872 | tf_op jit(solution)/shard_map/ppermute | solution.py:302
  56.1 18.1 %collective-permute-start.3 = (bf16[2,256,512]{2,1,0:T(8,128)(2,1)}, bf16[2,256,512]{2,1,0:T(8,128)(2,1)}, u32[]{:S(2)}, u32[]{:S(2)}) collective-permute-start(bf16[2,256,512]{2,1,0:T(8,128)(2,1)} %broadcast_select_fusion), channel_id=1, source_target_pairs={{0,4},{8,12},{16,20},{12,8},{20,16},{28,24},{1,5},{9,13},{17,21},{... | collective-permute-start | bytes 1572872 | tf_op jit(solution)/shard_map/ppermute | solution.py:293
  58.0 25.8 %collective-permute-start.9 = (bf16[512,512]{1,0:T(8,128)(2,1)}, bf16[512,512]{1,0:T(8,128)(2,1)}, u32[]{:S(2)}, u32[]{:S(2)}) collective-permute-start(bf16[512,512]{1,0:T(8,128)(2,1)} %collective-permute-done.8.rest_2_), channel_id=1, source_target_pairs={{8,0},{12,4},{16,24},{20,28},{9,1},{13,5},{17,25},{21,29},{10,2},{... | collective-permute-start | bytes 1572872 | tf_op jit(solution)/shard_map/ppermute | solution.py:302
  64.8 19.0 %collective-permute-start.11 = (bf16[512,512]{1,0:T(8,128)(2,1)}, bf16[512,512]{1,0:T(8,128)(2,1)}, u32[]{:S(2)}, u32[]{:S(2)}) collective-permute-start(bf16[512,512]{1,0:T(8,128)(2,1)} %collective-permute-done.10.rest_4_), channel_id=1, source_target_pairs={{8,0},{12,4},{16,24},{20,28},{9,1},{13,5},{17,25},{21,29},{10,2},{... | collective-permute-start | bytes 1572872 | tf_op jit(solution)/shard_map/ppermute | solution.py:302
  67.6 5.5 %collective-permute-start.5 = (bf16[2,128,512]{2,1,0:T(8,128)(2,1)}, bf16[2,128,512]{2,1,0:T(8,128)(2,1)}, u32[]{:S(2)}, u32[]{:S(2)}) collective-permute-start(bf16[2,128,512]{2,1,0:T(8,128)(2,1)} %fusion.9), channel_id=1, source_target_pairs={{4,28},{0,12},{16,20},{8,24},{5,29},{1,13},{17,21},{9,25},{6,30},{... | collective-permute-start | bytes 786440 | tf_op jit(solution)/shard_map/ppermute | solution.py:298
  82.5 8.3 %collective-permute-start.6 = (bf16[256,512]{1,0:T(8,128)(2,1)}, bf16[256,512]{1,0:T(8,128)(2,1)}, u32[]{:S(2)}, u32[]{:S(2)}) collective-permute-start(bf16[256,512]{1,0:T(8,128)(2,1)} %get-tuple-element.35.mixed_ref.rest_2_.rest_5_), channel_id=1, source_target_pairs={{0,4},{4,0},{8,12},{12,8},{16,20},{20,16},{24,28},{28,24},{1,5},{5... | collective-permute-start | bytes 786440 | tf_op jit(solution)/shard_map/ppermute | solution.py:62
  87.5 7.5 %collective-permute-start.12 = (bf16[256,512]{1,0:T(8,128)(2,1)S(1)}, bf16[256,512]{1,0:T(8,128)(2,1)S(1)}, u32[]{:S(2)}, u32[]{:S(2)}) collective-permute-start(bf16[256,512]{1,0:T(8,128)(2,1)S(1)} %get-tuple-element.38), channel_id=1, source_target_pairs={{0,4},{4,0},{8,12},{12,8},{16,20},{20,16},{24,28},{28,24},{1,5},{5... | collective-permute-start | bytes 786440 | tf_op jit(solution)/shard_map/ppermute | solution.py:62
  105.2 8.1 %copy-start.10 = (bf16[2,128,512]{2,1,0:T(8,128)(2,1)S(1)}, bf16[2,128,512]{2,1,0:T(8,128)(2,1)}, u32[]{:S(2)}) copy-start(bf16[2,128,512]{2,1,0:T(8,128)(2,1)} %copy-done.8) | copy-start | bytes 786436
  105.2 38.0 %collective-permute-start.15 = (bf16[512,512]{1,0:T(8,128)(2,1)}, bf16[512,512]{1,0:T(8,128)(2,1)S(1)}, u32[]{:S(2)}, u32[]{:S(2)}) collective-permute-start(bf16[512,512]{1,0:T(8,128)(2,1)} %copy-done.20), channel_id=1, source_target_pairs={{0,8},{4,12},{8,16},{12,20},{16,24},{20,28},{24,0},{28,4},{1,9},{5... | collective-permute-start | bytes 1572872 | tf_op jit(solution)/shard_map/ppermute | solution.py:58
  109.8 41.5 %collective-permute-start.16 = (bf16[512,512]{1,0:T(8,128)(2,1)}, bf16[512,512]{1,0:T(8,128)(2,1)S(1)}, u32[]{:S(2)}, u32[]{:S(2)}) collective-permute-start(bf16[512,512]{1,0:T(8,128)(2,1)} %copy-done.19), channel_id=1, source_target_pairs={{0,16},{4,20},{8,24},{12,28},{16,0},{20,4},{24,8},{28,12},{1,17},{... | collective-permute-start | bytes 1572872 | tf_op jit(solution)/shard_map/ppermute | solution.py:58
  109.8 42.5 %collective-permute-start.17 = (bf16[512,512]{1,0:T(8,128)(2,1)}, bf16[512,512]{1,0:T(8,128)(2,1)S(1)}, u32[]{:S(2)}, u32[]{:S(2)}) collective-permute-start(bf16[512,512]{1,0:T(8,128)(2,1)} %copy-done.18), channel_id=1, source_target_pairs={{0,24},{4,28},{8,0},{12,4},{16,8},{20,12},{24,16},{28,20},{1,25},{... | collective-permute-start | bytes 1572872 | tf_op jit(solution)/shard_map/ppermute | solution.py:58
  111.6 40.8 %collective-permute-start.18 = (bf16[2,384,512]{2,1,0:T(8,128)(2,1)S(1)}, bf16[2,384,512]{2,1,0:T(8,128)(2,1)S(1)}, u32[]{:S(2)}, u32[]{:S(2)}) collective-permute-start(bf16[2,384,512]{2,1,0:T(8,128)(2,1)S(1)} %copy-done.12), channel_id=1, source_target_pairs={{0,4},{4,0},{8,12},{12,8},{16,20},{20,16},{24,28},{28,24},{1,5},{5... | collective-permute-start | bytes 2359304 | tf_op jit(solution)/shard_map/ppermute | solution.py:62
  124.3 29.6 %copy-start.7 = (f32[2,256,512]{2,1,0:T(8,128)}, f32[2,256,512]{2,1,0:T(8,128)S(1)}, u32[]{:S(2)}) copy-start(f32[2,256,512]{2,1,0:T(8,128)S(1)} %get-tuple-element.49.own_ref) | copy-start | bytes 3145732
  124.3 38.2 %collective-permute-start.13 = (bf16[2,256,512]{2,1,0:T(8,128)(2,1)S(1)}, bf16[2,256,512]{2,1,0:T(8,128)(2,1)S(1)}, u32[]{:S(2)}, u32[]{:S(2)}) collective-permute-start(bf16[2,256,512]{2,1,0:T(8,128)(2,1)S(1)} %get-tuple-element.46), channel_id=1, source_target_pairs={{0,4},{4,0},{8,12},{12,8},{16,20},{20,16},{24,28},{28,24},{1,5},{5... | collective-permute-start | bytes 1572872 | tf_op jit(solution)/shard_map/ppermute | solution.py:62
  143.3 10.6 %copy-start.22 = (bf16[512,512]{1,0:T(8,128)(2,1)}, bf16[512,512]{1,0:T(8,128)(2,1)S(1)}, u32[]{:S(2)}) copy-start(bf16[512,512]{1,0:T(8,128)(2,1)S(1)} %collective-permute-done.15) | copy-start | bytes 1572868
  152.5 11.3 %copy-start.6 = (f32[512,512]{1,0:T(8,128)S(1)}, f32[512,512]{1,0:T(8,128)}, u32[]{:S(2)}) copy-start(f32[512,512]{1,0:T(8,128)} %copy-done.5) | copy-start | bytes 3145732
  153.9 18.6 %collective-permute-start.22 = (bf16[2,128,512]{2,1,0:T(8,128)(2,1)S(1)}, bf16[2,128,512]{2,1,0:T(8,128)(2,1)}, u32[]{:S(2)}, u32[]{:S(2)}) collective-permute-start(bf16[2,128,512]{2,1,0:T(8,128)(2,1)S(1)} %get-tuple-element.60), channel_id=1, source_target_pairs={{24,0},{25,1},{26,2},{27,3}} | collective-permute-start | bytes 786440 | tf_op jit(solution)/shard_map/ppermute | solution.py:453
  155.2 22.6 %collective-permute-start.21 = (bf16[2,128,512]{2,1,0:T(8,128)(2,1)S(1)}, bf16[2,128,512]{2,1,0:T(8,128)(2,1)}, u32[]{:S(2)}, u32[]{:S(2)}) collective-permute-start(bf16[2,128,512]{2,1,0:T(8,128)(2,1)S(1)} %get-tuple-element.60), channel_id=1, source_target_pairs={{16,0},{17,1},{18,2},{19,3}} | collective-permute-start | bytes 786440 | tf_op jit(solution)/shard_map/ppermute | solution.py:453
  156.6 21.2 %collective-permute-start.19 = (bf16[2,256,512]{2,1,0:T(8,128)(2,1)}, bf16[2,256,512]{2,1,0:T(8,128)(2,1)S(1)}, u32[]{:S(2)}, u32[]{:S(2)}) collective-permute-start(bf16[2,256,512]{2,1,0:T(8,128)(2,1)} %get-tuple-element.58), channel_id=1, source_target_pairs={{8,0},{12,4},{16,8},{20,12},{24,16},{28,20},{9,1},{13,5},{17,9},{2... | collective-permute-start | bytes 1572872 | tf_op jit(solution)/shard_map/ppermute | solution.py:27
  158.5 19.3 %collective-permute-start.20 = (bf16[2,256,512]{2,1,0:T(8,128)(2,1)}, bf16[2,256,512]{2,1,0:T(8,128)(2,1)}, u32[]{:S(2)}, u32[]{:S(2)}) collective-permute-start(bf16[2,256,512]{2,1,0:T(8,128)(2,1)} %get-tuple-element.59), channel_id=1, source_target_pairs={{0,8},{4,12},{8,16},{12,20},{16,24},{20,28},{1,9},{5,13},{9,17},{1... | collective-permute-start | bytes 1572872 | tf_op jit(solution)/shard_map/ppermute | solution.py:27
  163.8 7.7 %collective-permute-start.14 = (bf16[256,512]{1,0:T(8,128)(2,1)S(1)}, bf16[256,512]{1,0:T(8,128)(2,1)S(1)}, u32[]{:S(2)}, u32[]{:S(2)}) collective-permute-start(bf16[256,512]{1,0:T(8,128)(2,1)S(1)} %get-tuple-element.70), channel_id=1, source_target_pairs={{0,4},{4,0},{8,12},{12,8},{16,20},{20,16},{24,28},{28,24},{1,5},{5... | collective-permute-start | bytes 786440 | tf_op jit(solution)/shard_map/ppermute | solution.py:62
  (22 other events, 63.2 us)
Sparse Core Ops, SparseCore 0:
  29.9 22.7 all-gather.1
  105.4 34.0 reduce-scatter.1

commit v4 on v2

--- a/solution.py
+++ b/solution.py
@@ -433,11 +433,11 @@
         to_before, to_after, _ = lax.optimization_barrier((to_before, to_after, weight_turns))
         to_before = to_before.astype(jnp.float32) + jnp.where(side == 1, diagonal, 0.0) + folded
         to_after = to_after.astype(jnp.float32) + jnp.where(side == 0, diagonal, 0.0)
+        to_before, to_after = to_before.astype(jnp.bfloat16), to_after.astype(jnp.bfloat16)
+        to_before, to_after, to_beside, near, last_part = lax.optimization_barrier(
+            (to_before, to_after, to_beside, first_sum.astype(jnp.bfloat16), weight_parts[1])
+        )
         back_pair = swapped(to_beside, range(length))
-        to_before, to_after = to_before.astype(jnp.bfloat16), to_after.astype(jnp.bfloat16)
-        to_before, to_after, near, last_part = lax.optimization_barrier(
-            (to_before, to_after, first_sum.astype(jnp.bfloat16), weight_parts[1])
-        )
         back_down = shifted(to_before, -2)
         back_up = shifted(to_after, 2)
         scattered = tied(scattered, back_pair)

time: 187 us -> 187 us (level)
  waiting for transfers between devices: 59.6 us -> 64 us
  starting transfers between devices: 56.7 us -> 52.9 us
    ppermute x4, starting transfers between devices: 13.3 us -> 10.5 us  [shifted(): lax.ppermute(x, 'ctx', [(i, i + by) for i in range(peers) if 0 <= i + by...]
    ppermute x6, waiting for transfers between devices: 19.9 us -> 22 us  [swapped(): lax.ppermute(piece, 'ctx', [(2 * z + n, 2 * z + 1 - n) for z in places fo...]
where the time goes in v4:
time: 187 us; the launch traced here: 186 us
  waiting for transfers between devices  64 us (34%)
  starting transfers between devices  52.9 us (28%)
  Pallas kernels  33.6 us (18%)
  between operations  14.5 us (8%)
  other arithmetic  10.9 us (6%)
  local copies, waits for them, and re-layouts  10.5 us (6%)
    ppermute x6, waiting for transfers between devices, swapped(): lax.ppermute(piece, 'ctx', [(2 * z + n, 2 * z + 1 - n) for z in places fo...  22 us
    ppermute x5, starting transfers between devices, between(): lax.ppermute(x, 'ctx', [(2 * a + n, 2 * b + n) for a, b in places for n i...  21.7 us
    ppermute x4, waiting for transfers between devices, shifted(): lax.ppermute(x, 'ctx', [(i, i + by) for i in range(peers) if 0 <= i + by...  13.9 us
    ppermute x3, waiting for transfers between devices, turned(): lax.ppermute(x, 'ctx', [(2 * z + n, 2 * ((z + by) % length) + n) for z in...  13 us
    ppermute x5, waiting for transfers between devices, between(): lax.ppermute(x, 'ctx', [(2 * a + n, 2 * b + n) for a, b in places for n i...  11.8 us
    ppermute x4, starting transfers between devices, shifted(): lax.ppermute(x, 'ctx', [(i, i + by) for i in range(peers) if 0 <= i + by...  10.5 us
    pallas_call x1, Pallas kernels, local(): pl.pallas_call(functools.partial(bwd_kernel, offsets, early, per_dev, sca...  9.04 us
    unnamed x63, local copies, waits for them, and re-layouts  8.27 us
  transfers between devices with their start and end apart: 25, of which 10 were waited for; matrix products, arithmetic and copies ran while one was open for 4% of the time, Pallas kernels for 17%

profile of v4, /device:TPU:12, one launch (start us, length us, event | category | flops | bytes accessed | tf_op | source)
XLA Modules:
  0.0 186.3 jit_solution(9759565979805741337)
XLA Ops:
  11.1 2.4 %collective-permute-start.1 = (bf16[2,256,512]{2,1,0:T(8,128)(2,1)S(1)}, bf16[2,256,512]{2,1,0:T(8,128)(2,1)S(1)}, u32[]{:S(2)}, u32[]{:S(2)}) collective-permute-start(bf16[2,256,512]{2,1,0:T(8,128)(2,1)S(1)} %pad_maximum_fusion.1), channel_id=1, source_target_pairs={{8,0},{12,4},{16,8},{20,12},{24,16},{28,20},{9,1},{13,5},{17,9},{2... | collective-permute-start | bytes 1572872 | tf_op jit(solution)/shard_map/ppermute | solution.py:27
  13.5 3.5 %collective-permute-start = (bf16[2,256,512]{2,1,0:T(8,128)(2,1)S(1)}, bf16[2,256,512]{2,1,0:T(8,128)(2,1)S(1)}, u32[]{:S(2)}, u32[]{:S(2)}) collective-permute-start(bf16[2,256,512]{2,1,0:T(8,128)(2,1)S(1)} %pad_maximum_fusion.1), channel_id=1, source_target_pairs={{0,8},{4,12},{8,16},{12,20},{16,24},{20,28},{1,9},{5,13},{9,17},{1... | collective-permute-start | bytes 1572872 | tf_op jit(solution)/shard_map/ppermute | solution.py:27
  17.0 11.9 %collective-permute-done.2.rest_2_ = bf16[3,256,512]{2,1,0:T(8,128)(2,1)S(1)} collective-permute-done((bf16[3,256,512]{2,1,0:T(8,128)(2,1)S(1)}, bf16[3,256,512]{2,1,0:T(8,128)(2,1)S(1)}, u32[]{:S(2)}, u32[]{:S(2)}) %collective-permute-start.2) | collective-permute-done | bytes 786464 | tf_op jit(solution)/shard_map/ppermute | solution.py:62
  30.7 10.4 %collective-permute-start.7 = (bf16[512,512]{1,0:T(8,128)(2,1)S(1)}, bf16[512,512]{1,0:T(8,128)(2,1)}, u32[]{:S(2)}, u32[]{:S(2)}) collective-permute-start(bf16[512,512]{1,0:T(8,128)(2,1)S(1)} %copy-done.8), channel_id=1, source_target_pairs={{0,8},{4,12},{8,0},{12,4},{16,24},{20,28},{24,16},{28,20},{1,9},{5... | collective-permute-start | bytes 1572872 | tf_op jit(solution)/shard_map/ppermute | solution.py:302
  41.1 3.8 %collective-permute-start.8 = (bf16[512,512]{1,0:T(8,128)(2,1)S(1)}, bf16[512,512]{1,0:T(8,128)(2,1)}, u32[]{:S(2)}, u32[]{:S(2)}) collective-permute-start(bf16[512,512]{1,0:T(8,128)(2,1)S(1)} %copy-done.8), channel_id=1, source_target_pairs={{8,16},{12,20},{16,8},{20,12},{9,17},{13,21},{17,9},{21,13},{10,18... | collective-permute-start | bytes 1572872 | tf_op jit(solution)/shard_map/ppermute | solution.py:302
  44.9 6.5 %collective-permute-done.7.rest_1_ = bf16[512,512]{1,0:T(8,128)(2,1)} collective-permute-done((bf16[512,512]{1,0:T(8,128)(2,1)S(1)}, bf16[512,512]{1,0:T(8,128)(2,1)}, u32[]{:S(2)}, u32[]{:S(2)}) %collective-permute-start.7) | collective-permute-done | bytes 524320 | tf_op jit(solution)/shard_map/ppermute | solution.py:302
  51.4 4.0 %collective-permute-start.10 = (bf16[512,512]{1,0:T(8,128)(2,1)}, bf16[512,512]{1,0:T(8,128)(2,1)}, u32[]{:S(2)}, u32[]{:S(2)}) collective-permute-start(bf16[512,512]{1,0:T(8,128)(2,1)} %collective-permute-done.7.rest_1_), channel_id=1, source_target_pairs={{8,16},{12,20},{16,8},{20,12},{9,17},{13,21},{17,9},{21,13},{10,18... | collective-permute-start | bytes 1572872 | tf_op jit(solution)/shard_map/ppermute | solution.py:302
  56.3 1.9 %collective-permute-start.3 = (bf16[2,256,512]{2,1,0:T(8,128)(2,1)}, bf16[2,256,512]{2,1,0:T(8,128)(2,1)}, u32[]{:S(2)}, u32[]{:S(2)}) collective-permute-start(bf16[2,256,512]{2,1,0:T(8,128)(2,1)} %broadcast_select_fusion), channel_id=1, source_target_pairs={{0,4},{8,12},{16,20},{12,8},{20,16},{28,24},{1,5},{9,13},{17,21},{... | collective-permute-start | bytes 1572872 | tf_op jit(solution)/shard_map/ppermute | solution.py:293
  59.5 5.4 %collective-permute-done.10.rest_4_ = bf16[512,512]{1,0:T(8,128)(2,1)} collective-permute-done((bf16[512,512]{1,0:T(8,128)(2,1)}, bf16[512,512]{1,0:T(8,128)(2,1)}, u32[]{:S(2)}, u32[]{:S(2)}) %collective-permute-start.10) | collective-permute-done | bytes 524320 | tf_op jit(solution)/shard_map/ppermute | solution.py:302
  64.9 2.1 %collective-permute-start.11 = (bf16[512,512]{1,0:T(8,128)(2,1)}, bf16[512,512]{1,0:T(8,128)(2,1)}, u32[]{:S(2)}, u32[]{:S(2)}) collective-permute-start(bf16[512,512]{1,0:T(8,128)(2,1)} %collective-permute-done.10.rest_4_), channel_id=1, source_target_pairs={{8,0},{12,4},{16,24},{20,28},{9,1},{13,5},{17,25},{21,29},{10,2},{... | collective-permute-start | bytes 1572872 | tf_op jit(solution)/shard_map/ppermute | solution.py:302
  67.1 2.0 %collective-permute-start.5 = (bf16[2,128,512]{2,1,0:T(8,128)(2,1)S(1)}, bf16[2,128,512]{2,1,0:T(8,128)(2,1)}, u32[]{:S(2)}, u32[]{:S(2)}) collective-permute-start(bf16[2,128,512]{2,1,0:T(8,128)(2,1)S(1)} %fusion.9), channel_id=1, source_target_pairs={{4,28},{0,12},{16,20},{8,24},{5,29},{1,13},{17,21},{9,25},{6,30},{... | collective-permute-start | bytes 786440 | tf_op jit(solution)/shard_map/ppermute | solution.py:298
  69.2 3.1 %collective-permute-done.5 = bf16[2,128,512]{2,1,0:T(8,128)(2,1)} collective-permute-done((bf16[2,128,512]{2,1,0:T(8,128)(2,1)S(1)}, bf16[2,128,512]{2,1,0:T(8,128)(2,1)}, u32[]{:S(2)}, u32[]{:S(2)}) %collective-permute-start.5) | collective-permute-done | bytes 262176 | tf_op jit(solution)/shard_map/ppermute | solution.py:298
  73.4 6.2 %attend.1 = (bf16[256,512]{1,0:T(8,128)(2,1)S(1)}, f32[4,1,256]{2,1,0:T(1,128)S(1)}) custom-call(s32[1]{0:T(128)} %bitcast.run_ref, s32[16,3]{1,0:T(8,128)S(1)} %copy.11.lists_ref, bf16[256,512]{1,0:T(8,128)(2,1)S(1)} %copy-done.22, bf16[256,512]{1,0:T(8,128)(2,1)S(1)} %copy-done.3, bf16[256,512]{1,0:T(8,128)(2,1)S(1)} %copy-done.2, ...), custom_call_target="tpu_custom_call" | custom-call | flops 1 | bytes 1 | tf_op jit(solution)/shard_map/attend/pallas_call | solution.py:335
  79.6 1.8 collective-permute-start.6
  85.9 3.5 %project_grad.1 = (f32[256,512]{1,0:T(8,128)S(1)}, bf16[256,512]{1,0:T(8,128)(2,1)}) custom-call(bf16[512,2048]{1,0:T(8,128)(2,1)S(1)} %copy-done, bf16[512,512]{1,0:T(8,128)(2,1)S(1)} %copy-done.9, bf16[512,512]{1,0:T(8,128)(2,1)} %collective-permute-done.7.rest_1_, bf16[512,512]{1,0:T(8,128)(2,1)} %collective-permute-done.8.rest_2_, ...), custom_call_target="tpu_custom_call" | custom-call | flops 1 | bytes 1 | tf_op jit(solution)/shard_map/project_grad/pallas_call | solution.py:352
  90.5 3.2 %weight_part.1 = (f32[512,512]{1,0:T(8,128)S(1)}, bf16[512,512]{1,0:T(8,128)(2,1)}, bf16[512,512]{1,0:T(8,128)(2,1)S(1)}, bf16[512,512]{1,0:T(8,128)(2,1)}) custom-call(bf16[512,2048]{1,0:T(8,128)(2,1)S(1)} %copy-done.1, bf16[256,512]{1,0:T(8,128)(2,1)S(1)} %get-tuple-element.37.mixed_ref.rest_2_.rest_5_, bf16[256,512]{1,0:T(8,128)(2,1)} %collective-permute-done.6.other_ref), custom_call_target="tpu_custom_call" | custom-call | flops 1 | bytes 1 | tf_op jit(solution)/shard_map/weight_part/pallas_call | solution.py:367
  95.4 5.3 %project_out.1 = bf16[512,2048]{1,0:T(8,128)(2,1)} custom-call(bf16[256,512]{1,0:T(8,128)(2,1)S(1)} %get-tuple-element.37.mixed_ref.rest_2_.rest_5_, bf16[256,512]{1,0:T(8,128)(2,1)} %collective-permute-done.6.other_ref, bf16[512,512]{1,0:T(8,128)(2,1)S(1)} %copy-done.10, bf16[512,512]{1,0:T(8,128)(2,1)} %collective-permute-done.7.rest_1_, ...), custom_call_target="tpu_custom_call" | custom-call | flops 1 | bytes 1 | tf_op jit(solution)/shard_map/project_out/pallas_call | solution.py:378
  100.8 5.3 %collective-permute-start.13 = (bf16[512,512]{1,0:T(8,128)(2,1)}, bf16[512,512]{1,0:T(8,128)(2,1)S(1)}, u32[]{:S(2)}, u32[]{:S(2)}) collective-permute-start(bf16[512,512]{1,0:T(8,128)(2,1)} %get-tuple-element.50), channel_id=1, source_target_pairs={{0,8},{4,12},{8,16},{12,20},{16,24},{20,28},{24,0},{28,4},{1,9},{5... | collective-permute-start | bytes 1572872 | tf_op jit(solution)/shard_map/ppermute | solution.py:58
  107.1 3.8 %first_grad.1 = bf16[2,384,512]{2,1,0:T(8,128)(2,1)S(1)} custom-call(s32[1]{0:T(128)} %bitcast.run_ref, s32[16,3]{1,0:T(8,128)S(1)} %copy.11.lists_ref, bf16[256,512]{1,0:T(8,128)(2,1)S(1)} %copy-done.23, bf16[2,256,512]{2,1,0:T(8,128)(2,1)} %collective-permute-done.3.rest_3_.rest_0_, bf16[2,128,512]{2,1,0:T(8,128)(2,1)S(1)} %copy-done.18, ...), custom_call_target="tpu_custom_call" | custom-call | flops 10000000000 | bytes 1 | tf_op jit(solution)/shard_map/first_grad/pallas_call | solution.py:398
  111.6 9.0 %attend_grad.1 = (bf16[256,512]{1,0:T(8,128)(2,1)}, f32[2,256,512]{2,1,0:T(8,128)S(1)}, bf16[2,256,512]{2,1,0:T(8,128)(2,1)S(1)}, bf16[2,256,512]{2,1,0:T(8,128)(2,1)S(1)}, bf16[2,256,512]{2,1,0:T(8,128)(2,1)S(1)}) custom-call(s32[1]{0:T(128)} %bitcast.run_ref, s32[16,3]{1,0:T(8,128)S(1)} %copy.11.lists_ref, bf16[256,512]{1,0:T(8,128)(2,1)S(1)} %copy-done.23, ...), custom_call_target="tpu_custom_call" | custom-call | flops 30000001024 | bytes 1 | tf_op jit(solution)/shard_map/attend_grad/pallas_call | solution.py:411
  120.7 3.9 %collective-permute-done.13 = bf16[512,512]{1,0:T(8,128)(2,1)S(1)} collective-permute-done((bf16[512,512]{1,0:T(8,128)(2,1)}, bf16[512,512]{1,0:T(8,128)(2,1)S(1)}, u32[]{:S(2)}, u32[]{:S(2)}) %collective-permute-start.13) | collective-permute-done | bytes 524320 | tf_op jit(solution)/shard_map/ppermute | solution.py:58
  124.6 2.2 %collective-permute-done.14 = bf16[512,512]{1,0:T(8,128)(2,1)S(1)} collective-permute-done((bf16[512,512]{1,0:T(8,128)(2,1)}, bf16[512,512]{1,0:T(8,128)(2,1)S(1)}, u32[]{:S(2)}, u32[]{:S(2)}) %collective-permute-start.14) | collective-permute-done | bytes 524320 | tf_op jit(solution)/shard_map/ppermute | solution.py:58
  129.1 2.3 %collective-permute-start.22 = (bf16[512,512]{1,0:T(8,128)(2,1)S(1)}, bf16[512,512]{1,0:T(8,128)(2,1)S(1)}, u32[]{:S(2)}, u32[]{:S(2)}) collective-permute-start(bf16[512,512]{1,0:T(8,128)(2,1)S(1)} %copy-done.25), channel_id=1, source_target_pairs={{0,16},{4,20},{8,24},{12,28},{16,0},{20,4},{24,8},{28,12},{1,17},{... | collective-permute-start | bytes 1572872 | tf_op jit(solution)/shard_map/ppermute | solution.py:58
  133.5 2.7 %collective-permute-start.18 = (bf16[2,256,512]{2,1,0:T(8,128)(2,1)}, bf16[2,256,512]{2,1,0:T(8,128)(2,1)}, u32[]{:S(2)}, u32[]{:S(2)}) collective-permute-start(bf16[2,256,512]{2,1,0:T(8,128)(2,1)} %get-tuple-element.61), channel_id=1, source_target_pairs={{8,0},{12,4},{16,8},{20,12},{24,16},{28,20},{9,1},{13,5},{17,9},{2... | collective-permute-start | bytes 1572872 | tf_op jit(solution)/shard_map/ppermute | solution.py:27
  136.3 6.0 %collective-permute-done.16.a_ref = bf16[2,256,512]{2,1,0:T(8,128)(2,1)S(1)} collective-permute-done((bf16[2,256,512]{2,1,0:T(8,128)(2,1)S(1)}, bf16[2,256,512]{2,1,0:T(8,128)(2,1)S(1)}, u32[]{:S(2)}, u32[]{:S(2)}) %collective-permute-start.16) | collective-permute-done | bytes 524320 | tf_op jit(solution)/shard_map/ppermute | solution.py:62
  142.3 1.9 %collective-permute-start.19 = (bf16[2,256,512]{2,1,0:T(8,128)(2,1)}, bf16[2,256,512]{2,1,0:T(8,128)(2,1)}, u32[]{:S(2)}, u32[]{:S(2)}) collective-permute-start(bf16[2,256,512]{2,1,0:T(8,128)(2,1)} %get-tuple-element.62), channel_id=1, source_target_pairs={{0,8},{4,12},{8,16},{12,20},{16,24},{20,28},{1,9},{5,13},{9,17},{1... | collective-permute-start | bytes 1572872 | tf_op jit(solution)/shard_map/ppermute | solution.py:27
  145.3 6.9 %collective-permute-done.22 = bf16[512,512]{1,0:T(8,128)(2,1)S(1)} collective-permute-done((bf16[512,512]{1,0:T(8,128)(2,1)S(1)}, bf16[512,512]{1,0:T(8,128)(2,1)S(1)}, u32[]{:S(2)}, u32[]{:S(2)}) %collective-permute-start.22) | collective-permute-done | bytes 524320 | tf_op jit(solution)/shard_map/ppermute | solution.py:58
  153.3 2.4 %convert_add_fusion = f32[512,512]{1,0:T(8,128)} fusion(bf16[512,512]{1,0:T(8,128)(2,1)S(1)} %collective-permute-done.22, bf16[512,512]{1,0:T(8,128)(2,1)} %copy-done.28, f32[512,512]{1,0:T(8,128)S(1)} %copy-done.15, bf16[512,512]{1,0:T(8,128)(2,1)} %copy-done.27), kind=kLoop, calls=%fused_computation.7 | loop fusion | flops 1572864 | bytes 3670016 | tf_op jit(solution)/shard_map/add | solution.py:450
  155.8 4.2 %collective-permute-done.17 = bf16[256,512]{1,0:T(8,128)(2,1)S(1)} collective-permute-done((bf16[256,512]{1,0:T(8,128)(2,1)S(1)}, bf16[256,512]{1,0:T(8,128)(2,1)S(1)}, u32[]{:S(2)}, u32[]{:S(2)}) %collective-permute-start.17) | collective-permute-done | bytes 262176 | tf_op jit(solution)/shard_map/ppermute | solution.py:62
  160.9 13.9 %collective-permute-done.18.b_ref = bf16[2,256,512]{2,1,0:T(8,128)(2,1)} collective-permute-done((bf16[2,256,512]{2,1,0:T(8,128)(2,1)}, bf16[2,256,512]{2,1,0:T(8,128)(2,1)}, u32[]{:S(2)}, u32[]{:S(2)}) %collective-permute-start.18) | collective-permute-done | bytes 524320 | tf_op jit(solution)/shard_map/ppermute | solution.py:27
  174.8 2.0 %convert_add_fusion.1.first_ref = f32[2,128,512]{2,1,0:T(8,128)} fusion(bf16[2,128,512]{2,1,0:T(8,128)(2,1)S(1)} %collective-permute-done.21, bf16[2,128,512]{2,1,0:T(8,128)(2,1)} %collective-permute-done.20, bf16[2,384,512]{2,1,0:T(8,128)(2,1)} %copy-done.21, bf16[2,384,512]{2,1,0:T(8,128)(2,1)} %copy-done.26), kind=kLoop, calls=%fused_computation.14 | loop fusion | flops 917504 | bytes 1572864 | tf_op jit(solution)/shard_map/add | solution.py:453
  176.8 2.6 %finish.1 = (bf16[256,512]{1,0:T(8,128)(2,1)}, bf16[256,512]{1,0:T(8,128)(2,1)}) custom-call(s32[1]{0:T(128)} %bitcast.run_ref, f32[2,256,512]{2,1,0:T(8,128)} %copy-done.16, bf16[2,256,512]{2,1,0:T(8,128)(2,1)} %copy-done.29, bf16[2,256,512]{2,1,0:T(8,128)(2,1)} %collective-permute-done.18.b_ref, bf16[2,256,512]{2,1,0:T(8,128)(2,1)} %collective-permute-done.19.c_ref, ...), custom_call_target="tpu_custom_call" | custom-call | flops 1 | bytes 1 | tf_op jit(solution)/shard_map/finish/pallas_call | solution.py:457
  (106 shorter events, 25.6 us)
Async XLA Ops:
  7.2 75.1 %all-gather.2.cloned.1.call-start = ((), (), s32[]{:S(2)}) async-start(), calls=%async_computation.1 | async-start | bytes 2621440 | tf_op jit(solution)/shard_map/all_gather | solution.py:290
  9.5 21.2 %copy-start.8 = (bf16[512,512]{1,0:T(8,128)(2,1)S(1)}, bf16[512,512]{1,0:T(8,128)(2,1)}, u32[]{:S(2)}) copy-start(bf16[512,512]{1,0:T(8,128)(2,1)} %rest_0_.1) | copy-start | bytes 1572868
  9.5 19.3 %collective-permute-start.2 = (bf16[3,256,512]{2,1,0:T(8,128)(2,1)S(1)}, bf16[3,256,512]{2,1,0:T(8,128)(2,1)S(1)}, u32[]{:S(2)}, u32[]{:S(2)}) collective-permute-start(bf16[3,256,512]{2,1,0:T(8,128)(2,1)S(1)} %pad_maximum_fusion), channel_id=1, source_target_pairs={{0,4},{4,0},{8,12},{12,8},{16,20},{20,16},{24,28},{28,24},{1,5},{5... | collective-permute-start | bytes 2359304 | tf_op jit(solution)/shard_map/ppermute | solution.py:62
  11.1 17.8 %collective-permute-start.1 = (bf16[2,256,512]{2,1,0:T(8,128)(2,1)S(1)}, bf16[2,256,512]{2,1,0:T(8,128)(2,1)S(1)}, u32[]{:S(2)}, u32[]{:S(2)}) collective-permute-start(bf16[2,256,512]{2,1,0:T(8,128)(2,1)S(1)} %pad_maximum_fusion.1), channel_id=1, source_target_pairs={{8,0},{12,4},{16,8},{20,12},{24,16},{28,20},{9,1},{13,5},{17,9},{2... | collective-permute-start | bytes 1572872 | tf_op jit(solution)/shard_map/ppermute | solution.py:27
  13.5 15.4 %collective-permute-start = (bf16[2,256,512]{2,1,0:T(8,128)(2,1)S(1)}, bf16[2,256,512]{2,1,0:T(8,128)(2,1)S(1)}, u32[]{:S(2)}, u32[]{:S(2)}) collective-permute-start(bf16[2,256,512]{2,1,0:T(8,128)(2,1)S(1)} %pad_maximum_fusion.1), channel_id=1, source_target_pairs={{0,8},{4,12},{8,16},{12,20},{16,24},{20,28},{1,9},{5,13},{9,17},{1... | collective-permute-start | bytes 1572872 | tf_op jit(solution)/shard_map/ppermute | solution.py:27
  28.9 43.5 %copy-start.4 = (bf16[3,256,512]{2,1,0:T(8,128)(2,1)}, bf16[3,256,512]{2,1,0:T(8,128)(2,1)S(1)}, u32[]{:S(2)}) copy-start(bf16[3,256,512]{2,1,0:T(8,128)(2,1)S(1)} %collective-permute-done.2.rest_2_) | copy-start | bytes 2359300
  28.9 43.5 %copy-start.6 = (bf16[2,256,512]{2,1,0:T(8,128)(2,1)}, bf16[2,256,512]{2,1,0:T(8,128)(2,1)S(1)}, u32[]{:S(2)}) copy-start(bf16[2,256,512]{2,1,0:T(8,128)(2,1)S(1)} %collective-permute-done.1.rest_1_) | copy-start | bytes 1572868
  29.9 39.2 %copy-start.30 = (s32[16,3]{0,1:T(4,128)S(1)}, s32[16,3]{0,1:T(4,128)}, u32[]{:S(2)}) copy-start(s32[16,3]{0,1:T(4,128)} %param.10) | copy-start | bytes 580
  29.9 114.3 %reduce-scatter.2.cloned.1.call-start = ((), (), s32[]{:S(2)}) async-start(), calls=%async_computation.2 | async-start | bytes 2621440 | tf_op jit(solution)/shard_map/reduce_scatter | solution.py:388
  30.0 0.7 collective-permute-start.4
  30.7 20.7 %collective-permute-start.7 = (bf16[512,512]{1,0:T(8,128)(2,1)S(1)}, bf16[512,512]{1,0:T(8,128)(2,1)}, u32[]{:S(2)}, u32[]{:S(2)}) collective-permute-start(bf16[512,512]{1,0:T(8,128)(2,1)S(1)} %copy-done.8), channel_id=1, source_target_pairs={{0,8},{4,12},{8,0},{12,4},{16,24},{20,28},{24,16},{28,20},{1,9},{5... | collective-permute-start | bytes 1572872 | tf_op jit(solution)/shard_map/ppermute | solution.py:302
  41.1 17.1 %collective-permute-start.8 = (bf16[512,512]{1,0:T(8,128)(2,1)S(1)}, bf16[512,512]{1,0:T(8,128)(2,1)}, u32[]{:S(2)}, u32[]{:S(2)}) collective-permute-start(bf16[512,512]{1,0:T(8,128)(2,1)S(1)} %copy-done.8), channel_id=1, source_target_pairs={{8,16},{12,20},{16,8},{20,12},{9,17},{13,21},{17,9},{21,13},{10,18... | collective-permute-start | bytes 1572872 | tf_op jit(solution)/shard_map/ppermute | solution.py:302
  51.4 13.5 %collective-permute-start.10 = (bf16[512,512]{1,0:T(8,128)(2,1)}, bf16[512,512]{1,0:T(8,128)(2,1)}, u32[]{:S(2)}, u32[]{:S(2)}) collective-permute-start(bf16[512,512]{1,0:T(8,128)(2,1)} %collective-permute-done.7.rest_1_), channel_id=1, source_target_pairs={{8,16},{12,20},{16,8},{20,12},{9,17},{13,21},{17,9},{21,13},{10,18... | collective-permute-start | bytes 1572872 | tf_op jit(solution)/shard_map/ppermute | solution.py:302
  56.3 16.1 %collective-permute-start.3 = (bf16[2,256,512]{2,1,0:T(8,128)(2,1)}, bf16[2,256,512]{2,1,0:T(8,128)(2,1)}, u32[]{:S(2)}, u32[]{:S(2)}) collective-permute-start(bf16[2,256,512]{2,1,0:T(8,128)(2,1)} %broadcast_select_fusion), channel_id=1, source_target_pairs={{0,4},{8,12},{16,20},{12,8},{20,16},{28,24},{1,5},{9,13},{17,21},{... | collective-permute-start | bytes 1572872 | tf_op jit(solution)/shard_map/ppermute | solution.py:293
  58.2 23.2 %collective-permute-start.9 = (bf16[512,512]{1,0:T(8,128)(2,1)}, bf16[512,512]{1,0:T(8,128)(2,1)S(1)}, u32[]{:S(2)}, u32[]{:S(2)}) collective-permute-start(bf16[512,512]{1,0:T(8,128)(2,1)} %collective-permute-done.8.rest_2_), channel_id=1, source_target_pairs={{8,0},{12,4},{16,24},{20,28},{9,1},{13,5},{17,25},{21,29},{10,2},{... | collective-permute-start | bytes 1572872 | tf_op jit(solution)/shard_map/ppermute | solution.py:302
  64.9 17.3 %collective-permute-start.11 = (bf16[512,512]{1,0:T(8,128)(2,1)}, bf16[512,512]{1,0:T(8,128)(2,1)}, u32[]{:S(2)}, u32[]{:S(2)}) collective-permute-start(bf16[512,512]{1,0:T(8,128)(2,1)} %collective-permute-done.10.rest_4_), channel_id=1, source_target_pairs={{8,0},{12,4},{16,24},{20,28},{9,1},{13,5},{17,25},{21,29},{10,2},{... | collective-permute-start | bytes 1572872 | tf_op jit(solution)/shard_map/ppermute | solution.py:302
  67.1 5.2 %collective-permute-start.5 = (bf16[2,128,512]{2,1,0:T(8,128)(2,1)S(1)}, bf16[2,128,512]{2,1,0:T(8,128)(2,1)}, u32[]{:S(2)}, u32[]{:S(2)}) collective-permute-start(bf16[2,128,512]{2,1,0:T(8,128)(2,1)S(1)} %fusion.9), channel_id=1, source_target_pairs={{4,28},{0,12},{16,20},{8,24},{5,29},{1,13},{17,21},{9,25},{6,30},{... | collective-permute-start | bytes 786440 | tf_op jit(solution)/shard_map/ppermute | solution.py:298
  79.6 10.9 %collective-permute-start.6 = (bf16[256,512]{1,0:T(8,128)(2,1)S(1)}, bf16[256,512]{1,0:T(8,128)(2,1)}, u32[]{:S(2)}, u32[]{:S(2)}) collective-permute-start(bf16[256,512]{1,0:T(8,128)(2,1)S(1)} %get-tuple-element.37.mixed_ref.rest_2_.rest_5_), channel_id=1, source_target_pairs={{0,4},{4,0},{8,12},{12,8},{16,20},{20,16},{24,28},{28,24},{1,5},{5... | collective-permute-start | bytes 786440 | tf_op jit(solution)/shard_map/ppermute | solution.py:62
  90.2 15.8 %collective-permute-start.12 = (bf16[256,512]{1,0:T(8,128)(2,1)}, bf16[256,512]{1,0:T(8,128)(2,1)}, u32[]{:S(2)}, u32[]{:S(2)}) collective-permute-start(bf16[256,512]{1,0:T(8,128)(2,1)} %get-tuple-element.40), channel_id=1, source_target_pairs={{0,4},{4,0},{8,12},{12,8},{16,20},{20,16},{24,28},{28,24},{1,5},{5... | collective-permute-start | bytes 786440 | tf_op jit(solution)/shard_map/ppermute | solution.py:62
  100.8 23.9 %collective-permute-start.13 = (bf16[512,512]{1,0:T(8,128)(2,1)}, bf16[512,512]{1,0:T(8,128)(2,1)S(1)}, u32[]{:S(2)}, u32[]{:S(2)}) collective-permute-start(bf16[512,512]{1,0:T(8,128)(2,1)} %get-tuple-element.50), channel_id=1, source_target_pairs={{0,8},{4,12},{8,16},{12,20},{16,24},{20,28},{24,0},{28,4},{1,9},{5... | collective-permute-start | bytes 1572872 | tf_op jit(solution)/shard_map/ppermute | solution.py:58
  106.1 20.8 %collective-permute-start.14 = (bf16[512,512]{1,0:T(8,128)(2,1)}, bf16[512,512]{1,0:T(8,128)(2,1)S(1)}, u32[]{:S(2)}, u32[]{:S(2)}) collective-permute-start(bf16[512,512]{1,0:T(8,128)(2,1)} %get-tuple-element.51), channel_id=1, source_target_pairs={{0,24},{4,28},{8,0},{12,4},{16,8},{20,12},{24,16},{28,20},{1,25},{... | collective-permute-start | bytes 1572872 | tf_op jit(solution)/shard_map/ppermute | solution.py:58
  111.0 15.9 %copy-start.21 = (bf16[2,384,512]{2,1,0:T(8,128)(2,1)}, bf16[2,384,512]{2,1,0:T(8,128)(2,1)S(1)}, u32[]{:S(2)}) copy-start(bf16[2,384,512]{2,1,0:T(8,128)(2,1)S(1)} %first_grad.1) | copy-start | bytes 2359300
  111.0 15.9 %collective-permute-start.15 = (bf16[2,384,512]{2,1,0:T(8,128)(2,1)S(1)}, bf16[2,384,512]{2,1,0:T(8,128)(2,1)S(1)}, u32[]{:S(2)}, u32[]{:S(2)}) collective-permute-start(bf16[2,384,512]{2,1,0:T(8,128)(2,1)S(1)} %first_grad.1), channel_id=1, source_target_pairs={{0,4},{4,0},{8,12},{12,8},{16,20},{20,16},{24,28},{28,24},{1,5},{5... | collective-permute-start | bytes 2359304 | tf_op jit(solution)/shard_map/ppermute | solution.py:62
  124.6 17.6 %copy-start.27 = (bf16[512,512]{1,0:T(8,128)(2,1)}, bf16[512,512]{1,0:T(8,128)(2,1)S(1)}, u32[]{:S(2)}) copy-start(bf16[512,512]{1,0:T(8,128)(2,1)S(1)} %collective-permute-done.13) | copy-start | bytes 1572868
  127.0 26.4 %copy-start.15 = (f32[512,512]{1,0:T(8,128)S(1)}, f32[512,512]{1,0:T(8,128)}, u32[]{:S(2)}) copy-start(f32[512,512]{1,0:T(8,128)} %copy-done.14) | copy-start | bytes 3145732
  128.3 14.0 %collective-permute-start.16 = (bf16[2,256,512]{2,1,0:T(8,128)(2,1)S(1)}, bf16[2,256,512]{2,1,0:T(8,128)(2,1)S(1)}, u32[]{:S(2)}, u32[]{:S(2)}) collective-permute-start(bf16[2,256,512]{2,1,0:T(8,128)(2,1)S(1)} %get-tuple-element.58), channel_id=1, source_target_pairs={{0,4},{4,0},{8,12},{12,8},{16,20},{20,16},{24,28},{28,24},{1,5},{5... | collective-permute-start | bytes 1572872 | tf_op jit(solution)/shard_map/ppermute | solution.py:62
  129.1 23.0 %collective-permute-start.22 = (bf16[512,512]{1,0:T(8,128)(2,1)S(1)}, bf16[512,512]{1,0:T(8,128)(2,1)S(1)}, u32[]{:S(2)}, u32[]{:S(2)}) collective-permute-start(bf16[512,512]{1,0:T(8,128)(2,1)S(1)} %copy-done.25), channel_id=1, source_target_pairs={{0,16},{4,20},{8,24},{12,28},{16,0},{20,4},{24,8},{28,12},{1,17},{... | collective-permute-start | bytes 1572872 | tf_op jit(solution)/shard_map/ppermute | solution.py:58
  131.5 29.4 %collective-permute-start.21 = (bf16[2,128,512]{2,1,0:T(8,128)(2,1)S(1)}, bf16[2,128,512]{2,1,0:T(8,128)(2,1)S(1)}, u32[]{:S(2)}, u32[]{:S(2)}) collective-permute-start(bf16[2,128,512]{2,1,0:T(8,128)(2,1)S(1)} %get-tuple-element.63), channel_id=1, source_target_pairs={{24,0},{25,1},{26,2},{27,3}} | collective-permute-start | bytes 786440 | tf_op jit(solution)/shard_map/ppermute | solution.py:452
  132.2 42.6 %collective-permute-start.20 = (bf16[2,128,512]{2,1,0:T(8,128)(2,1)S(1)}, bf16[2,128,512]{2,1,0:T(8,128)(2,1)}, u32[]{:S(2)}, u32[]{:S(2)}) collective-permute-start(bf16[2,128,512]{2,1,0:T(8,128)(2,1)S(1)} %get-tuple-element.63), channel_id=1, source_target_pairs={{16,0},{17,1},{18,2},{19,3}} | collective-permute-start | bytes 786440 | tf_op jit(solution)/shard_map/ppermute | solution.py:452
  133.5 41.2 %collective-permute-start.18 = (bf16[2,256,512]{2,1,0:T(8,128)(2,1)}, bf16[2,256,512]{2,1,0:T(8,128)(2,1)}, u32[]{:S(2)}, u32[]{:S(2)}) collective-permute-start(bf16[2,256,512]{2,1,0:T(8,128)(2,1)} %get-tuple-element.61), channel_id=1, source_target_pairs={{8,0},{12,4},{16,8},{20,12},{24,16},{28,20},{9,1},{13,5},{17,9},{2... | collective-permute-start | bytes 1572872 | tf_op jit(solution)/shard_map/ppermute | solution.py:27
  142.3 32.5 %collective-permute-start.19 = (bf16[2,256,512]{2,1,0:T(8,128)(2,1)}, bf16[2,256,512]{2,1,0:T(8,128)(2,1)}, u32[]{:S(2)}, u32[]{:S(2)}) collective-permute-start(bf16[2,256,512]{2,1,0:T(8,128)(2,1)} %get-tuple-element.62), channel_id=1, source_target_pairs={{0,8},{4,12},{8,16},{12,20},{16,24},{20,28},{1,9},{5,13},{9,17},{1... | collective-permute-start | bytes 1572872 | tf_op jit(solution)/shard_map/ppermute | solution.py:27
  152.2 7.8 %collective-permute-start.17 = (bf16[256,512]{1,0:T(8,128)(2,1)S(1)}, bf16[256,512]{1,0:T(8,128)(2,1)S(1)}, u32[]{:S(2)}, u32[]{:S(2)}) collective-permute-start(bf16[256,512]{1,0:T(8,128)(2,1)S(1)} %get-tuple-element.74), channel_id=1, source_target_pairs={{0,4},{4,0},{8,12},{12,8},{16,20},{20,16},{24,28},{28,24},{1,5},{5... | collective-permute-start | bytes 786440 | tf_op jit(solution)/shard_map/ppermute | solution.py:62
  (24 other events, 107.8 us)
Sparse Core Ops, SparseCore 0:
  30.0 22.7 all-gather.1
  100.9 34.9 reduce-scatter.1

commit v5 on v2

--- a/solution.py
+++ b/solution.py
@@ -301,9 +301,10 @@
         def between(x, places):
             return lax.ppermute(x, "ctx", [(2 * a + n, 2 * b + n) for a, b in places for n in range(2)])
 
-        base = tied(out_weight, before, after, middle_rows)
+        base = tied(out_weight, before, after)
         near = between(base, ((0, 1), (1, 0), (2, 3), (3, 2)))
         middle = between(base, ((1, 2), (2, 1)))
+        near, middle, _ = lax.optimization_barrier((near, middle, middle_rows))
         far = between(near, ((1, 2), (2, 1)))
         outer = between(middle, ((1, 0), (2, 3)))
         farthest = between(far, ((1, 0), (2, 3)))

time: 187 us -> 194 us (1.037)
  waiting for transfers between devices: 59.6 us -> 72.6 us
  starting transfers between devices: 56.7 us -> 46.5 us
  local copies, waits for them, and re-layouts: 10.5 us -> 13.3 us
  other arithmetic: 10.9 us -> 13.2 us
    ppermute x5, waiting for transfers between devices: 11.8 us -> 19.4 us  [between(): lax.ppermute(x, 'ctx', [(2 * a + n, 2 * b + n) for a, b in places for n i...]
    ppermute x5, starting transfers between devices: 21.7 us -> 15 us  [between(): lax.ppermute(x, 'ctx', [(2 * a + n, 2 * b + n) for a, b in places for n i...]
    ppermute x3, starting transfers between devices: 8.72 us -> 4.24 us  [turned(): lax.ppermute(x, 'ctx', [(2 * z + n, 2 * ((z + by) % length) + n) for z in...]
    ppermute x4, waiting for transfers between devices: 12.8 us -> 16.9 us  [shifted(): lax.ppermute(x, 'ctx', [(i, i + by) for i in range(peers) if 0 <= i + by...]
    ppermute x3, waiting for transfers between devices: 11.9 us -> 15.4 us  [turned(): lax.ppermute(x, 'ctx', [(2 * z + n, 2 * ((z + by) % length) + n) for z in...]
    unnamed x63 -> x73, local copies, waits for them, and re-layouts: 8.27 us -> 11.1 us
    ppermute x6, waiting for transfers between devices: 19.9 us -> 17.5 us  [swapped(): lax.ppermute(piece, 'ctx', [(2 * z + n, 2 * z + 1 - n) for z in places fo...]
  transfers between devices with their start and end apart: 25 -> 25, of which waited for: 10 -> 11; matrix products, arithmetic and copies ran while one was open for 4% -> 5% of each run, Pallas kernels for 17% -> 16%
where the time goes in v5:
time: 194 us; the launch traced here: 193 us
  waiting for transfers between devices  72.6 us (37%)
  starting transfers between devices  46.5 us (24%)
  Pallas kernels  33.2 us (17%)
  between operations  14.5 us (7%)
  local copies, waits for them, and re-layouts  13.3 us (7%)
  other arithmetic  13.2 us (7%)
    ppermute x5, waiting for transfers between devices, between(): lax.ppermute(x, 'ctx', [(2 * a + n, 2 * b + n) for a, b in places for n i...  19.4 us
    ppermute x6, waiting for transfers between devices, swapped(): lax.ppermute(piece, 'ctx', [(2 * z + n, 2 * z + 1 - n) for z in places fo...  17.5 us
    ppermute x4, waiting for transfers between devices, shifted(): lax.ppermute(x, 'ctx', [(i, i + by) for i in range(peers) if 0 <= i + by...  16.9 us
    ppermute x3, waiting for transfers between devices, turned(): lax.ppermute(x, 'ctx', [(2 * z + n, 2 * ((z + by) % length) + n) for z in...  15.4 us
    ppermute x5, starting transfers between devices, between(): lax.ppermute(x, 'ctx', [(2 * a + n, 2 * b + n) for a, b in places for n i...  15 us
    ppermute x4, starting transfers between devices, shifted(): lax.ppermute(x, 'ctx', [(i, i + by) for i in range(peers) if 0 <= i + by...  12.7 us
    unnamed x73, local copies, waits for them, and re-layouts  11.1 us
    pallas_call x1, Pallas kernels, local(): pl.pallas_call(functools.partial(bwd_kernel, offsets, early, per_dev, sca...  9.09 us
  transfers between devices with their start and end apart: 25, of which 11 were waited for; matrix products, arithmetic and copies ran while one was open for 5% of the time, Pallas kernels for 16%

profile of v5, /device:TPU:12, one launch (start us, length us, event | category | flops | bytes accessed | tf_op | source)
XLA Modules:
  0.0 193.2 jit_solution(5168912241926653204)
XLA Ops:
  11.2 2.4 %collective-permute-start.1 = (bf16[2,256,512]{2,1,0:T(8,128)(2,1)S(1)}, bf16[2,256,512]{2,1,0:T(8,128)(2,1)S(1)}, u32[]{:S(2)}, u32[]{:S(2)}) collective-permute-start(bf16[2,256,512]{2,1,0:T(8,128)(2,1)S(1)} %pad_maximum_fusion.1), channel_id=1, source_target_pairs={{8,0},{12,4},{16,8},{20,12},{24,16},{28,20},{9,1},{13,5},{17,9},{2... | collective-permute-start | bytes 1572872 | tf_op jit(solution)/shard_map/ppermute | solution.py:27
  13.6 3.5 %collective-permute-start = (bf16[2,256,512]{2,1,0:T(8,128)(2,1)S(1)}, bf16[2,256,512]{2,1,0:T(8,128)(2,1)S(1)}, u32[]{:S(2)}, u32[]{:S(2)}) collective-permute-start(bf16[2,256,512]{2,1,0:T(8,128)(2,1)S(1)} %pad_maximum_fusion.1), channel_id=1, source_target_pairs={{0,8},{4,12},{8,16},{12,20},{16,24},{20,28},{1,9},{5,13},{9,17},{1... | collective-permute-start | bytes 1572872 | tf_op jit(solution)/shard_map/ppermute | solution.py:27
  17.1 11.9 %collective-permute-done.2.rest_2_ = bf16[3,256,512]{2,1,0:T(8,128)(2,1)S(1)} collective-permute-done((bf16[3,256,512]{2,1,0:T(8,128)(2,1)S(1)}, bf16[3,256,512]{2,1,0:T(8,128)(2,1)S(1)}, u32[]{:S(2)}, u32[]{:S(2)}) %collective-permute-start.2) | collective-permute-done | bytes 786464 | tf_op jit(solution)/shard_map/ppermute | solution.py:62
  30.0 3.5 %collective-permute-start.8 = (bf16[512,512]{1,0:T(8,128)(2,1)S(1)}, bf16[512,512]{1,0:T(8,128)(2,1)S(1)}, u32[]{:S(2)}, u32[]{:S(2)}) collective-permute-start(bf16[512,512]{1,0:T(8,128)(2,1)S(1)} %copy-done.8), channel_id=1, source_target_pairs={{8,16},{12,20},{16,8},{20,12},{9,17},{13,21},{17,9},{21,13},{10,18... | collective-permute-start | bytes 1572872 | tf_op jit(solution)/shard_map/ppermute | solution.py:302
  34.3 10.4 %collective-permute-done.8.rest_2_ = bf16[512,512]{1,0:T(8,128)(2,1)S(1)} collective-permute-done((bf16[512,512]{1,0:T(8,128)(2,1)S(1)}, bf16[512,512]{1,0:T(8,128)(2,1)S(1)}, u32[]{:S(2)}, u32[]{:S(2)}) %collective-permute-start.8) | collective-permute-done | bytes 524320 | tf_op jit(solution)/shard_map/ppermute | solution.py:302
  44.7 3.8 %collective-permute-done.7.rest_1_ = bf16[512,512]{1,0:T(8,128)(2,1)} collective-permute-done((bf16[512,512]{1,0:T(8,128)(2,1)S(1)}, bf16[512,512]{1,0:T(8,128)(2,1)}, u32[]{:S(2)}, u32[]{:S(2)}) %collective-permute-start.7) | collective-permute-done | bytes 524320 | tf_op jit(solution)/shard_map/ppermute | solution.py:302
  48.5 7.2 %collective-permute-start.10 = (bf16[512,512]{1,0:T(8,128)(2,1)}, bf16[512,512]{1,0:T(8,128)(2,1)S(1)}, u32[]{:S(2)}, u32[]{:S(2)}) collective-permute-start(bf16[512,512]{1,0:T(8,128)(2,1)} %collective-permute-done.7.rest_1_), channel_id=1, source_target_pairs={{8,16},{12,20},{16,8},{20,12},{9,17},{13,21},{17,9},{21,13},{10,18... | collective-permute-start | bytes 1572872 | tf_op jit(solution)/shard_map/ppermute | solution.py:302
  56.6 1.9 collective-permute-start.3
  58.6 2.1 %collective-permute-start.9 = (bf16[512,512]{1,0:T(8,128)(2,1)S(1)}, bf16[512,512]{1,0:T(8,128)(2,1)}, u32[]{:S(2)}, u32[]{:S(2)}) collective-permute-start(bf16[512,512]{1,0:T(8,128)(2,1)S(1)} %collective-permute-done.8.rest_2_), channel_id=1, source_target_pairs={{8,0},{12,4},{16,24},{20,28},{9,1},{13,5},{17,25},{21,29},{10,2},{... | collective-permute-start | bytes 1572872 | tf_op jit(solution)/shard_map/ppermute | solution.py:302
  60.7 5.2 %collective-permute-done.10.rest_4_ = bf16[512,512]{1,0:T(8,128)(2,1)S(1)} collective-permute-done((bf16[512,512]{1,0:T(8,128)(2,1)}, bf16[512,512]{1,0:T(8,128)(2,1)S(1)}, u32[]{:S(2)}, u32[]{:S(2)}) %collective-permute-start.10) | collective-permute-done | bytes 524320 | tf_op jit(solution)/shard_map/ppermute | solution.py:302
  65.8 2.1 %collective-permute-start.11 = (bf16[512,512]{1,0:T(8,128)(2,1)S(1)}, bf16[512,512]{1,0:T(8,128)(2,1)}, u32[]{:S(2)}, u32[]{:S(2)}) collective-permute-start(bf16[512,512]{1,0:T(8,128)(2,1)S(1)} %collective-permute-done.10.rest_4_), channel_id=1, source_target_pairs={{8,0},{12,4},{16,24},{20,28},{9,1},{13,5},{17,25},{21,29},{10,2},{... | collective-permute-start | bytes 1572872 | tf_op jit(solution)/shard_map/ppermute | solution.py:302
  68.7 2.0 %collective-permute-start.5 = (bf16[2,128,512]{2,1,0:T(8,128)(2,1)}, bf16[2,128,512]{2,1,0:T(8,128)(2,1)}, u32[]{:S(2)}, u32[]{:S(2)}) collective-permute-start(bf16[2,128,512]{2,1,0:T(8,128)(2,1)} %fusion.9), channel_id=1, source_target_pairs={{4,28},{0,12},{16,20},{8,24},{5,29},{1,13},{17,21},{9,25},{6,30},{... | collective-permute-start | bytes 786440 | tf_op jit(solution)/shard_map/ppermute | solution.py:298
  70.7 3.5 %collective-permute-done.5 = bf16[2,128,512]{2,1,0:T(8,128)(2,1)} collective-permute-done((bf16[2,128,512]{2,1,0:T(8,128)(2,1)}, bf16[2,128,512]{2,1,0:T(8,128)(2,1)}, u32[]{:S(2)}, u32[]{:S(2)}) %collective-permute-start.5) | collective-permute-done | bytes 262176 | tf_op jit(solution)/shard_map/ppermute | solution.py:298
  76.2 6.8 %attend.1 = (bf16[256,512]{1,0:T(8,128)(2,1)}, f32[4,1,256]{2,1,0:T(1,128)S(1)}) custom-call(s32[1]{0:T(128)} %bitcast.run_ref, s32[16,3]{1,0:T(8,128)S(1)} %copy.11.lists_ref, bf16[256,512]{1,0:T(8,128)(2,1)S(1)} %copy-done.24, bf16[256,512]{1,0:T(8,128)(2,1)S(1)} %copy-done.3, bf16[256,512]{1,0:T(8,128)(2,1)S(1)} %copy-done.2, ...), custom_call_target="tpu_custom_call" | custom-call | flops 1 | bytes 1 | tf_op jit(solution)/shard_map/attend/pallas_call | solution.py:336
  83.0 3.2 %collective-permute-start.6 = (bf16[256,512]{1,0:T(8,128)(2,1)}, bf16[256,512]{1,0:T(8,128)(2,1)}, u32[]{:S(2)}, u32[]{:S(2)}) collective-permute-start(bf16[256,512]{1,0:T(8,128)(2,1)} %get-tuple-element.38.mixed_ref.rest_2_.rest_5_), channel_id=1, source_target_pairs={{0,4},{4,0},{8,12},{12,8},{16,20},{20,16},{24,28},{28,24},{1,5},{5... | collective-permute-start | bytes 786440 | tf_op jit(solution)/shard_map/ppermute | solution.py:62
  91.0 2.8 %project_grad.1 = (f32[256,512]{1,0:T(8,128)S(1)}, bf16[256,512]{1,0:T(8,128)(2,1)S(1)}) custom-call(bf16[512,2048]{1,0:T(8,128)(2,1)S(1)} %copy-done, bf16[512,512]{1,0:T(8,128)(2,1)S(1)} %copy-done.9, bf16[512,512]{1,0:T(8,128)(2,1)} %collective-permute-done.7.rest_1_, bf16[512,512]{1,0:T(8,128)(2,1)S(1)} %copy-done.12, ...), custom_call_target="tpu_custom_call" | custom-call | flops 1 | bytes 1 | tf_op jit(solution)/shard_map/project_grad/pallas_call | solution.py:353
  94.6 2.7 %weight_part.1 = (f32[512,512]{1,0:T(8,128)S(1)}, bf16[512,512]{1,0:T(8,128)(2,1)}, bf16[512,512]{1,0:T(8,128)(2,1)S(1)}, bf16[512,512]{1,0:T(8,128)(2,1)S(1)}) custom-call(bf16[512,2048]{1,0:T(8,128)(2,1)S(1)} %copy-done.1, bf16[256,512]{1,0:T(8,128)(2,1)} %get-tuple-element.38.mixed_ref.rest_2_.rest_5_, bf16[256,512]{1,0:T(8,128)(2,1)} %collective-permute-done.6.other_ref), custom_call_target="tpu_custom_call" | custom-call | flops 1 | bytes 1 | tf_op jit(solution)/shard_map/weight_part/pallas_call | solution.py:368
  100.0 5.4 %project_out.1 = bf16[512,2048]{1,0:T(8,128)(2,1)} custom-call(bf16[256,512]{1,0:T(8,128)(2,1)} %get-tuple-element.38.mixed_ref.rest_2_.rest_5_, bf16[256,512]{1,0:T(8,128)(2,1)} %collective-permute-done.6.other_ref, bf16[512,512]{1,0:T(8,128)(2,1)S(1)} %copy-done.10, bf16[512,512]{1,0:T(8,128)(2,1)} %collective-permute-done.7.rest_1_, ...), custom_call_target="tpu_custom_call" | custom-call | flops 1 | bytes 1 | tf_op jit(solution)/shard_map/project_out/pallas_call | solution.py:379
  108.6 3.8 %first_grad.1 = bf16[2,384,512]{2,1,0:T(8,128)(2,1)S(1)} custom-call(s32[1]{0:T(128)} %bitcast.run_ref, s32[16,3]{1,0:T(8,128)S(1)} %copy.11.lists_ref, bf16[256,512]{1,0:T(8,128)(2,1)S(1)} %copy-done.25, bf16[2,256,512]{2,1,0:T(8,128)(2,1)} %collective-permute-done.3.rest_3_.rest_0_, bf16[2,128,512]{2,1,0:T(8,128)(2,1)S(1)} %copy-done.21, ...), custom_call_target="tpu_custom_call" | custom-call | flops 10000000000 | bytes 1 | tf_op jit(solution)/shard_map/first_grad/pallas_call | solution.py:399
  112.4 2.1 %collective-permute-start.17 = (bf16[2,384,512]{2,1,0:T(8,128)(2,1)S(1)}, bf16[2,384,512]{2,1,0:T(8,128)(2,1)S(1)}, u32[]{:S(2)}, u32[]{:S(2)}) collective-permute-start(bf16[2,384,512]{2,1,0:T(8,128)(2,1)S(1)} %first_grad.1), channel_id=1, source_target_pairs={{0,4},{4,0},{8,12},{12,8},{16,20},{20,16},{24,28},{28,24},{1,5},{5... | collective-permute-start | bytes 2359304 | tf_op jit(solution)/shard_map/ppermute | solution.py:62
  114.5 9.1 %attend_grad.1 = (bf16[256,512]{1,0:T(8,128)(2,1)}, f32[2,256,512]{2,1,0:T(8,128)S(1)}, bf16[2,256,512]{2,1,0:T(8,128)(2,1)S(1)}, bf16[2,256,512]{2,1,0:T(8,128)(2,1)S(1)}, bf16[2,256,512]{2,1,0:T(8,128)(2,1)S(1)}) custom-call(s32[1]{0:T(128)} %bitcast.run_ref, s32[16,3]{1,0:T(8,128)S(1)} %copy.11.lists_ref, bf16[256,512]{1,0:T(8,128)(2,1)S(1)} %copy-done.25, ...), custom_call_target="tpu_custom_call" | custom-call | flops 30000001024 | bytes 1 | tf_op jit(solution)/shard_map/attend_grad/pallas_call | solution.py:412
  123.6 2.4 %collective-permute-done.15 = bf16[512,512]{1,0:T(8,128)(2,1)S(1)} collective-permute-done((bf16[512,512]{1,0:T(8,128)(2,1)}, bf16[512,512]{1,0:T(8,128)(2,1)S(1)}, u32[]{:S(2)}, u32[]{:S(2)}) %collective-permute-start.15) | collective-permute-done | bytes 524320 | tf_op jit(solution)/shard_map/ppermute | solution.py:58
  126.0 5.3 %collective-permute-done.16 = bf16[512,512]{1,0:T(8,128)(2,1)S(1)} collective-permute-done((bf16[512,512]{1,0:T(8,128)(2,1)S(1)}, bf16[512,512]{1,0:T(8,128)(2,1)S(1)}, u32[]{:S(2)}, u32[]{:S(2)}) %collective-permute-start.16) | collective-permute-done | bytes 524320 | tf_op jit(solution)/shard_map/ppermute | solution.py:58
  134.8 3.1 %collective-permute-start.22 = (bf16[512,512]{1,0:T(8,128)(2,1)S(1)}, bf16[512,512]{1,0:T(8,128)(2,1)S(1)}, u32[]{:S(2)}, u32[]{:S(2)}) collective-permute-start(bf16[512,512]{1,0:T(8,128)(2,1)S(1)} %copy-done.27), channel_id=1, source_target_pairs={{0,16},{4,20},{8,24},{12,28},{16,0},{20,4},{24,8},{28,12},{1,17},{... | collective-permute-start | bytes 1572872 | tf_op jit(solution)/shard_map/ppermute | solution.py:58
  140.6 2.2 %collective-permute-start.18 = (bf16[2,256,512]{2,1,0:T(8,128)(2,1)}, bf16[2,256,512]{2,1,0:T(8,128)(2,1)}, u32[]{:S(2)}, u32[]{:S(2)}) collective-permute-start(bf16[2,256,512]{2,1,0:T(8,128)(2,1)} %get-tuple-element.63), channel_id=1, source_target_pairs={{8,0},{12,4},{16,8},{20,12},{24,16},{28,20},{9,1},{13,5},{17,9},{2... | collective-permute-start | bytes 1572872 | tf_op jit(solution)/shard_map/ppermute | solution.py:27
  143.6 4.7 %collective-permute-start.19 = (bf16[2,256,512]{2,1,0:T(8,128)(2,1)S(1)}, bf16[2,256,512]{2,1,0:T(8,128)(2,1)}, u32[]{:S(2)}, u32[]{:S(2)}) collective-permute-start(bf16[2,256,512]{2,1,0:T(8,128)(2,1)S(1)} %get-tuple-element.64), channel_id=1, source_target_pairs={{0,8},{4,12},{8,16},{12,20},{16,24},{20,28},{1,9},{5,13},{9,17},{1... | collective-permute-start | bytes 1572872 | tf_op jit(solution)/shard_map/ppermute | solution.py:27
  149.4 7.7 %collective-permute-done.22 = bf16[512,512]{1,0:T(8,128)(2,1)S(1)} collective-permute-done((bf16[512,512]{1,0:T(8,128)(2,1)S(1)}, bf16[512,512]{1,0:T(8,128)(2,1)S(1)}, u32[]{:S(2)}, u32[]{:S(2)}) %collective-permute-start.22) | collective-permute-done | bytes 524320 | tf_op jit(solution)/shard_map/ppermute | solution.py:58
  157.4 2.4 %convert_add_fusion = f32[512,512]{1,0:T(8,128)} fusion(bf16[512,512]{1,0:T(8,128)(2,1)S(1)} %collective-permute-done.22, bf16[512,512]{1,0:T(8,128)(2,1)} %copy-done.32, f32[512,512]{1,0:T(8,128)S(1)} %copy-done.18, bf16[512,512]{1,0:T(8,128)(2,1)} %copy-done.31), kind=kLoop, calls=%fused_computation.7 | loop fusion | flops 1572864 | bytes 3670016 | tf_op jit(solution)/shard_map/add | solution.py:451
  159.9 4.0 %collective-permute-done.14 = bf16[256,512]{1,0:T(8,128)(2,1)S(1)} collective-permute-done((bf16[256,512]{1,0:T(8,128)(2,1)S(1)}, bf16[256,512]{1,0:T(8,128)(2,1)S(1)}, u32[]{:S(2)}, u32[]{:S(2)}) %collective-permute-start.14) | collective-permute-done | bytes 262176 | tf_op jit(solution)/shard_map/ppermute | solution.py:62
  164.9 16.8 %collective-permute-done.18.b_ref = bf16[2,256,512]{2,1,0:T(8,128)(2,1)} collective-permute-done((bf16[2,256,512]{2,1,0:T(8,128)(2,1)}, bf16[2,256,512]{2,1,0:T(8,128)(2,1)}, u32[]{:S(2)}, u32[]{:S(2)}) %collective-permute-start.18) | collective-permute-done | bytes 524320 | tf_op jit(solution)/shard_map/ppermute | solution.py:27
  181.7 2.0 %convert_add_fusion.1.first_ref = f32[2,128,512]{2,1,0:T(8,128)} fusion(bf16[2,128,512]{2,1,0:T(8,128)(2,1)} %collective-permute-done.21, bf16[2,128,512]{2,1,0:T(8,128)(2,1)} %collective-permute-done.20, bf16[2,384,512]{2,1,0:T(8,128)(2,1)S(1)} %first_grad.1, bf16[2,384,512]{2,1,0:T(8,128)(2,1)} %copy-done.30), kind=kLoop, calls=%fused_computation.14 | loop fusion | flops 917504 | bytes 1572864 | tf_op jit(solution)/shard_map/add | solution.py:454
  183.8 2.6 %finish.1 = (bf16[256,512]{1,0:T(8,128)(2,1)}, bf16[256,512]{1,0:T(8,128)(2,1)}) custom-call(s32[1]{0:T(128)} %bitcast.run_ref, f32[2,256,512]{2,1,0:T(8,128)} %copy-done.19, bf16[2,256,512]{2,1,0:T(8,128)(2,1)} %copy-done.33, bf16[2,256,512]{2,1,0:T(8,128)(2,1)} %collective-permute-done.18.b_ref, bf16[2,256,512]{2,1,0:T(8,128)(2,1)} %collective-permute-done.19.c_ref, ...), custom_call_target="tpu_custom_call" | custom-call | flops 1 | bytes 1 | tf_op jit(solution)/shard_map/finish/pallas_call | solution.py:458
  (116 shorter events, 30.2 us)
Async XLA Ops:
  7.2 79.1 %all-gather.2.cloned.1.call-start = ((), (), s32[]{:S(2)}) async-start(), calls=%async_computation.1 | async-start | bytes 2621440 | tf_op jit(solution)/shard_map/all_gather | solution.py:290
  8.4 21.6 %copy-start.8 = (bf16[512,512]{1,0:T(8,128)(2,1)S(1)}, bf16[512,512]{1,0:T(8,128)(2,1)}, u32[]{:S(2)}) copy-start(bf16[512,512]{1,0:T(8,128)(2,1)} %rest_0_.1) | copy-start | bytes 1572868
  9.6 19.3 %collective-permute-start.2 = (bf16[3,256,512]{2,1,0:T(8,128)(2,1)S(1)}, bf16[3,256,512]{2,1,0:T(8,128)(2,1)S(1)}, u32[]{:S(2)}, u32[]{:S(2)}) collective-permute-start(bf16[3,256,512]{2,1,0:T(8,128)(2,1)S(1)} %pad_maximum_fusion), channel_id=1, source_target_pairs={{0,4},{4,0},{8,12},{12,8},{16,20},{20,16},{24,28},{28,24},{1,5},{5... | collective-permute-start | bytes 2359304 | tf_op jit(solution)/shard_map/ppermute | solution.py:62
  11.2 17.8 %collective-permute-start.1 = (bf16[2,256,512]{2,1,0:T(8,128)(2,1)S(1)}, bf16[2,256,512]{2,1,0:T(8,128)(2,1)S(1)}, u32[]{:S(2)}, u32[]{:S(2)}) collective-permute-start(bf16[2,256,512]{2,1,0:T(8,128)(2,1)S(1)} %pad_maximum_fusion.1), channel_id=1, source_target_pairs={{8,0},{12,4},{16,8},{20,12},{24,16},{28,20},{9,1},{13,5},{17,9},{2... | collective-permute-start | bytes 1572872 | tf_op jit(solution)/shard_map/ppermute | solution.py:27
  13.6 15.4 %collective-permute-start = (bf16[2,256,512]{2,1,0:T(8,128)(2,1)S(1)}, bf16[2,256,512]{2,1,0:T(8,128)(2,1)S(1)}, u32[]{:S(2)}, u32[]{:S(2)}) collective-permute-start(bf16[2,256,512]{2,1,0:T(8,128)(2,1)S(1)} %pad_maximum_fusion.1), channel_id=1, source_target_pairs={{0,8},{4,12},{8,16},{12,20},{16,24},{20,28},{1,9},{5,13},{9,17},{1... | collective-permute-start | bytes 1572872 | tf_op jit(solution)/shard_map/ppermute | solution.py:27
  28.9 46.3 %copy-start.4 = (bf16[3,256,512]{2,1,0:T(8,128)(2,1)}, bf16[3,256,512]{2,1,0:T(8,128)(2,1)S(1)}, u32[]{:S(2)}) copy-start(bf16[3,256,512]{2,1,0:T(8,128)(2,1)S(1)} %collective-permute-done.2.rest_2_) | copy-start | bytes 2359300
  29.0 46.2 %copy-start.6 = (bf16[2,256,512]{2,1,0:T(8,128)(2,1)}, bf16[2,256,512]{2,1,0:T(8,128)(2,1)S(1)}, u32[]{:S(2)}) copy-start(bf16[2,256,512]{2,1,0:T(8,128)(2,1)S(1)} %collective-permute-done.1.rest_1_) | copy-start | bytes 1572868
  29.9 40.7 %copy-start.35 = (s32[16,3]{0,1:T(4,128)S(1)}, s32[16,3]{0,1:T(4,128)}, u32[]{:S(2)}) copy-start(s32[16,3]{0,1:T(4,128)} %param.10) | copy-start | bytes 580
  30.0 118.4 %reduce-scatter.2.cloned.1.call-start = ((), (), s32[]{:S(2)}) async-start(), calls=%async_computation.2 | async-start | bytes 2621440 | tf_op jit(solution)/shard_map/reduce_scatter | solution.py:389
  30.0 14.7 %collective-permute-start.8 = (bf16[512,512]{1,0:T(8,128)(2,1)S(1)}, bf16[512,512]{1,0:T(8,128)(2,1)S(1)}, u32[]{:S(2)}, u32[]{:S(2)}) collective-permute-start(bf16[512,512]{1,0:T(8,128)(2,1)S(1)} %copy-done.8), channel_id=1, source_target_pairs={{8,16},{12,20},{16,8},{20,12},{9,17},{13,21},{17,9},{21,13},{10,18... | collective-permute-start | bytes 1572872 | tf_op jit(solution)/shard_map/ppermute | solution.py:302
  33.5 15.0 %collective-permute-start.7 = (bf16[512,512]{1,0:T(8,128)(2,1)S(1)}, bf16[512,512]{1,0:T(8,128)(2,1)}, u32[]{:S(2)}, u32[]{:S(2)}) collective-permute-start(bf16[512,512]{1,0:T(8,128)(2,1)S(1)} %copy-done.8), channel_id=1, source_target_pairs={{0,8},{4,12},{8,0},{12,4},{16,24},{20,28},{24,16},{28,20},{1,9},{5... | collective-permute-start | bytes 1572872 | tf_op jit(solution)/shard_map/ppermute | solution.py:302
  33.6 0.7 collective-permute-start.4
  44.7 41.5 %copy-start.11 = (bf16[512,512]{1,0:T(8,128)(2,1)}, bf16[512,512]{1,0:T(8,128)(2,1)S(1)}, u32[]{:S(2)}) copy-start(bf16[512,512]{1,0:T(8,128)(2,1)S(1)} %collective-permute-done.8.rest_2_) | copy-start | bytes 1572868
  48.5 17.3 %collective-permute-start.10 = (bf16[512,512]{1,0:T(8,128)(2,1)}, bf16[512,512]{1,0:T(8,128)(2,1)S(1)}, u32[]{:S(2)}, u32[]{:S(2)}) collective-permute-start(bf16[512,512]{1,0:T(8,128)(2,1)} %collective-permute-done.7.rest_1_), channel_id=1, source_target_pairs={{8,16},{12,20},{16,8},{20,12},{9,17},{13,21},{17,9},{21,13},{10,18... | collective-permute-start | bytes 1572872 | tf_op jit(solution)/shard_map/ppermute | solution.py:302
  56.6 18.5 %collective-permute-start.3 = (bf16[2,256,512]{2,1,0:T(8,128)(2,1)}, bf16[2,256,512]{2,1,0:T(8,128)(2,1)}, u32[]{:S(2)}, u32[]{:S(2)}) collective-permute-start(bf16[2,256,512]{2,1,0:T(8,128)(2,1)} %broadcast_select_fusion), channel_id=1, source_target_pairs={{0,4},{8,12},{16,20},{12,8},{20,16},{28,24},{1,5},{9,13},{17,21},{... | collective-permute-start | bytes 1572872 | tf_op jit(solution)/shard_map/ppermute | solution.py:293
  58.6 27.7 %collective-permute-start.9 = (bf16[512,512]{1,0:T(8,128)(2,1)S(1)}, bf16[512,512]{1,0:T(8,128)(2,1)}, u32[]{:S(2)}, u32[]{:S(2)}) collective-permute-start(bf16[512,512]{1,0:T(8,128)(2,1)S(1)} %collective-permute-done.8.rest_2_), channel_id=1, source_target_pairs={{8,0},{12,4},{16,24},{20,28},{9,1},{13,5},{17,25},{21,29},{10,2},{... | collective-permute-start | bytes 1572872 | tf_op jit(solution)/shard_map/ppermute | solution.py:302
  65.8 17.2 %copy-start.14 = (bf16[512,512]{1,0:T(8,128)(2,1)}, bf16[512,512]{1,0:T(8,128)(2,1)S(1)}, u32[]{:S(2)}) copy-start(bf16[512,512]{1,0:T(8,128)(2,1)S(1)} %collective-permute-done.10.rest_4_) | copy-start | bytes 1572868
  65.8 20.4 %collective-permute-start.11 = (bf16[512,512]{1,0:T(8,128)(2,1)S(1)}, bf16[512,512]{1,0:T(8,128)(2,1)}, u32[]{:S(2)}, u32[]{:S(2)}) collective-permute-start(bf16[512,512]{1,0:T(8,128)(2,1)S(1)} %collective-permute-done.10.rest_4_), channel_id=1, source_target_pairs={{8,0},{12,4},{16,24},{20,28},{9,1},{13,5},{17,25},{21,29},{10,2},{... | collective-permute-start | bytes 1572872 | tf_op jit(solution)/shard_map/ppermute | solution.py:302
  68.7 5.5 %collective-permute-start.5 = (bf16[2,128,512]{2,1,0:T(8,128)(2,1)}, bf16[2,128,512]{2,1,0:T(8,128)(2,1)}, u32[]{:S(2)}, u32[]{:S(2)}) collective-permute-start(bf16[2,128,512]{2,1,0:T(8,128)(2,1)} %fusion.9), channel_id=1, source_target_pairs={{4,28},{0,12},{16,20},{8,24},{5,29},{1,13},{17,21},{9,25},{6,30},{... | collective-permute-start | bytes 786440 | tf_op jit(solution)/shard_map/ppermute | solution.py:298
  83.0 11.6 %collective-permute-start.6 = (bf16[256,512]{1,0:T(8,128)(2,1)}, bf16[256,512]{1,0:T(8,128)(2,1)}, u32[]{:S(2)}, u32[]{:S(2)}) collective-permute-start(bf16[256,512]{1,0:T(8,128)(2,1)} %get-tuple-element.38.mixed_ref.rest_2_.rest_5_), channel_id=1, source_target_pairs={{0,4},{4,0},{8,12},{12,8},{16,20},{20,16},{24,28},{28,24},{1,5},{5... | collective-permute-start | bytes 786440 | tf_op jit(solution)/shard_map/ppermute | solution.py:62
  94.6 13.0 %collective-permute-start.12 = (bf16[256,512]{1,0:T(8,128)(2,1)S(1)}, bf16[256,512]{1,0:T(8,128)(2,1)}, u32[]{:S(2)}, u32[]{:S(2)}) collective-permute-start(bf16[256,512]{1,0:T(8,128)(2,1)S(1)} %get-tuple-element.43), channel_id=1, source_target_pairs={{0,4},{4,0},{8,12},{12,8},{16,20},{20,16},{24,28},{28,24},{1,5},{5... | collective-permute-start | bytes 786440 | tf_op jit(solution)/shard_map/ppermute | solution.py:62
  105.4 20.6 %collective-permute-start.15 = (bf16[512,512]{1,0:T(8,128)(2,1)}, bf16[512,512]{1,0:T(8,128)(2,1)S(1)}, u32[]{:S(2)}, u32[]{:S(2)}) collective-permute-start(bf16[512,512]{1,0:T(8,128)(2,1)} %get-tuple-element.57), channel_id=1, source_target_pairs={{0,8},{4,12},{8,16},{12,20},{16,24},{20,28},{24,0},{28,4},{1,9},{5... | collective-permute-start | bytes 1572872 | tf_op jit(solution)/shard_map/ppermute | solution.py:58
  106.4 24.9 %collective-permute-start.16 = (bf16[512,512]{1,0:T(8,128)(2,1)S(1)}, bf16[512,512]{1,0:T(8,128)(2,1)S(1)}, u32[]{:S(2)}, u32[]{:S(2)}) collective-permute-start(bf16[512,512]{1,0:T(8,128)(2,1)S(1)} %copy-done.29), channel_id=1, source_target_pairs={{0,24},{4,28},{8,0},{12,4},{16,8},{20,12},{24,16},{28,20},{1,25},{... | collective-permute-start | bytes 1572872 | tf_op jit(solution)/shard_map/ppermute | solution.py:58
  112.4 20.4 %collective-permute-start.17 = (bf16[2,384,512]{2,1,0:T(8,128)(2,1)S(1)}, bf16[2,384,512]{2,1,0:T(8,128)(2,1)S(1)}, u32[]{:S(2)}, u32[]{:S(2)}) collective-permute-start(bf16[2,384,512]{2,1,0:T(8,128)(2,1)S(1)} %first_grad.1), channel_id=1, source_target_pairs={{0,4},{4,0},{8,12},{12,8},{16,20},{20,16},{24,28},{28,24},{1,5},{5... | collective-permute-start | bytes 2359304 | tf_op jit(solution)/shard_map/ppermute | solution.py:62
  123.6 19.2 %collective-permute-start.13 = (bf16[2,256,512]{2,1,0:T(8,128)(2,1)S(1)}, bf16[2,256,512]{2,1,0:T(8,128)(2,1)S(1)}, u32[]{:S(2)}, u32[]{:S(2)}) collective-permute-start(bf16[2,256,512]{2,1,0:T(8,128)(2,1)S(1)} %get-tuple-element.51), channel_id=1, source_target_pairs={{0,4},{4,0},{8,12},{12,8},{16,20},{20,16},{24,28},{28,24},{1,5},{5... | collective-permute-start | bytes 1572872 | tf_op jit(solution)/shard_map/ppermute | solution.py:62
  133.7 23.8 %copy-start.18 = (f32[512,512]{1,0:T(8,128)S(1)}, f32[512,512]{1,0:T(8,128)}, u32[]{:S(2)}) copy-start(f32[512,512]{1,0:T(8,128)} %copy-done.17) | copy-start | bytes 3145732
  134.8 22.3 %collective-permute-start.22 = (bf16[512,512]{1,0:T(8,128)(2,1)S(1)}, bf16[512,512]{1,0:T(8,128)(2,1)S(1)}, u32[]{:S(2)}, u32[]{:S(2)}) collective-permute-start(bf16[512,512]{1,0:T(8,128)(2,1)S(1)} %copy-done.27), channel_id=1, source_target_pairs={{0,16},{4,20},{8,24},{12,28},{16,0},{20,4},{24,8},{28,12},{1,17},{... | collective-permute-start | bytes 1572872 | tf_op jit(solution)/shard_map/ppermute | solution.py:58
  137.9 27.0 %collective-permute-start.21 = (bf16[2,128,512]{2,1,0:T(8,128)(2,1)}, bf16[2,128,512]{2,1,0:T(8,128)(2,1)}, u32[]{:S(2)}, u32[]{:S(2)}) collective-permute-start(bf16[2,128,512]{2,1,0:T(8,128)(2,1)} %get-tuple-element.65), channel_id=1, source_target_pairs={{24,0},{25,1},{26,2},{27,3}} | collective-permute-start | bytes 786440 | tf_op jit(solution)/shard_map/ppermute | solution.py:453
  139.2 42.5 %collective-permute-start.20 = (bf16[2,128,512]{2,1,0:T(8,128)(2,1)}, bf16[2,128,512]{2,1,0:T(8,128)(2,1)}, u32[]{:S(2)}, u32[]{:S(2)}) collective-permute-start(bf16[2,128,512]{2,1,0:T(8,128)(2,1)} %get-tuple-element.65), channel_id=1, source_target_pairs={{16,0},{17,1},{18,2},{19,3}} | collective-permute-start | bytes 786440 | tf_op jit(solution)/shard_map/ppermute | solution.py:453
  140.6 41.1 %collective-permute-start.18 = (bf16[2,256,512]{2,1,0:T(8,128)(2,1)}, bf16[2,256,512]{2,1,0:T(8,128)(2,1)}, u32[]{:S(2)}, u32[]{:S(2)}) collective-permute-start(bf16[2,256,512]{2,1,0:T(8,128)(2,1)} %get-tuple-element.63), channel_id=1, source_target_pairs={{8,0},{12,4},{16,8},{20,12},{24,16},{28,20},{9,1},{13,5},{17,9},{2... | collective-permute-start | bytes 1572872 | tf_op jit(solution)/shard_map/ppermute | solution.py:27
  143.6 38.1 %collective-permute-start.19 = (bf16[2,256,512]{2,1,0:T(8,128)(2,1)S(1)}, bf16[2,256,512]{2,1,0:T(8,128)(2,1)}, u32[]{:S(2)}, u32[]{:S(2)}) collective-permute-start(bf16[2,256,512]{2,1,0:T(8,128)(2,1)S(1)} %get-tuple-element.64), channel_id=1, source_target_pairs={{0,8},{4,12},{8,16},{12,20},{16,24},{20,28},{1,9},{5,13},{9,17},{1... | collective-permute-start | bytes 1572872 | tf_op jit(solution)/shard_map/ppermute | solution.py:27
  157.1 6.8 %collective-permute-start.14 = (bf16[256,512]{1,0:T(8,128)(2,1)S(1)}, bf16[256,512]{1,0:T(8,128)(2,1)S(1)}, u32[]{:S(2)}, u32[]{:S(2)}) collective-permute-start(bf16[256,512]{1,0:T(8,128)(2,1)S(1)} %get-tuple-element.76), channel_id=1, source_target_pairs={{0,4},{4,0},{8,12},{12,8},{16,20},{20,16},{24,28},{28,24},{1,5},{5... | collective-permute-start | bytes 786440 | tf_op jit(solution)/shard_map/ppermute | solution.py:62
  (29 other events, 127.9 us)
Sparse Core Ops, SparseCore 0:
  30.1 22.7 all-gather.1
  105.6 32.0 reduce-scatter.1

commit v6 on v2

--- a/solution.py
+++ b/solution.py
@@ -134,11 +134,15 @@
         out_ref[...] = mm(rows_ref[:, pl.ds(column, width)], both_ref[...], TN).astype(out_ref.dtype)
 
 
-def finish_kernel(scale, run_ref, own_ref, a_ref, b_ref, c_ref, first_ref, key_ref, value_ref):
+def finish_kernel(scale, run_ref, own_ref, a_ref, b_ref, c_ref, first_ref, *rest):
+    key_ref, value_ref = rest[-2:]
     there = jnp.where((run_ref[0] == 0) & (pl.program_id(0) == 0), 1.0, 0.0).astype(jnp.float32)
     for n, out_ref in enumerate((key_ref, value_ref)):
         total = own_ref[n] + a_ref[n].astype(jnp.float32) + b_ref[n].astype(jnp.float32) + c_ref[n].astype(jnp.float32)
-        total = total + there * first_ref[n]
+        head = first_ref[n]
+        for ref in rest[:-2]:
+            head = head + ref[n].astype(jnp.float32)
+        total = total + there * head
         out_ref[...] = (total * (scale if n == 0 else 1.0)).astype(jnp.bfloat16)
 
 
@@ -448,21 +452,22 @@
         weight_grad = own_part
         for part in weight_turns + [turned(last_part, 2, length)]:
             weight_grad = weight_grad + part.astype(jnp.float32)
+        near_sums = []
         for c in range(length, ctx, 2):
             got = tied(lax.ppermute(near, "ctx", [(c, 0)]), back_down, back_up, attended)
-            first_sum = first_sum + got.astype(jnp.float32)
+            near_sums.append(got)
         wide = pl.BlockSpec((2, BLK, features), lambda n: (0, n, 0))
         top = pl.BlockSpec((2, BLK, features), lambda n: (0, 0, 0))
         slab = pl.BlockSpec((BLK, features), lambda n: (n, 0))
         key_grad, value_grad = pl.pallas_call(
             functools.partial(finish_kernel, scale),
             grid=(per_dev,),
-            in_specs=[smem] + [wide] * 4 + [top],
+            in_specs=[smem] + [wide] * 4 + [top] * (1 + len(near_sums)),
             out_specs=[slab, slab],
             out_shape=[jax.ShapeDtypeStruct((tokens, features), jnp.bfloat16)] * 2,
             cost_estimate=CHEAP,
             name="finish",
-        )(run_word, own, back_pair, back_down, back_up, first_sum)
+        )(run_word, own, back_pair, back_down, back_up, first_sum, *near_sums)
 
     else:
         first_sum = to_first(early_grads.astype(jnp.float32))

time: 187 us -> 186 us (level)
  transfers between devices with their start and end apart: 25 -> 25, of which waited for: 10 -> 10; matrix products, arithmetic and copies ran while one was open for 4% -> 5% of each run, Pallas kernels for 17% -> 16%
where the time goes in v6:
time: 186 us; the launch traced here: 185 us
  waiting for transfers between devices  58.9 us (32%)
  starting transfers between devices  56.9 us (31%)
  Pallas kernels  33.3 us (18%)
  between operations  14.5 us (8%)
  local copies, waits for them, and re-layouts  11.3 us (6%)
  other arithmetic  9.72 us (5%)
    ppermute x5, starting transfers between devices, between(): lax.ppermute(x, 'ctx', [(2 * a + n, 2 * b + n) for a, b in places for n i...  21.7 us
    ppermute x6, waiting for transfers between devices, swapped(): lax.ppermute(piece, 'ctx', [(2 * z + n, 2 * z + 1 - n) for z in places fo...  19.9 us
    ppermute x4, starting transfers between devices, shifted(): lax.ppermute(x, 'ctx', [(i, i + by) for i in range(peers) if 0 <= i + by...  12.9 us
    ppermute x4, waiting for transfers between devices, shifted(): lax.ppermute(x, 'ctx', [(i, i + by) for i in range(peers) if 0 <= i + by...  12.2 us
    ppermute x5, waiting for transfers between devices, between(): lax.ppermute(x, 'ctx', [(2 * a + n, 2 * b + n) for a, b in places for n i...  11.8 us
    ppermute x3, waiting for transfers between devices, turned(): lax.ppermute(x, 'ctx', [(2 * z + n, 2 * ((z + by) % length) + n) for z in...  11.8 us
    unnamed x63, local copies, waits for them, and re-layouts  9.12 us
    pallas_call x1, Pallas kernels, local(): pl.pallas_call(functools.partial(bwd_kernel, offsets, early, per_dev, sca...  9.05 us
  transfers between devices with their start and end apart: 25, of which 10 were waited for; matrix products, arithmetic and copies ran while one was open for 5% of the time, Pallas kernels for 16%

profile of v6, /device:TPU:12, one launch (start us, length us, event | category | flops | bytes accessed | tf_op | source)
XLA Modules:
  0.0 184.7 jit_solution(10839751783784404807)
XLA Ops:
  11.1 2.4 %collective-permute-start.1 = (bf16[2,256,512]{2,1,0:T(8,128)(2,1)S(1)}, bf16[2,256,512]{2,1,0:T(8,128)(2,1)S(1)}, u32[]{:S(2)}, u32[]{:S(2)}) collective-permute-start(bf16[2,256,512]{2,1,0:T(8,128)(2,1)S(1)} %pad_maximum_fusion.1), channel_id=1, source_target_pairs={{8,0},{12,4},{16,8},{20,12},{24,16},{28,20},{9,1},{13,5},{17,9},{2... | collective-permute-start | bytes 1572872 | tf_op jit(solution)/shard_map/ppermute | solution.py:27
  13.5 3.5 %collective-permute-start = (bf16[2,256,512]{2,1,0:T(8,128)(2,1)S(1)}, bf16[2,256,512]{2,1,0:T(8,128)(2,1)S(1)}, u32[]{:S(2)}, u32[]{:S(2)}) collective-permute-start(bf16[2,256,512]{2,1,0:T(8,128)(2,1)S(1)} %pad_maximum_fusion.1), channel_id=1, source_target_pairs={{0,8},{4,12},{8,16},{12,20},{16,24},{20,28},{1,9},{5,13},{9,17},{1... | collective-permute-start | bytes 1572872 | tf_op jit(solution)/shard_map/ppermute | solution.py:27
  17.0 11.9 %collective-permute-done.2.rest_2_ = bf16[3,256,512]{2,1,0:T(8,128)(2,1)S(1)} collective-permute-done((bf16[3,256,512]{2,1,0:T(8,128)(2,1)S(1)}, bf16[3,256,512]{2,1,0:T(8,128)(2,1)S(1)}, u32[]{:S(2)}, u32[]{:S(2)}) %collective-permute-start.2) | collective-permute-done | bytes 786464 | tf_op jit(solution)/shard_map/ppermute | solution.py:62
  30.7 10.4 %collective-permute-start.7 = (bf16[512,512]{1,0:T(8,128)(2,1)S(1)}, bf16[512,512]{1,0:T(8,128)(2,1)}, u32[]{:S(2)}, u32[]{:S(2)}) collective-permute-start(bf16[512,512]{1,0:T(8,128)(2,1)S(1)} %copy-done.8), channel_id=1, source_target_pairs={{0,8},{4,12},{8,0},{12,4},{16,24},{20,28},{24,16},{28,20},{1,9},{5... | collective-permute-start | bytes 1572872 | tf_op jit(solution)/shard_map/ppermute | solution.py:306
  41.1 3.8 %collective-permute-start.8 = (bf16[512,512]{1,0:T(8,128)(2,1)S(1)}, bf16[512,512]{1,0:T(8,128)(2,1)}, u32[]{:S(2)}, u32[]{:S(2)}) collective-permute-start(bf16[512,512]{1,0:T(8,128)(2,1)S(1)} %copy-done.8), channel_id=1, source_target_pairs={{8,16},{12,20},{16,8},{20,12},{9,17},{13,21},{17,9},{21,13},{10,18... | collective-permute-start | bytes 1572872 | tf_op jit(solution)/shard_map/ppermute | solution.py:306
  44.9 6.5 %collective-permute-done.7.rest_1_ = bf16[512,512]{1,0:T(8,128)(2,1)} collective-permute-done((bf16[512,512]{1,0:T(8,128)(2,1)S(1)}, bf16[512,512]{1,0:T(8,128)(2,1)}, u32[]{:S(2)}, u32[]{:S(2)}) %collective-permute-start.7) | collective-permute-done | bytes 524320 | tf_op jit(solution)/shard_map/ppermute | solution.py:306
  51.4 4.0 %collective-permute-start.10 = (bf16[512,512]{1,0:T(8,128)(2,1)}, bf16[512,512]{1,0:T(8,128)(2,1)}, u32[]{:S(2)}, u32[]{:S(2)}) collective-permute-start(bf16[512,512]{1,0:T(8,128)(2,1)} %collective-permute-done.7.rest_1_), channel_id=1, source_target_pairs={{8,16},{12,20},{16,8},{20,12},{9,17},{13,21},{17,9},{21,13},{10,18... | collective-permute-start | bytes 1572872 | tf_op jit(solution)/shard_map/ppermute | solution.py:306
  56.3 1.9 %collective-permute-start.3 = (bf16[2,256,512]{2,1,0:T(8,128)(2,1)}, bf16[2,256,512]{2,1,0:T(8,128)(2,1)}, u32[]{:S(2)}, u32[]{:S(2)}) collective-permute-start(bf16[2,256,512]{2,1,0:T(8,128)(2,1)} %broadcast_select_fusion), channel_id=1, source_target_pairs={{0,4},{8,12},{16,20},{12,8},{20,16},{28,24},{1,5},{9,13},{17,21},{... | collective-permute-start | bytes 1572872 | tf_op jit(solution)/shard_map/ppermute | solution.py:297
  59.5 5.4 %collective-permute-done.10.rest_4_ = bf16[512,512]{1,0:T(8,128)(2,1)} collective-permute-done((bf16[512,512]{1,0:T(8,128)(2,1)}, bf16[512,512]{1,0:T(8,128)(2,1)}, u32[]{:S(2)}, u32[]{:S(2)}) %collective-permute-start.10) | collective-permute-done | bytes 524320 | tf_op jit(solution)/shard_map/ppermute | solution.py:306
  64.9 2.1 %collective-permute-start.11 = (bf16[512,512]{1,0:T(8,128)(2,1)}, bf16[512,512]{1,0:T(8,128)(2,1)}, u32[]{:S(2)}, u32[]{:S(2)}) collective-permute-start(bf16[512,512]{1,0:T(8,128)(2,1)} %collective-permute-done.10.rest_4_), channel_id=1, source_target_pairs={{8,0},{12,4},{16,24},{20,28},{9,1},{13,5},{17,25},{21,29},{10,2},{... | collective-permute-start | bytes 1572872 | tf_op jit(solution)/shard_map/ppermute | solution.py:306
  67.1 2.0 %collective-permute-start.5 = (bf16[2,128,512]{2,1,0:T(8,128)(2,1)S(1)}, bf16[2,128,512]{2,1,0:T(8,128)(2,1)}, u32[]{:S(2)}, u32[]{:S(2)}) collective-permute-start(bf16[2,128,512]{2,1,0:T(8,128)(2,1)S(1)} %fusion.7), channel_id=1, source_target_pairs={{4,28},{0,12},{16,20},{8,24},{5,29},{1,13},{17,21},{9,25},{6,30},{... | collective-permute-start | bytes 786440 | tf_op jit(solution)/shard_map/ppermute | solution.py:302
  69.1 3.1 %collective-permute-done.5 = bf16[2,128,512]{2,1,0:T(8,128)(2,1)} collective-permute-done((bf16[2,128,512]{2,1,0:T(8,128)(2,1)S(1)}, bf16[2,128,512]{2,1,0:T(8,128)(2,1)}, u32[]{:S(2)}, u32[]{:S(2)}) %collective-permute-start.5) | collective-permute-done | bytes 262176 | tf_op jit(solution)/shard_map/ppermute | solution.py:302
  73.4 6.2 %attend.1 = (bf16[256,512]{1,0:T(8,128)(2,1)S(1)}, f32[4,1,256]{2,1,0:T(1,128)S(1)}) custom-call(s32[1]{0:T(128)} %bitcast.run_ref, s32[16,3]{1,0:T(8,128)S(1)} %copy.11.lists_ref, bf16[256,512]{1,0:T(8,128)(2,1)S(1)} %copy-done.21, bf16[256,512]{1,0:T(8,128)(2,1)S(1)} %copy-done.3, bf16[256,512]{1,0:T(8,128)(2,1)S(1)} %copy-done.2, ...), custom_call_target="tpu_custom_call" | custom-call | flops 1 | bytes 1 | tf_op jit(solution)/shard_map/attend/pallas_call | solution.py:339
  79.6 1.9 %collective-permute-start.6 = (bf16[256,512]{1,0:T(8,128)(2,1)S(1)}, bf16[256,512]{1,0:T(8,128)(2,1)}, u32[]{:S(2)}, u32[]{:S(2)}) collective-permute-start(bf16[256,512]{1,0:T(8,128)(2,1)S(1)} %get-tuple-element.36.mixed_ref.rest_2_.rest_5_), channel_id=1, source_target_pairs={{0,4},{4,0},{8,12},{12,8},{16,20},{20,16},{24,28},{28,24},{1,5},{5... | collective-permute-start | bytes 786440 | tf_op jit(solution)/shard_map/ppermute | solution.py:62
  82.2 1.6 copy-done
  85.9 3.5 %project_grad.1 = (f32[256,512]{1,0:T(8,128)S(1)}, bf16[256,512]{1,0:T(8,128)(2,1)}) custom-call(bf16[512,2048]{1,0:T(8,128)(2,1)S(1)} %copy-done, bf16[512,512]{1,0:T(8,128)(2,1)S(1)} %copy-done.9, bf16[512,512]{1,0:T(8,128)(2,1)} %collective-permute-done.7.rest_1_, bf16[512,512]{1,0:T(8,128)(2,1)} %collective-permute-done.8.rest_2_, ...), custom_call_target="tpu_custom_call" | custom-call | flops 1 | bytes 1 | tf_op jit(solution)/shard_map/project_grad/pallas_call | solution.py:356
  90.5 2.6 %weight_part.1 = (f32[512,512]{1,0:T(8,128)S(1)}, bf16[512,512]{1,0:T(8,128)(2,1)}, bf16[512,512]{1,0:T(8,128)(2,1)S(1)}, bf16[512,512]{1,0:T(8,128)(2,1)S(1)}) custom-call(bf16[512,2048]{1,0:T(8,128)(2,1)S(1)} %copy-done.1, bf16[256,512]{1,0:T(8,128)(2,1)S(1)} %get-tuple-element.36.mixed_ref.rest_2_.rest_5_, bf16[256,512]{1,0:T(8,128)(2,1)} %collective-permute-done.6.other_ref), custom_call_target="tpu_custom_call" | custom-call | flops 1 | bytes 1 | tf_op jit(solution)/shard_map/weight_part/pallas_call | solution.py:371
  95.7 5.3 %project_out.1 = bf16[512,2048]{1,0:T(8,128)(2,1)} custom-call(bf16[256,512]{1,0:T(8,128)(2,1)S(1)} %get-tuple-element.36.mixed_ref.rest_2_.rest_5_, bf16[256,512]{1,0:T(8,128)(2,1)} %collective-permute-done.6.other_ref, bf16[512,512]{1,0:T(8,128)(2,1)S(1)} %copy-done.10, bf16[512,512]{1,0:T(8,128)(2,1)} %collective-permute-done.7.rest_1_, ...), custom_call_target="tpu_custom_call" | custom-call | flops 1 | bytes 1 | tf_op jit(solution)/shard_map/project_out/pallas_call | solution.py:382
  101.1 5.3 %collective-permute-start.15 = (bf16[512,512]{1,0:T(8,128)(2,1)}, bf16[512,512]{1,0:T(8,128)(2,1)S(1)}, u32[]{:S(2)}, u32[]{:S(2)}) collective-permute-start(bf16[512,512]{1,0:T(8,128)(2,1)} %get-tuple-element.53), channel_id=1, source_target_pairs={{0,8},{4,12},{8,16},{12,20},{16,24},{20,28},{24,0},{28,4},{1,9},{5... | collective-permute-start | bytes 1572872 | tf_op jit(solution)/shard_map/ppermute | solution.py:58
  107.5 3.8 %first_grad.1 = bf16[2,384,512]{2,1,0:T(8,128)(2,1)S(1)} custom-call(s32[1]{0:T(128)} %bitcast.run_ref, s32[16,3]{1,0:T(8,128)S(1)} %copy.11.lists_ref, bf16[256,512]{1,0:T(8,128)(2,1)S(1)} %copy-done.22, bf16[2,256,512]{2,1,0:T(8,128)(2,1)} %collective-permute-done.3.rest_3_.rest_0_, bf16[2,128,512]{2,1,0:T(8,128)(2,1)S(1)} %copy-done.17, ...), custom_call_target="tpu_custom_call" | custom-call | flops 10000000000 | bytes 1 | tf_op jit(solution)/shard_map/first_grad/pallas_call | solution.py:402
  112.0 9.1 %attend_grad.1 = (bf16[256,512]{1,0:T(8,128)(2,1)}, f32[2,256,512]{2,1,0:T(8,128)S(1)}, bf16[2,256,512]{2,1,0:T(8,128)(2,1)S(1)}, bf16[2,256,512]{2,1,0:T(8,128)(2,1)S(1)}, bf16[2,256,512]{2,1,0:T(8,128)(2,1)S(1)}) custom-call(s32[1]{0:T(128)} %bitcast.run_ref, s32[16,3]{1,0:T(8,128)S(1)} %copy.11.lists_ref, bf16[256,512]{1,0:T(8,128)(2,1)S(1)} %copy-done.22, ...), custom_call_target="tpu_custom_call" | custom-call | flops 30000001024 | bytes 1 | tf_op jit(solution)/shard_map/attend_grad/pallas_call | solution.py:415
  122.5 2.5 %collective-permute-done.15 = bf16[512,512]{1,0:T(8,128)(2,1)S(1)} collective-permute-done((bf16[512,512]{1,0:T(8,128)(2,1)}, bf16[512,512]{1,0:T(8,128)(2,1)S(1)}, u32[]{:S(2)}, u32[]{:S(2)}) %collective-permute-start.15) | collective-permute-done | bytes 524320 | tf_op jit(solution)/shard_map/ppermute | solution.py:58
  125.0 2.2 %collective-permute-done.16 = bf16[512,512]{1,0:T(8,128)(2,1)S(1)} collective-permute-done((bf16[512,512]{1,0:T(8,128)(2,1)S(1)}, bf16[512,512]{1,0:T(8,128)(2,1)S(1)}, u32[]{:S(2)}, u32[]{:S(2)}) %collective-permute-start.16) | collective-permute-done | bytes 524320 | tf_op jit(solution)/shard_map/ppermute | solution.py:58
  127.2 4.6 %collective-permute-done.17 = bf16[2,384,512]{2,1,0:T(8,128)(2,1)S(1)} collective-permute-done((bf16[2,384,512]{2,1,0:T(8,128)(2,1)S(1)}, bf16[2,384,512]{2,1,0:T(8,128)(2,1)S(1)}, u32[]{:S(2)}, u32[]{:S(2)}) %collective-permute-start.17) | collective-permute-done | bytes 786464 | tf_op jit(solution)/shard_map/ppermute | solution.py:62
  134.1 3.3 %collective-permute-start.22 = (bf16[512,512]{1,0:T(8,128)(2,1)S(1)}, bf16[512,512]{1,0:T(8,128)(2,1)S(1)}, u32[]{:S(2)}, u32[]{:S(2)}) collective-permute-start(bf16[512,512]{1,0:T(8,128)(2,1)S(1)} %copy-done.24), channel_id=1, source_target_pairs={{0,16},{4,20},{8,24},{12,28},{16,0},{20,4},{24,8},{28,12},{1,17},{... | collective-permute-start | bytes 1572872 | tf_op jit(solution)/shard_map/ppermute | solution.py:58
  140.2 2.4 %collective-permute-start.18 = (bf16[2,256,512]{2,1,0:T(8,128)(2,1)}, bf16[2,256,512]{2,1,0:T(8,128)(2,1)}, u32[]{:S(2)}, u32[]{:S(2)}) collective-permute-start(bf16[2,256,512]{2,1,0:T(8,128)(2,1)} %get-tuple-element.59), channel_id=1, source_target_pairs={{8,0},{12,4},{16,8},{20,12},{24,16},{28,20},{9,1},{13,5},{17,9},{2... | collective-permute-start | bytes 1572872 | tf_op jit(solution)/shard_map/ppermute | solution.py:27
  142.7 4.7 %collective-permute-start.19 = (bf16[2,256,512]{2,1,0:T(8,128)(2,1)}, bf16[2,256,512]{2,1,0:T(8,128)(2,1)}, u32[]{:S(2)}, u32[]{:S(2)}) collective-permute-start(bf16[2,256,512]{2,1,0:T(8,128)(2,1)} %get-tuple-element.60), channel_id=1, source_target_pairs={{0,8},{4,12},{8,16},{12,20},{16,24},{20,28},{1,9},{5,13},{9,17},{1... | collective-permute-start | bytes 1572872 | tf_op jit(solution)/shard_map/ppermute | solution.py:27
  148.5 7.0 %collective-permute-done.22 = bf16[512,512]{1,0:T(8,128)(2,1)S(1)} collective-permute-done((bf16[512,512]{1,0:T(8,128)(2,1)S(1)}, bf16[512,512]{1,0:T(8,128)(2,1)S(1)}, u32[]{:S(2)}, u32[]{:S(2)}) %collective-permute-start.22) | collective-permute-done | bytes 524320 | tf_op jit(solution)/shard_map/ppermute | solution.py:58
  156.0 2.4 %convert_add_fusion = f32[512,512]{1,0:T(8,128)} fusion(bf16[512,512]{1,0:T(8,128)(2,1)S(1)} %collective-permute-done.22, bf16[512,512]{1,0:T(8,128)(2,1)} %copy-done.28, f32[512,512]{1,0:T(8,128)S(1)} %copy-done.15, bf16[512,512]{1,0:T(8,128)(2,1)} %copy-done.27), kind=kLoop, calls=%fused_computation.7 | loop fusion | flops 1572864 | bytes 3670016 | tf_op jit(solution)/shard_map/add | solution.py:454
  158.4 3.4 %collective-permute-done.14 = bf16[256,512]{1,0:T(8,128)(2,1)S(1)} collective-permute-done((bf16[256,512]{1,0:T(8,128)(2,1)S(1)}, bf16[256,512]{1,0:T(8,128)(2,1)S(1)}, u32[]{:S(2)}, u32[]{:S(2)}) %collective-permute-start.14) | collective-permute-done | bytes 262176 | tf_op jit(solution)/shard_map/ppermute | solution.py:62
  162.8 12.2 %collective-permute-done.18.b_ref = bf16[2,256,512]{2,1,0:T(8,128)(2,1)} collective-permute-done((bf16[2,256,512]{2,1,0:T(8,128)(2,1)}, bf16[2,256,512]{2,1,0:T(8,128)(2,1)}, u32[]{:S(2)}, u32[]{:S(2)}) %collective-permute-start.18) | collective-permute-done | bytes 524320 | tf_op jit(solution)/shard_map/ppermute | solution.py:27
  175.0 2.9 %finish.1 = (bf16[256,512]{1,0:T(8,128)(2,1)}, bf16[256,512]{1,0:T(8,128)(2,1)}) custom-call(s32[1]{0:T(128)} %bitcast.run_ref, f32[2,256,512]{2,1,0:T(8,128)} %copy-done.18, bf16[2,256,512]{2,1,0:T(8,128)(2,1)} %copy-done.29, bf16[2,256,512]{2,1,0:T(8,128)(2,1)} %collective-permute-done.18.b_ref, bf16[2,256,512]{2,1,0:T(8,128)(2,1)} %collective-permute-done.19.c_ref, ...), custom_call_target="tpu_custom_call" | custom-call | flops 1 | bytes 1 | tf_op jit(solution)/shard_map/finish/pallas_call | solution.py:462
  (105 shorter events, 26.3 us)
Async XLA Ops:
  7.2 75.0 %all-gather.2.cloned.1.call-start = ((), (), s32[]{:S(2)}) async-start(), calls=%async_computation.1 | async-start | bytes 2621440 | tf_op jit(solution)/shard_map/all_gather | solution.py:294
  9.5 21.2 %copy-start.8 = (bf16[512,512]{1,0:T(8,128)(2,1)S(1)}, bf16[512,512]{1,0:T(8,128)(2,1)}, u32[]{:S(2)}) copy-start(bf16[512,512]{1,0:T(8,128)(2,1)} %rest_0_.1) | copy-start | bytes 1572868
  9.5 19.3 %collective-permute-start.2 = (bf16[3,256,512]{2,1,0:T(8,128)(2,1)S(1)}, bf16[3,256,512]{2,1,0:T(8,128)(2,1)S(1)}, u32[]{:S(2)}, u32[]{:S(2)}) collective-permute-start(bf16[3,256,512]{2,1,0:T(8,128)(2,1)S(1)} %pad_maximum_fusion), channel_id=1, source_target_pairs={{0,4},{4,0},{8,12},{12,8},{16,20},{20,16},{24,28},{28,24},{1,5},{5... | collective-permute-start | bytes 2359304 | tf_op jit(solution)/shard_map/ppermute | solution.py:62
  11.1 17.8 %collective-permute-start.1 = (bf16[2,256,512]{2,1,0:T(8,128)(2,1)S(1)}, bf16[2,256,512]{2,1,0:T(8,128)(2,1)S(1)}, u32[]{:S(2)}, u32[]{:S(2)}) collective-permute-start(bf16[2,256,512]{2,1,0:T(8,128)(2,1)S(1)} %pad_maximum_fusion.1), channel_id=1, source_target_pairs={{8,0},{12,4},{16,8},{20,12},{24,16},{28,20},{9,1},{13,5},{17,9},{2... | collective-permute-start | bytes 1572872 | tf_op jit(solution)/shard_map/ppermute | solution.py:27
  13.5 15.4 %collective-permute-start = (bf16[2,256,512]{2,1,0:T(8,128)(2,1)S(1)}, bf16[2,256,512]{2,1,0:T(8,128)(2,1)S(1)}, u32[]{:S(2)}, u32[]{:S(2)}) collective-permute-start(bf16[2,256,512]{2,1,0:T(8,128)(2,1)S(1)} %pad_maximum_fusion.1), channel_id=1, source_target_pairs={{0,8},{4,12},{8,16},{12,20},{16,24},{20,28},{1,9},{5,13},{9,17},{1... | collective-permute-start | bytes 1572872 | tf_op jit(solution)/shard_map/ppermute | solution.py:27
  28.9 43.5 %copy-start.4 = (bf16[3,256,512]{2,1,0:T(8,128)(2,1)}, bf16[3,256,512]{2,1,0:T(8,128)(2,1)S(1)}, u32[]{:S(2)}) copy-start(bf16[3,256,512]{2,1,0:T(8,128)(2,1)S(1)} %collective-permute-done.2.rest_2_) | copy-start | bytes 2359300
  28.9 43.4 %copy-start.6 = (bf16[2,256,512]{2,1,0:T(8,128)(2,1)}, bf16[2,256,512]{2,1,0:T(8,128)(2,1)S(1)}, u32[]{:S(2)}) copy-start(bf16[2,256,512]{2,1,0:T(8,128)(2,1)S(1)} %collective-permute-done.1.rest_1_) | copy-start | bytes 1572868
  29.9 39.2 %copy-start.30 = (s32[16,3]{0,1:T(4,128)S(1)}, s32[16,3]{0,1:T(4,128)}, u32[]{:S(2)}) copy-start(s32[16,3]{0,1:T(4,128)} %param.10) | copy-start | bytes 580
  29.9 117.5 %reduce-scatter.2.cloned.1.call-start = ((), (), s32[]{:S(2)}) async-start(), calls=%async_computation.2 | async-start | bytes 2621440 | tf_op jit(solution)/shard_map/reduce_scatter | solution.py:392
  30.0 0.7 collective-permute-start.4
  30.7 20.7 %collective-permute-start.7 = (bf16[512,512]{1,0:T(8,128)(2,1)S(1)}, bf16[512,512]{1,0:T(8,128)(2,1)}, u32[]{:S(2)}, u32[]{:S(2)}) collective-permute-start(bf16[512,512]{1,0:T(8,128)(2,1)S(1)} %copy-done.8), channel_id=1, source_target_pairs={{0,8},{4,12},{8,0},{12,4},{16,24},{20,28},{24,16},{28,20},{1,9},{5... | collective-permute-start | bytes 1572872 | tf_op jit(solution)/shard_map/ppermute | solution.py:306
  41.1 17.1 %collective-permute-start.8 = (bf16[512,512]{1,0:T(8,128)(2,1)S(1)}, bf16[512,512]{1,0:T(8,128)(2,1)}, u32[]{:S(2)}, u32[]{:S(2)}) collective-permute-start(bf16[512,512]{1,0:T(8,128)(2,1)S(1)} %copy-done.8), channel_id=1, source_target_pairs={{8,16},{12,20},{16,8},{20,12},{9,17},{13,21},{17,9},{21,13},{10,18... | collective-permute-start | bytes 1572872 | tf_op jit(solution)/shard_map/ppermute | solution.py:306
  51.4 13.5 %collective-permute-start.10 = (bf16[512,512]{1,0:T(8,128)(2,1)}, bf16[512,512]{1,0:T(8,128)(2,1)}, u32[]{:S(2)}, u32[]{:S(2)}) collective-permute-start(bf16[512,512]{1,0:T(8,128)(2,1)} %collective-permute-done.7.rest_1_), channel_id=1, source_target_pairs={{8,16},{12,20},{16,8},{20,12},{9,17},{13,21},{17,9},{21,13},{10,18... | collective-permute-start | bytes 1572872 | tf_op jit(solution)/shard_map/ppermute | solution.py:306
  56.3 16.0 %collective-permute-start.3 = (bf16[2,256,512]{2,1,0:T(8,128)(2,1)}, bf16[2,256,512]{2,1,0:T(8,128)(2,1)}, u32[]{:S(2)}, u32[]{:S(2)}) collective-permute-start(bf16[2,256,512]{2,1,0:T(8,128)(2,1)} %broadcast_select_fusion), channel_id=1, source_target_pairs={{0,4},{8,12},{16,20},{12,8},{20,16},{28,24},{1,5},{9,13},{17,21},{... | collective-permute-start | bytes 1572872 | tf_op jit(solution)/shard_map/ppermute | solution.py:297
  58.2 23.2 %collective-permute-start.9 = (bf16[512,512]{1,0:T(8,128)(2,1)}, bf16[512,512]{1,0:T(8,128)(2,1)S(1)}, u32[]{:S(2)}, u32[]{:S(2)}) collective-permute-start(bf16[512,512]{1,0:T(8,128)(2,1)} %collective-permute-done.8.rest_2_), channel_id=1, source_target_pairs={{8,0},{12,4},{16,24},{20,28},{9,1},{13,5},{17,25},{21,29},{10,2},{... | collective-permute-start | bytes 1572872 | tf_op jit(solution)/shard_map/ppermute | solution.py:306
  64.9 17.3 %collective-permute-start.11 = (bf16[512,512]{1,0:T(8,128)(2,1)}, bf16[512,512]{1,0:T(8,128)(2,1)}, u32[]{:S(2)}, u32[]{:S(2)}) collective-permute-start(bf16[512,512]{1,0:T(8,128)(2,1)} %collective-permute-done.10.rest_4_), channel_id=1, source_target_pairs={{8,0},{12,4},{16,24},{20,28},{9,1},{13,5},{17,25},{21,29},{10,2},{... | collective-permute-start | bytes 1572872 | tf_op jit(solution)/shard_map/ppermute | solution.py:306
  67.1 5.2 %collective-permute-start.5 = (bf16[2,128,512]{2,1,0:T(8,128)(2,1)S(1)}, bf16[2,128,512]{2,1,0:T(8,128)(2,1)}, u32[]{:S(2)}, u32[]{:S(2)}) collective-permute-start(bf16[2,128,512]{2,1,0:T(8,128)(2,1)S(1)} %fusion.7), channel_id=1, source_target_pairs={{4,28},{0,12},{16,20},{8,24},{5,29},{1,13},{17,21},{9,25},{6,30},{... | collective-permute-start | bytes 786440 | tf_op jit(solution)/shard_map/ppermute | solution.py:302
  79.6 10.9 %collective-permute-start.6 = (bf16[256,512]{1,0:T(8,128)(2,1)S(1)}, bf16[256,512]{1,0:T(8,128)(2,1)}, u32[]{:S(2)}, u32[]{:S(2)}) collective-permute-start(bf16[256,512]{1,0:T(8,128)(2,1)S(1)} %get-tuple-element.36.mixed_ref.rest_2_.rest_5_), channel_id=1, source_target_pairs={{0,4},{4,0},{8,12},{12,8},{16,20},{20,16},{24,28},{28,24},{1,5},{5... | collective-permute-start | bytes 786440 | tf_op jit(solution)/shard_map/ppermute | solution.py:62
  90.2 16.2 %collective-permute-start.12 = (bf16[256,512]{1,0:T(8,128)(2,1)}, bf16[256,512]{1,0:T(8,128)(2,1)}, u32[]{:S(2)}, u32[]{:S(2)}) collective-permute-start(bf16[256,512]{1,0:T(8,128)(2,1)} %get-tuple-element.39), channel_id=1, source_target_pairs={{0,4},{4,0},{8,12},{12,8},{16,20},{20,16},{24,28},{28,24},{1,5},{5... | collective-permute-start | bytes 786440 | tf_op jit(solution)/shard_map/ppermute | solution.py:62
  101.1 23.9 %collective-permute-start.15 = (bf16[512,512]{1,0:T(8,128)(2,1)}, bf16[512,512]{1,0:T(8,128)(2,1)S(1)}, u32[]{:S(2)}, u32[]{:S(2)}) collective-permute-start(bf16[512,512]{1,0:T(8,128)(2,1)} %get-tuple-element.53), channel_id=1, source_target_pairs={{0,8},{4,12},{8,16},{12,20},{16,24},{20,28},{24,0},{28,4},{1,9},{5... | collective-permute-start | bytes 1572872 | tf_op jit(solution)/shard_map/ppermute | solution.py:58
  106.4 20.8 %collective-permute-start.16 = (bf16[512,512]{1,0:T(8,128)(2,1)S(1)}, bf16[512,512]{1,0:T(8,128)(2,1)S(1)}, u32[]{:S(2)}, u32[]{:S(2)}) collective-permute-start(bf16[512,512]{1,0:T(8,128)(2,1)S(1)} %copy-done.26), channel_id=1, source_target_pairs={{0,24},{4,28},{8,0},{12,4},{16,8},{20,12},{24,16},{28,20},{1,25},{... | collective-permute-start | bytes 1572872 | tf_op jit(solution)/shard_map/ppermute | solution.py:58
  111.3 20.5 %collective-permute-start.17 = (bf16[2,384,512]{2,1,0:T(8,128)(2,1)S(1)}, bf16[2,384,512]{2,1,0:T(8,128)(2,1)S(1)}, u32[]{:S(2)}, u32[]{:S(2)}) collective-permute-start(bf16[2,384,512]{2,1,0:T(8,128)(2,1)S(1)} %first_grad.1), channel_id=1, source_target_pairs={{0,4},{4,0},{8,12},{12,8},{16,20},{20,16},{24,28},{28,24},{1,5},{5... | collective-permute-start | bytes 2359304 | tf_op jit(solution)/shard_map/ppermute | solution.py:62
  121.0 21.6 %collective-permute-start.13 = (bf16[2,256,512]{2,1,0:T(8,128)(2,1)S(1)}, bf16[2,256,512]{2,1,0:T(8,128)(2,1)S(1)}, u32[]{:S(2)}, u32[]{:S(2)}) collective-permute-start(bf16[2,256,512]{2,1,0:T(8,128)(2,1)S(1)} %get-tuple-element.47), channel_id=1, source_target_pairs={{0,4},{4,0},{8,12},{12,8},{16,20},{20,16},{24,28},{28,24},{1,5},{5... | collective-permute-start | bytes 1572872 | tf_op jit(solution)/shard_map/ppermute | solution.py:62
  125.0 17.7 %copy-start.27 = (bf16[512,512]{1,0:T(8,128)(2,1)}, bf16[512,512]{1,0:T(8,128)(2,1)S(1)}, u32[]{:S(2)}) copy-start(bf16[512,512]{1,0:T(8,128)(2,1)S(1)} %collective-permute-done.15) | copy-start | bytes 1572868
  132.8 23.2 %copy-start.15 = (f32[512,512]{1,0:T(8,128)S(1)}, f32[512,512]{1,0:T(8,128)}, u32[]{:S(2)}) copy-start(f32[512,512]{1,0:T(8,128)} %copy-done.14) | copy-start | bytes 3145732
  134.1 21.3 %collective-permute-start.22 = (bf16[512,512]{1,0:T(8,128)(2,1)S(1)}, bf16[512,512]{1,0:T(8,128)(2,1)S(1)}, u32[]{:S(2)}, u32[]{:S(2)}) collective-permute-start(bf16[512,512]{1,0:T(8,128)(2,1)S(1)} %copy-done.24), channel_id=1, source_target_pairs={{0,16},{4,20},{8,24},{12,28},{16,0},{20,4},{24,8},{28,12},{1,17},{... | collective-permute-start | bytes 1572872 | tf_op jit(solution)/shard_map/ppermute | solution.py:58
  137.5 25.3 %collective-permute-start.21 = (bf16[2,128,512]{2,1,0:T(8,128)(2,1)S(1)}, bf16[2,128,512]{2,1,0:T(8,128)(2,1)}, u32[]{:S(2)}, u32[]{:S(2)}) collective-permute-start(bf16[2,128,512]{2,1,0:T(8,128)(2,1)S(1)} %get-tuple-element.61), channel_id=1, source_target_pairs={{24,0},{25,1},{26,2},{27,3}} | collective-permute-start | bytes 786440 | tf_op jit(solution)/shard_map/ppermute | solution.py:457
  138.9 36.1 %collective-permute-start.20 = (bf16[2,128,512]{2,1,0:T(8,128)(2,1)S(1)}, bf16[2,128,512]{2,1,0:T(8,128)(2,1)}, u32[]{:S(2)}, u32[]{:S(2)}) collective-permute-start(bf16[2,128,512]{2,1,0:T(8,128)(2,1)S(1)} %get-tuple-element.61), channel_id=1, source_target_pairs={{16,0},{17,1},{18,2},{19,3}} | collective-permute-start | bytes 786440 | tf_op jit(solution)/shard_map/ppermute | solution.py:457
  140.2 34.8 %collective-permute-start.18 = (bf16[2,256,512]{2,1,0:T(8,128)(2,1)}, bf16[2,256,512]{2,1,0:T(8,128)(2,1)}, u32[]{:S(2)}, u32[]{:S(2)}) collective-permute-start(bf16[2,256,512]{2,1,0:T(8,128)(2,1)} %get-tuple-element.59), channel_id=1, source_target_pairs={{8,0},{12,4},{16,8},{20,12},{24,16},{28,20},{9,1},{13,5},{17,9},{2... | collective-permute-start | bytes 1572872 | tf_op jit(solution)/shard_map/ppermute | solution.py:27
  142.7 15.7 %copy-start.29 = (bf16[2,256,512]{2,1,0:T(8,128)(2,1)}, bf16[2,256,512]{2,1,0:T(8,128)(2,1)S(1)}, u32[]{:S(2)}) copy-start(bf16[2,256,512]{2,1,0:T(8,128)(2,1)S(1)} %collective-permute-done.13.a_ref) | copy-start | bytes 1572868
  142.7 32.3 %collective-permute-start.19 = (bf16[2,256,512]{2,1,0:T(8,128)(2,1)}, bf16[2,256,512]{2,1,0:T(8,128)(2,1)}, u32[]{:S(2)}, u32[]{:S(2)}) collective-permute-start(bf16[2,256,512]{2,1,0:T(8,128)(2,1)} %get-tuple-element.60), channel_id=1, source_target_pairs={{0,8},{4,12},{8,16},{12,20},{16,24},{20,28},{1,9},{5,13},{9,17},{1... | collective-permute-start | bytes 1572872 | tf_op jit(solution)/shard_map/ppermute | solution.py:27
  155.5 6.4 %collective-permute-start.14 = (bf16[256,512]{1,0:T(8,128)(2,1)S(1)}, bf16[256,512]{1,0:T(8,128)(2,1)S(1)}, u32[]{:S(2)}, u32[]{:S(2)}) collective-permute-start(bf16[256,512]{1,0:T(8,128)(2,1)S(1)} %get-tuple-element.73), channel_id=1, source_target_pairs={{0,4},{4,0},{8,12},{12,8},{16,20},{20,16},{24,28},{28,24},{1,5},{5... | collective-permute-start | bytes 786440 | tf_op jit(solution)/shard_map/ppermute | solution.py:62
  (24 other events, 105.2 us)
Sparse Core Ops, SparseCore 0:
  30.0 22.7 all-gather.1
  101.2 34.9 reduce-scatter.1

commit v7 on v6

--- a/solution.py
+++ b/solution.py
@@ -437,14 +437,14 @@
         to_before, to_after, _ = lax.optimization_barrier((to_before, to_after, weight_turns))
         to_before = to_before.astype(jnp.float32) + jnp.where(side == 1, diagonal, 0.0) + folded
         to_after = to_after.astype(jnp.float32) + jnp.where(side == 0, diagonal, 0.0)
+        to_before, to_after = to_before.astype(jnp.bfloat16), to_after.astype(jnp.bfloat16)
+        to_before, to_after, to_beside, near, last_part = lax.optimization_barrier(
+            (to_before, to_after, to_beside, first_sum.astype(jnp.bfloat16), weight_parts[1])
+        )
         back_pair = swapped(to_beside, range(length))
-        to_before, to_after = to_before.astype(jnp.bfloat16), to_after.astype(jnp.bfloat16)
-        to_before, to_after, near, last_part = lax.optimization_barrier(
-            (to_before, to_after, first_sum.astype(jnp.bfloat16), weight_parts[1])
-        )
         back_down = shifted(to_before, -2)
         back_up = shifted(to_after, 2)
-        scattered = tied(scattered, back_pair)
+        scattered = tied(scattered, back_up)
         mine, theirs = scattered[:tokens], swapped(scattered[tokens:], range(length))
         attended = jnp.where(
             side == 0, jnp.concatenate([mine, theirs], axis=1), jnp.concatenate([theirs, mine], axis=1)

time: 186 us -> 193 us (1.038); the launches traced: 185 us -> 190 us
  waiting for transfers between devices: 58.9 us -> 69.4 us
  starting transfers between devices: 56.9 us -> 51.7 us
    ppermute x4, waiting for transfers between devices: 12.2 us -> 26.4 us  [shifted(): lax.ppermute(x, 'ctx', [(i, i + by) for i in range(peers) if 0 <= i + by...]
    ppermute x6, waiting for transfers between devices: 19.9 us -> 15.2 us  [swapped(): lax.ppermute(piece, 'ctx', [(2 * z + n, 2 * z + 1 - n) for z in places fo...]
    ppermute x3, starting transfers between devices: 8.69 us -> 5.96 us  [turned(): lax.ppermute(x, 'ctx', [(2 * z + n, 2 * ((z + by) % length) + n) for z in...]
    ppermute x4, starting transfers between devices: 12.9 us -> 10.8 us  [shifted(): lax.ppermute(x, 'ctx', [(i, i + by) for i in range(peers) if 0 <= i + by...]
where the time goes in v7:
time: 193 us; the launch traced here: 190 us
  waiting for transfers between devices  69.4 us (36%)
  starting transfers between devices  51.7 us (27%)
  Pallas kernels  33.4 us (17%)
  between operations  14.5 us (8%)
  local copies, waits for them, and re-layouts  11.3 us (6%)
  other arithmetic  9.55 us (5%)
    ppermute x4, waiting for transfers between devices, shifted(): lax.ppermute(x, 'ctx', [(i, i + by) for i in range(peers) if 0 <= i + by...  26.4 us
    ppermute x5, starting transfers between devices, between(): lax.ppermute(x, 'ctx', [(2 * a + n, 2 * b + n) for a, b in places for n i...  21.7 us
    ppermute x6, waiting for transfers between devices, swapped(): lax.ppermute(piece, 'ctx', [(2 * z + n, 2 * z + 1 - n) for z in places fo...  15.2 us
    ppermute x3, waiting for transfers between devices, turned(): lax.ppermute(x, 'ctx', [(2 * z + n, 2 * ((z + by) % length) + n) for z in...  12.7 us
    ppermute x5, waiting for transfers between devices, between(): lax.ppermute(x, 'ctx', [(2 * a + n, 2 * b + n) for a, b in places for n i...  11.8 us
    ppermute x4, starting transfers between devices, shifted(): lax.ppermute(x, 'ctx', [(i, i + by) for i in range(peers) if 0 <= i + by...  10.8 us
    unnamed x63, local copies, waits for them, and re-layouts  9.12 us
    pallas_call x1, Pallas kernels, local(): pl.pallas_call(functools.partial(bwd_kernel, offsets, early, per_dev, sca...  9.09 us
  transfers between devices with their start and end apart: 25, of which 10 were waited for; matrix products, arithmetic and copies ran while one was open for 5% of the time, Pallas kernels for 16%

profile of v7, /device:TPU:12, one launch (start us, length us, event | category | flops | bytes accessed | tf_op | source)
XLA Modules:
  0.0 189.8 jit_solution(2014688369438434762)
XLA Ops:
  9.5 1.6 collective-permute-start.2
  11.1 2.4 %collective-permute-start.1 = (bf16[2,256,512]{2,1,0:T(8,128)(2,1)S(1)}, bf16[2,256,512]{2,1,0:T(8,128)(2,1)S(1)}, u32[]{:S(2)}, u32[]{:S(2)}) collective-permute-start(bf16[2,256,512]{2,1,0:T(8,128)(2,1)S(1)} %pad_maximum_fusion.1), channel_id=1, source_target_pairs={{8,0},{12,4},{16,8},{20,12},{24,16},{28,20},{9,1},{13,5},{17,9},{2... | collective-permute-start | bytes 1572872 | tf_op jit(solution)/shard_map/ppermute | solution.py:27
  13.5 3.5 %collective-permute-start = (bf16[2,256,512]{2,1,0:T(8,128)(2,1)S(1)}, bf16[2,256,512]{2,1,0:T(8,128)(2,1)S(1)}, u32[]{:S(2)}, u32[]{:S(2)}) collective-permute-start(bf16[2,256,512]{2,1,0:T(8,128)(2,1)S(1)} %pad_maximum_fusion.1), channel_id=1, source_target_pairs={{0,8},{4,12},{8,16},{12,20},{16,24},{20,28},{1,9},{5,13},{9,17},{1... | collective-permute-start | bytes 1572872 | tf_op jit(solution)/shard_map/ppermute | solution.py:27
  17.0 11.9 %collective-permute-done.2.rest_2_ = bf16[3,256,512]{2,1,0:T(8,128)(2,1)S(1)} collective-permute-done((bf16[3,256,512]{2,1,0:T(8,128)(2,1)S(1)}, bf16[3,256,512]{2,1,0:T(8,128)(2,1)S(1)}, u32[]{:S(2)}, u32[]{:S(2)}) %collective-permute-start.2) | collective-permute-done | bytes 786464 | tf_op jit(solution)/shard_map/ppermute | solution.py:62
  30.7 10.4 %collective-permute-start.7 = (bf16[512,512]{1,0:T(8,128)(2,1)S(1)}, bf16[512,512]{1,0:T(8,128)(2,1)}, u32[]{:S(2)}, u32[]{:S(2)}) collective-permute-start(bf16[512,512]{1,0:T(8,128)(2,1)S(1)} %copy-done.8), channel_id=1, source_target_pairs={{0,8},{4,12},{8,0},{12,4},{16,24},{20,28},{24,16},{28,20},{1,9},{5... | collective-permute-start | bytes 1572872 | tf_op jit(solution)/shard_map/ppermute | solution.py:306
  41.1 3.8 %collective-permute-start.8 = (bf16[512,512]{1,0:T(8,128)(2,1)S(1)}, bf16[512,512]{1,0:T(8,128)(2,1)}, u32[]{:S(2)}, u32[]{:S(2)}) collective-permute-start(bf16[512,512]{1,0:T(8,128)(2,1)S(1)} %copy-done.8), channel_id=1, source_target_pairs={{8,16},{12,20},{16,8},{20,12},{9,17},{13,21},{17,9},{21,13},{10,18... | collective-permute-start | bytes 1572872 | tf_op jit(solution)/shard_map/ppermute | solution.py:306
  44.9 6.5 %collective-permute-done.7.rest_1_ = bf16[512,512]{1,0:T(8,128)(2,1)} collective-permute-done((bf16[512,512]{1,0:T(8,128)(2,1)S(1)}, bf16[512,512]{1,0:T(8,128)(2,1)}, u32[]{:S(2)}, u32[]{:S(2)}) %collective-permute-start.7) | collective-permute-done | bytes 524320 | tf_op jit(solution)/shard_map/ppermute | solution.py:306
  51.4 4.0 %collective-permute-start.10 = (bf16[512,512]{1,0:T(8,128)(2,1)}, bf16[512,512]{1,0:T(8,128)(2,1)}, u32[]{:S(2)}, u32[]{:S(2)}) collective-permute-start(bf16[512,512]{1,0:T(8,128)(2,1)} %collective-permute-done.7.rest_1_), channel_id=1, source_target_pairs={{8,16},{12,20},{16,8},{20,12},{9,17},{13,21},{17,9},{21,13},{10,18... | collective-permute-start | bytes 1572872 | tf_op jit(solution)/shard_map/ppermute | solution.py:306
  56.3 1.9 %collective-permute-start.3 = (bf16[2,256,512]{2,1,0:T(8,128)(2,1)}, bf16[2,256,512]{2,1,0:T(8,128)(2,1)}, u32[]{:S(2)}, u32[]{:S(2)}) collective-permute-start(bf16[2,256,512]{2,1,0:T(8,128)(2,1)} %broadcast_select_fusion), channel_id=1, source_target_pairs={{0,4},{8,12},{16,20},{12,8},{20,16},{28,24},{1,5},{9,13},{17,21},{... | collective-permute-start | bytes 1572872 | tf_op jit(solution)/shard_map/ppermute | solution.py:297
  59.5 5.4 %collective-permute-done.10.rest_4_ = bf16[512,512]{1,0:T(8,128)(2,1)} collective-permute-done((bf16[512,512]{1,0:T(8,128)(2,1)}, bf16[512,512]{1,0:T(8,128)(2,1)}, u32[]{:S(2)}, u32[]{:S(2)}) %collective-permute-start.10) | collective-permute-done | bytes 524320 | tf_op jit(solution)/shard_map/ppermute | solution.py:306
  64.9 2.1 %collective-permute-start.11 = (bf16[512,512]{1,0:T(8,128)(2,1)}, bf16[512,512]{1,0:T(8,128)(2,1)}, u32[]{:S(2)}, u32[]{:S(2)}) collective-permute-start(bf16[512,512]{1,0:T(8,128)(2,1)} %collective-permute-done.10.rest_4_), channel_id=1, source_target_pairs={{8,0},{12,4},{16,24},{20,28},{9,1},{13,5},{17,25},{21,29},{10,2},{... | collective-permute-start | bytes 1572872 | tf_op jit(solution)/shard_map/ppermute | solution.py:306
  67.1 2.0 %collective-permute-start.5 = (bf16[2,128,512]{2,1,0:T(8,128)(2,1)S(1)}, bf16[2,128,512]{2,1,0:T(8,128)(2,1)}, u32[]{:S(2)}, u32[]{:S(2)}) collective-permute-start(bf16[2,128,512]{2,1,0:T(8,128)(2,1)S(1)} %fusion.7), channel_id=1, source_target_pairs={{4,28},{0,12},{16,20},{8,24},{5,29},{1,13},{17,21},{9,25},{6,30},{... | collective-permute-start | bytes 786440 | tf_op jit(solution)/shard_map/ppermute | solution.py:302
  69.1 3.1 %collective-permute-done.5 = bf16[2,128,512]{2,1,0:T(8,128)(2,1)} collective-permute-done((bf16[2,128,512]{2,1,0:T(8,128)(2,1)S(1)}, bf16[2,128,512]{2,1,0:T(8,128)(2,1)}, u32[]{:S(2)}, u32[]{:S(2)}) %collective-permute-start.5) | collective-permute-done | bytes 262176 | tf_op jit(solution)/shard_map/ppermute | solution.py:302
  73.4 6.2 %attend.1 = (bf16[256,512]{1,0:T(8,128)(2,1)S(1)}, f32[4,1,256]{2,1,0:T(1,128)S(1)}) custom-call(s32[1]{0:T(128)} %bitcast.run_ref, s32[16,3]{1,0:T(8,128)S(1)} %copy.11.lists_ref, bf16[256,512]{1,0:T(8,128)(2,1)S(1)} %copy-done.21, bf16[256,512]{1,0:T(8,128)(2,1)S(1)} %copy-done.3, bf16[256,512]{1,0:T(8,128)(2,1)S(1)} %copy-done.2, ...), custom_call_target="tpu_custom_call" | custom-call | flops 1 | bytes 1 | tf_op jit(solution)/shard_map/attend/pallas_call | solution.py:339
  79.6 1.9 collective-permute-start.6
  82.2 1.6 copy-done
  85.9 3.5 %project_grad.1 = (f32[256,512]{1,0:T(8,128)S(1)}, bf16[256,512]{1,0:T(8,128)(2,1)}) custom-call(bf16[512,2048]{1,0:T(8,128)(2,1)S(1)} %copy-done, bf16[512,512]{1,0:T(8,128)(2,1)S(1)} %copy-done.9, bf16[512,512]{1,0:T(8,128)(2,1)} %collective-permute-done.7.rest_1_, bf16[512,512]{1,0:T(8,128)(2,1)} %collective-permute-done.8.rest_2_, ...), custom_call_target="tpu_custom_call" | custom-call | flops 1 | bytes 1 | tf_op jit(solution)/shard_map/project_grad/pallas_call | solution.py:356
  90.5 2.6 %weight_part.1 = (f32[512,512]{1,0:T(8,128)S(1)}, bf16[512,512]{1,0:T(8,128)(2,1)}, bf16[512,512]{1,0:T(8,128)(2,1)S(1)}, bf16[512,512]{1,0:T(8,128)(2,1)S(1)}) custom-call(bf16[512,2048]{1,0:T(8,128)(2,1)S(1)} %copy-done.1, bf16[256,512]{1,0:T(8,128)(2,1)S(1)} %get-tuple-element.37.mixed_ref.rest_2_.rest_5_, bf16[256,512]{1,0:T(8,128)(2,1)} %collective-permute-done.6.other_ref), custom_call_target="tpu_custom_call" | custom-call | flops 1 | bytes 1 | tf_op jit(solution)/shard_map/weight_part/pallas_call | solution.py:371
  95.7 5.3 %project_out.1 = bf16[512,2048]{1,0:T(8,128)(2,1)} custom-call(bf16[256,512]{1,0:T(8,128)(2,1)S(1)} %get-tuple-element.37.mixed_ref.rest_2_.rest_5_, bf16[256,512]{1,0:T(8,128)(2,1)} %collective-permute-done.6.other_ref, bf16[512,512]{1,0:T(8,128)(2,1)S(1)} %copy-done.10, bf16[512,512]{1,0:T(8,128)(2,1)} %collective-permute-done.7.rest_1_, ...), custom_call_target="tpu_custom_call" | custom-call | flops 1 | bytes 1 | tf_op jit(solution)/shard_map/project_out/pallas_call | solution.py:382
  101.1 5.3 %collective-permute-start.13 = (bf16[512,512]{1,0:T(8,128)(2,1)}, bf16[512,512]{1,0:T(8,128)(2,1)S(1)}, u32[]{:S(2)}, u32[]{:S(2)}) collective-permute-start(bf16[512,512]{1,0:T(8,128)(2,1)} %get-tuple-element.50), channel_id=1, source_target_pairs={{0,8},{4,12},{8,16},{12,20},{16,24},{20,28},{24,0},{28,4},{1,9},{5... | collective-permute-start | bytes 1572872 | tf_op jit(solution)/shard_map/ppermute | solution.py:58
  107.5 3.8 %first_grad.1 = bf16[2,384,512]{2,1,0:T(8,128)(2,1)S(1)} custom-call(s32[1]{0:T(128)} %bitcast.run_ref, s32[16,3]{1,0:T(8,128)S(1)} %copy.11.lists_ref, bf16[256,512]{1,0:T(8,128)(2,1)S(1)} %copy-done.22, bf16[2,256,512]{2,1,0:T(8,128)(2,1)} %collective-permute-done.3.rest_3_.rest_0_, bf16[2,128,512]{2,1,0:T(8,128)(2,1)S(1)} %copy-done.17, ...), custom_call_target="tpu_custom_call" | custom-call | flops 10000000000 | bytes 1 | tf_op jit(solution)/shard_map/first_grad/pallas_call | solution.py:402
  112.0 9.1 %attend_grad.1 = (bf16[256,512]{1,0:T(8,128)(2,1)}, f32[2,256,512]{2,1,0:T(8,128)S(1)}, bf16[2,256,512]{2,1,0:T(8,128)(2,1)S(1)}, bf16[2,256,512]{2,1,0:T(8,128)(2,1)S(1)}, bf16[2,256,512]{2,1,0:T(8,128)(2,1)}) custom-call(s32[1]{0:T(128)} %bitcast.run_ref, s32[16,3]{1,0:T(8,128)S(1)} %copy.11.lists_ref, bf16[256,512]{1,0:T(8,128)(2,1)S(1)} %copy-done.22, ...), custom_call_target="tpu_custom_call" | custom-call | flops 30000001024 | bytes 1 | tf_op jit(solution)/shard_map/attend_grad/pallas_call | solution.py:415
  121.1 3.9 %collective-permute-done.13 = bf16[512,512]{1,0:T(8,128)(2,1)S(1)} collective-permute-done((bf16[512,512]{1,0:T(8,128)(2,1)}, bf16[512,512]{1,0:T(8,128)(2,1)S(1)}, u32[]{:S(2)}, u32[]{:S(2)}) %collective-permute-start.13) | collective-permute-done | bytes 524320 | tf_op jit(solution)/shard_map/ppermute | solution.py:58
  125.0 2.2 %collective-permute-done.14 = bf16[512,512]{1,0:T(8,128)(2,1)S(1)} collective-permute-done((bf16[512,512]{1,0:T(8,128)(2,1)S(1)}, bf16[512,512]{1,0:T(8,128)(2,1)S(1)}, u32[]{:S(2)}, u32[]{:S(2)}) %collective-permute-start.14) | collective-permute-done | bytes 524320 | tf_op jit(solution)/shard_map/ppermute | solution.py:58
  129.3 3.1 %collective-permute-start.16 = (bf16[2,256,512]{2,1,0:T(8,128)(2,1)S(1)}, bf16[2,256,512]{2,1,0:T(8,128)(2,1)S(1)}, u32[]{:S(2)}, u32[]{:S(2)}) collective-permute-start(bf16[2,256,512]{2,1,0:T(8,128)(2,1)S(1)} %get-tuple-element.58), channel_id=1, source_target_pairs={{0,8},{4,12},{8,16},{12,20},{16,24},{20,28},{1,9},{5,13},{9,17},{1... | collective-permute-start | bytes 1572872 | tf_op jit(solution)/shard_map/ppermute | solution.py:27
  136.6 19.3 %collective-permute-done.16.c_ref = bf16[2,256,512]{2,1,0:T(8,128)(2,1)S(1)} collective-permute-done((bf16[2,256,512]{2,1,0:T(8,128)(2,1)S(1)}, bf16[2,256,512]{2,1,0:T(8,128)(2,1)S(1)}, u32[]{:S(2)}, u32[]{:S(2)}) %collective-permute-start.16) | collective-permute-done | bytes 524320 | tf_op jit(solution)/shard_map/ppermute | solution.py:27
  155.9 1.9 %collective-permute-start.19 = (bf16[2,256,512]{2,1,0:T(8,128)(2,1)}, bf16[2,256,512]{2,1,0:T(8,128)(2,1)}, u32[]{:S(2)}, u32[]{:S(2)}) collective-permute-start(bf16[2,256,512]{2,1,0:T(8,128)(2,1)} %get-tuple-element.62), channel_id=1, source_target_pairs={{8,0},{12,4},{16,8},{20,12},{24,16},{28,20},{9,1},{13,5},{17,9},{2... | collective-permute-start | bytes 1572872 | tf_op jit(solution)/shard_map/ppermute | solution.py:27
  158.9 6.6 %collective-permute-done.22 = bf16[512,512]{1,0:T(8,128)(2,1)S(1)} collective-permute-done((bf16[512,512]{1,0:T(8,128)(2,1)S(1)}, bf16[512,512]{1,0:T(8,128)(2,1)S(1)}, u32[]{:S(2)}, u32[]{:S(2)}) %collective-permute-start.22) | collective-permute-done | bytes 524320 | tf_op jit(solution)/shard_map/ppermute | solution.py:58
  166.2 2.4 %convert_add_fusion = f32[512,512]{1,0:T(8,128)} fusion(bf16[512,512]{1,0:T(8,128)(2,1)S(1)} %collective-permute-done.22, bf16[512,512]{1,0:T(8,128)(2,1)} %copy-done.28, f32[512,512]{1,0:T(8,128)S(1)} %copy-done.15, bf16[512,512]{1,0:T(8,128)(2,1)} %copy-done.27), kind=kLoop, calls=%fused_computation.7 | loop fusion | flops 1572864 | bytes 3670016 | tf_op jit(solution)/shard_map/add | solution.py:454
  168.7 3.3 %collective-permute-done.17 = bf16[256,512]{1,0:T(8,128)(2,1)S(1)} collective-permute-done((bf16[256,512]{1,0:T(8,128)(2,1)S(1)}, bf16[256,512]{1,0:T(8,128)(2,1)S(1)}, u32[]{:S(2)}, u32[]{:S(2)}) %collective-permute-start.17) | collective-permute-done | bytes 262176 | tf_op jit(solution)/shard_map/ppermute | solution.py:62
  172.9 7.1 %collective-permute-done.19.b_ref = bf16[2,256,512]{2,1,0:T(8,128)(2,1)} collective-permute-done((bf16[2,256,512]{2,1,0:T(8,128)(2,1)}, bf16[2,256,512]{2,1,0:T(8,128)(2,1)}, u32[]{:S(2)}, u32[]{:S(2)}) %collective-permute-start.19) | collective-permute-done | bytes 524320 | tf_op jit(solution)/shard_map/ppermute | solution.py:27
  180.1 2.9 %finish.1 = (bf16[256,512]{1,0:T(8,128)(2,1)}, bf16[256,512]{1,0:T(8,128)(2,1)}) custom-call(s32[1]{0:T(128)} %bitcast.run_ref, f32[2,256,512]{2,1,0:T(8,128)} %copy-done.18, bf16[2,256,512]{2,1,0:T(8,128)(2,1)} %collective-permute-done.18.a_ref, bf16[2,256,512]{2,1,0:T(8,128)(2,1)} %collective-permute-done.19.b_ref, bf16[2,256,512]{2,1,0:T(8,128)(2,1)} %copy-done.29, ...), custom_call_target="tpu_custom_call" | custom-call | flops 1 | bytes 1 | tf_op jit(solution)/shard_map/finish/pallas_call | solution.py:462
  (105 shorter events, 24.8 us)
Async XLA Ops:
  7.2 75.0 %all-gather.2.cloned.1.call-start = ((), (), s32[]{:S(2)}) async-start(), calls=%async_computation.1 | async-start | bytes 2621440 | tf_op jit(solution)/shard_map/all_gather | solution.py:294
  9.5 21.2 %copy-start.8 = (bf16[512,512]{1,0:T(8,128)(2,1)S(1)}, bf16[512,512]{1,0:T(8,128)(2,1)}, u32[]{:S(2)}) copy-start(bf16[512,512]{1,0:T(8,128)(2,1)} %rest_0_.1) | copy-start | bytes 1572868
  9.5 19.3 %collective-permute-start.2 = (bf16[3,256,512]{2,1,0:T(8,128)(2,1)S(1)}, bf16[3,256,512]{2,1,0:T(8,128)(2,1)S(1)}, u32[]{:S(2)}, u32[]{:S(2)}) collective-permute-start(bf16[3,256,512]{2,1,0:T(8,128)(2,1)S(1)} %pad_maximum_fusion), channel_id=1, source_target_pairs={{0,4},{4,0},{8,12},{12,8},{16,20},{20,16},{24,28},{28,24},{1,5},{5... | collective-permute-start | bytes 2359304 | tf_op jit(solution)/shard_map/ppermute | solution.py:62
  11.1 17.8 %collective-permute-start.1 = (bf16[2,256,512]{2,1,0:T(8,128)(2,1)S(1)}, bf16[2,256,512]{2,1,0:T(8,128)(2,1)S(1)}, u32[]{:S(2)}, u32[]{:S(2)}) collective-permute-start(bf16[2,256,512]{2,1,0:T(8,128)(2,1)S(1)} %pad_maximum_fusion.1), channel_id=1, source_target_pairs={{8,0},{12,4},{16,8},{20,12},{24,16},{28,20},{9,1},{13,5},{17,9},{2... | collective-permute-start | bytes 1572872 | tf_op jit(solution)/shard_map/ppermute | solution.py:27
  13.5 15.4 %collective-permute-start = (bf16[2,256,512]{2,1,0:T(8,128)(2,1)S(1)}, bf16[2,256,512]{2,1,0:T(8,128)(2,1)S(1)}, u32[]{:S(2)}, u32[]{:S(2)}) collective-permute-start(bf16[2,256,512]{2,1,0:T(8,128)(2,1)S(1)} %pad_maximum_fusion.1), channel_id=1, source_target_pairs={{0,8},{4,12},{8,16},{12,20},{16,24},{20,28},{1,9},{5,13},{9,17},{1... | collective-permute-start | bytes 1572872 | tf_op jit(solution)/shard_map/ppermute | solution.py:27
  28.9 43.5 %copy-start.4 = (bf16[3,256,512]{2,1,0:T(8,128)(2,1)}, bf16[3,256,512]{2,1,0:T(8,128)(2,1)S(1)}, u32[]{:S(2)}) copy-start(bf16[3,256,512]{2,1,0:T(8,128)(2,1)S(1)} %collective-permute-done.2.rest_2_) | copy-start | bytes 2359300
  28.9 43.4 %copy-start.6 = (bf16[2,256,512]{2,1,0:T(8,128)(2,1)}, bf16[2,256,512]{2,1,0:T(8,128)(2,1)S(1)}, u32[]{:S(2)}) copy-start(bf16[2,256,512]{2,1,0:T(8,128)(2,1)S(1)} %collective-permute-done.1.rest_1_) | copy-start | bytes 1572868
  29.9 39.2 %copy-start.30 = (s32[16,3]{0,1:T(4,128)S(1)}, s32[16,3]{0,1:T(4,128)}, u32[]{:S(2)}) copy-start(s32[16,3]{0,1:T(4,128)} %param.10) | copy-start | bytes 580
  29.9 127.9 %reduce-scatter.2.cloned.1.call-start = ((), (), s32[]{:S(2)}) async-start(), calls=%async_computation.2 | async-start | bytes 2621440 | tf_op jit(solution)/shard_map/reduce_scatter | solution.py:392
  30.0 0.7 collective-permute-start.4
  30.7 20.7 %collective-permute-start.7 = (bf16[512,512]{1,0:T(8,128)(2,1)S(1)}, bf16[512,512]{1,0:T(8,128)(2,1)}, u32[]{:S(2)}, u32[]{:S(2)}) collective-permute-start(bf16[512,512]{1,0:T(8,128)(2,1)S(1)} %copy-done.8), channel_id=1, source_target_pairs={{0,8},{4,12},{8,0},{12,4},{16,24},{20,28},{24,16},{28,20},{1,9},{5... | collective-permute-start | bytes 1572872 | tf_op jit(solution)/shard_map/ppermute | solution.py:306
  41.1 17.1 %collective-permute-start.8 = (bf16[512,512]{1,0:T(8,128)(2,1)S(1)}, bf16[512,512]{1,0:T(8,128)(2,1)}, u32[]{:S(2)}, u32[]{:S(2)}) collective-permute-start(bf16[512,512]{1,0:T(8,128)(2,1)S(1)} %copy-done.8), channel_id=1, source_target_pairs={{8,16},{12,20},{16,8},{20,12},{9,17},{13,21},{17,9},{21,13},{10,18... | collective-permute-start | bytes 1572872 | tf_op jit(solution)/shard_map/ppermute | solution.py:306
  51.4 13.5 %collective-permute-start.10 = (bf16[512,512]{1,0:T(8,128)(2,1)}, bf16[512,512]{1,0:T(8,128)(2,1)}, u32[]{:S(2)}, u32[]{:S(2)}) collective-permute-start(bf16[512,512]{1,0:T(8,128)(2,1)} %collective-permute-done.7.rest_1_), channel_id=1, source_target_pairs={{8,16},{12,20},{16,8},{20,12},{9,17},{13,21},{17,9},{21,13},{10,18... | collective-permute-start | bytes 1572872 | tf_op jit(solution)/shard_map/ppermute | solution.py:306
  56.3 16.0 %collective-permute-start.3 = (bf16[2,256,512]{2,1,0:T(8,128)(2,1)}, bf16[2,256,512]{2,1,0:T(8,128)(2,1)}, u32[]{:S(2)}, u32[]{:S(2)}) collective-permute-start(bf16[2,256,512]{2,1,0:T(8,128)(2,1)} %broadcast_select_fusion), channel_id=1, source_target_pairs={{0,4},{8,12},{16,20},{12,8},{20,16},{28,24},{1,5},{9,13},{17,21},{... | collective-permute-start | bytes 1572872 | tf_op jit(solution)/shard_map/ppermute | solution.py:297
  58.2 23.2 %collective-permute-start.9 = (bf16[512,512]{1,0:T(8,128)(2,1)}, bf16[512,512]{1,0:T(8,128)(2,1)S(1)}, u32[]{:S(2)}, u32[]{:S(2)}) collective-permute-start(bf16[512,512]{1,0:T(8,128)(2,1)} %collective-permute-done.8.rest_2_), channel_id=1, source_target_pairs={{8,0},{12,4},{16,24},{20,28},{9,1},{13,5},{17,25},{21,29},{10,2},{... | collective-permute-start | bytes 1572872 | tf_op jit(solution)/shard_map/ppermute | solution.py:306
  64.9 17.3 %collective-permute-start.11 = (bf16[512,512]{1,0:T(8,128)(2,1)}, bf16[512,512]{1,0:T(8,128)(2,1)}, u32[]{:S(2)}, u32[]{:S(2)}) collective-permute-start(bf16[512,512]{1,0:T(8,128)(2,1)} %collective-permute-done.10.rest_4_), channel_id=1, source_target_pairs={{8,0},{12,4},{16,24},{20,28},{9,1},{13,5},{17,25},{21,29},{10,2},{... | collective-permute-start | bytes 1572872 | tf_op jit(solution)/shard_map/ppermute | solution.py:306
  67.1 5.2 %collective-permute-start.5 = (bf16[2,128,512]{2,1,0:T(8,128)(2,1)S(1)}, bf16[2,128,512]{2,1,0:T(8,128)(2,1)}, u32[]{:S(2)}, u32[]{:S(2)}) collective-permute-start(bf16[2,128,512]{2,1,0:T(8,128)(2,1)S(1)} %fusion.7), channel_id=1, source_target_pairs={{4,28},{0,12},{16,20},{8,24},{5,29},{1,13},{17,21},{9,25},{6,30},{... | collective-permute-start | bytes 786440 | tf_op jit(solution)/shard_map/ppermute | solution.py:302
  72.3 9.9 %copy-start.16 = (bf16[2,128,512]{2,1,0:T(8,128)(2,1)}, bf16[2,128,512]{2,1,0:T(8,128)(2,1)S(1)}, u32[]{:S(2)}) copy-start(bf16[2,128,512]{2,1,0:T(8,128)(2,1)S(1)} %broadcast_select_fusion.2.rest_4_.rest_1_) | copy-start | bytes 786436
  79.6 10.9 %collective-permute-start.6 = (bf16[256,512]{1,0:T(8,128)(2,1)S(1)}, bf16[256,512]{1,0:T(8,128)(2,1)}, u32[]{:S(2)}, u32[]{:S(2)}) collective-permute-start(bf16[256,512]{1,0:T(8,128)(2,1)S(1)} %get-tuple-element.37.mixed_ref.rest_2_.rest_5_), channel_id=1, source_target_pairs={{0,4},{4,0},{8,12},{12,8},{16,20},{20,16},{24,28},{28,24},{1,5},{5... | collective-permute-start | bytes 786440 | tf_op jit(solution)/shard_map/ppermute | solution.py:62
  90.2 16.2 %collective-permute-start.12 = (bf16[256,512]{1,0:T(8,128)(2,1)}, bf16[256,512]{1,0:T(8,128)(2,1)}, u32[]{:S(2)}, u32[]{:S(2)}) collective-permute-start(bf16[256,512]{1,0:T(8,128)(2,1)} %get-tuple-element.40), channel_id=1, source_target_pairs={{0,4},{4,0},{8,12},{12,8},{16,20},{20,16},{24,28},{28,24},{1,5},{5... | collective-permute-start | bytes 786440 | tf_op jit(solution)/shard_map/ppermute | solution.py:62
  101.1 23.9 %collective-permute-start.13 = (bf16[512,512]{1,0:T(8,128)(2,1)}, bf16[512,512]{1,0:T(8,128)(2,1)S(1)}, u32[]{:S(2)}, u32[]{:S(2)}) collective-permute-start(bf16[512,512]{1,0:T(8,128)(2,1)} %get-tuple-element.50), channel_id=1, source_target_pairs={{0,8},{4,12},{8,16},{12,20},{16,24},{20,28},{24,0},{28,4},{1,9},{5... | collective-permute-start | bytes 1572872 | tf_op jit(solution)/shard_map/ppermute | solution.py:58
  106.4 20.8 %collective-permute-start.14 = (bf16[512,512]{1,0:T(8,128)(2,1)S(1)}, bf16[512,512]{1,0:T(8,128)(2,1)S(1)}, u32[]{:S(2)}, u32[]{:S(2)}) collective-permute-start(bf16[512,512]{1,0:T(8,128)(2,1)S(1)} %copy-done.26), channel_id=1, source_target_pairs={{0,24},{4,28},{8,0},{12,4},{16,8},{20,12},{24,16},{28,20},{1,25},{... | collective-permute-start | bytes 1572872 | tf_op jit(solution)/shard_map/ppermute | solution.py:58
  111.3 15.9 %collective-permute-start.15 = (bf16[2,384,512]{2,1,0:T(8,128)(2,1)S(1)}, bf16[2,384,512]{2,1,0:T(8,128)(2,1)S(1)}, u32[]{:S(2)}, u32[]{:S(2)}) collective-permute-start(bf16[2,384,512]{2,1,0:T(8,128)(2,1)S(1)} %first_grad.1), channel_id=1, source_target_pairs={{0,4},{4,0},{8,12},{12,8},{16,20},{20,16},{24,28},{28,24},{1,5},{5... | collective-permute-start | bytes 2359304 | tf_op jit(solution)/shard_map/ppermute | solution.py:62
  128.2 38.1 %copy-start.15 = (f32[512,512]{1,0:T(8,128)S(1)}, f32[512,512]{1,0:T(8,128)}, u32[]{:S(2)}) copy-start(f32[512,512]{1,0:T(8,128)} %copy-done.14) | copy-start | bytes 3145732
  129.3 26.5 %collective-permute-start.16 = (bf16[2,256,512]{2,1,0:T(8,128)(2,1)S(1)}, bf16[2,256,512]{2,1,0:T(8,128)(2,1)S(1)}, u32[]{:S(2)}, u32[]{:S(2)}) collective-permute-start(bf16[2,256,512]{2,1,0:T(8,128)(2,1)S(1)} %get-tuple-element.58), channel_id=1, source_target_pairs={{0,8},{4,12},{8,16},{12,20},{16,24},{20,28},{1,9},{5,13},{9,17},{1... | collective-permute-start | bytes 1572872 | tf_op jit(solution)/shard_map/ppermute | solution.py:27
  132.4 33.0 %collective-permute-start.22 = (bf16[512,512]{1,0:T(8,128)(2,1)S(1)}, bf16[512,512]{1,0:T(8,128)(2,1)S(1)}, u32[]{:S(2)}, u32[]{:S(2)}) collective-permute-start(bf16[512,512]{1,0:T(8,128)(2,1)S(1)} %copy-done.24), channel_id=1, source_target_pairs={{0,16},{4,20},{8,24},{12,28},{16,0},{20,4},{24,8},{28,12},{1,17},{... | collective-permute-start | bytes 1572872 | tf_op jit(solution)/shard_map/ppermute | solution.py:58
  133.1 39.9 %collective-permute-start.21 = (bf16[2,128,512]{2,1,0:T(8,128)(2,1)S(1)}, bf16[2,128,512]{2,1,0:T(8,128)(2,1)}, u32[]{:S(2)}, u32[]{:S(2)}) collective-permute-start(bf16[2,128,512]{2,1,0:T(8,128)(2,1)S(1)} %get-tuple-element.63), channel_id=1, source_target_pairs={{24,0},{25,1},{26,2},{27,3}} | collective-permute-start | bytes 786440 | tf_op jit(solution)/shard_map/ppermute | solution.py:457
  134.4 45.6 %collective-permute-start.20 = (bf16[2,128,512]{2,1,0:T(8,128)(2,1)S(1)}, bf16[2,128,512]{2,1,0:T(8,128)(2,1)}, u32[]{:S(2)}, u32[]{:S(2)}) collective-permute-start(bf16[2,128,512]{2,1,0:T(8,128)(2,1)S(1)} %get-tuple-element.63), channel_id=1, source_target_pairs={{16,0},{17,1},{18,2},{19,3}} | collective-permute-start | bytes 786440 | tf_op jit(solution)/shard_map/ppermute | solution.py:457
  135.8 44.3 %collective-permute-start.18 = (bf16[2,256,512]{2,1,0:T(8,128)(2,1)}, bf16[2,256,512]{2,1,0:T(8,128)(2,1)}, u32[]{:S(2)}, u32[]{:S(2)}) collective-permute-start(bf16[2,256,512]{2,1,0:T(8,128)(2,1)} %get-tuple-element.61), channel_id=1, source_target_pairs={{0,4},{4,0},{8,12},{12,8},{16,20},{20,16},{24,28},{28,24},{1,5},{5... | collective-permute-start | bytes 1572872 | tf_op jit(solution)/shard_map/ppermute | solution.py:62
  155.9 12.8 %copy-start.29 = (bf16[2,256,512]{2,1,0:T(8,128)(2,1)}, bf16[2,256,512]{2,1,0:T(8,128)(2,1)S(1)}, u32[]{:S(2)}) copy-start(bf16[2,256,512]{2,1,0:T(8,128)(2,1)S(1)} %collective-permute-done.16.c_ref) | copy-start | bytes 1572868
  155.9 24.2 %collective-permute-start.19 = (bf16[2,256,512]{2,1,0:T(8,128)(2,1)}, bf16[2,256,512]{2,1,0:T(8,128)(2,1)}, u32[]{:S(2)}, u32[]{:S(2)}) collective-permute-start(bf16[2,256,512]{2,1,0:T(8,128)(2,1)} %get-tuple-element.62), channel_id=1, source_target_pairs={{8,0},{12,4},{16,8},{20,12},{24,16},{28,20},{9,1},{13,5},{17,9},{2... | collective-permute-start | bytes 1572872 | tf_op jit(solution)/shard_map/ppermute | solution.py:27
  165.5 6.5 %collective-permute-start.17 = (bf16[256,512]{1,0:T(8,128)(2,1)S(1)}, bf16[256,512]{1,0:T(8,128)(2,1)S(1)}, u32[]{:S(2)}, u32[]{:S(2)}) collective-permute-start(bf16[256,512]{1,0:T(8,128)(2,1)S(1)} %get-tuple-element.75), channel_id=1, source_target_pairs={{0,4},{4,0},{8,12},{12,8},{16,20},{20,16},{24,28},{28,24},{1,5},{5... | collective-permute-start | bytes 786440 | tf_op jit(solution)/shard_map/ppermute | solution.py:62
  (24 other events, 93.2 us)
Sparse Core Ops, SparseCore 0:
  30.0 22.7 all-gather.1
  101.2 34.9 reduce-scatter.1
